TPU v7x, 32 devices: a whole 2x2x4 slice. The times are simulated.
32 devices in a mesh: groups: 2 (over x), expert: 16 (over z, y, core).
Axes of the slice: x: 2, y: 2, z: 4, core: 2. Of those that a mesh axis runs over, the one named last changes fastest.
Arguments:
- down_proj: bfloat16 [32, 768, 4096], P(('groups', 'expert')), parts along dimension 0, may hold values from -0.21875 to 0.21875
- cov_factor: bfloat16 [32, 768, 768], P(('groups', 'expert')), parts along dimension 0, as said below
- sketch: bfloat16 [32, 768, 256], P(('groups', 'expert')), parts along dimension 0, may hold values from -6 to 6
- membership: int32 [32], P('groups'), parts along dimension 0, may hold values from 0 to 7, as said below
Outputs:
- coef: bfloat16 [32, 768, 256], P(('groups', 'expert')), parts along dimension 0
- basis: bfloat16 [16, 4096, 256], P('groups', 'expert'), parts along dimension 0
There are 2 independent parts, one for each index of `groups`. A program takes and returns all parts, laid end to end along the dimension named above; each array names one. Nothing has to cross between parts.
Inputs may be any that keep to these rules, and one draw needn't show every extreme that they name: `membership`: every cluster has one or more experts; cluster sizes differ. `cov_factor`: lower triangular with a positive diagonal.
All inputs are finite; a program needn't handle non-finite values.
Results may differ from a plain program's by a relative error of at most 0.0078.
Values may be sent and summed in bfloat16 or wider, within the bound.
No kernel may reach another device: no remote copies, remote signals or barrier semaphores. Data moves between devices by JAX's collectives and lax.ppermute only.
A program may use at most 64 MiB of HBM per device.

v0:
```python
import math

import jax
import jax.numpy as jnp
from jax import lax
from jax.sharding import PartitionSpec as P


def from_partner(block, axis, apart):
    count = lax.axis_size(axis)
    route = []
    for low in range(count):
        high = low | 1 << apart
        if high != low and high < count:
            route += [(low, high), (high, low)]
    return lax.ppermute(block, axis, route)


def local_gram(rows):
    return jnp.dot(rows.T, rows, preferred_element_type=jnp.float32)


def orthonormal_rows(rows, total_gram):
    factor = jnp.linalg.cholesky(total_gram)
    return jax.scipy.linalg.solve_triangular(factor, rows.T, lower=True).T


def local(down_proj, cov_factor, sketch, membership):
    devices = lax.axis_size("expert")
    weights = down_proj[0]
    width = weights.shape[1]
    weighted = jnp.dot(cov_factor[0], sketch[0], preferred_element_type=jnp.float32).astype(
        jnp.bfloat16
    )
    partial_sketch = lax.dot_general(
        weights, weighted, (((0,), (0,)), ((), ())), preferred_element_type=jnp.float32
    ).astype(jnp.bfloat16)
    rank_cols = partial_sketch.shape[1]
    block_rows = width // devices
    half_rows = block_rows // 2
    clusters = devices // 2
    received = lax.all_to_all(
        partial_sketch.reshape(devices, block_rows, rank_cols),
        "expert",
        split_axis=0,
        concat_axis=0,
        tiled=True,
    )
    member_table = (membership[None, :] == jnp.arange(clusters, dtype=jnp.int32)[:, None]).astype(
        jnp.bfloat16
    )
    cluster_rows = jnp.dot(
        member_table,
        received.reshape(devices, block_rows * rank_cols),
        preferred_element_type=jnp.float32,
    ).astype(jnp.bfloat16)
    scale = math.sqrt(width)
    pair_rows = lax.all_to_all(
        cluster_rows.reshape(devices, half_rows, rank_cols),
        "expert",
        split_axis=0,
        concat_axis=0,
        tiled=True,
    )
    pair_rows = pair_rows.reshape(width // 2, rank_cols)
    gram_one = local_gram(pair_rows)
    gram_one = gram_one + from_partner(gram_one, "expert", 0)
    single = orthonormal_rows(pair_rows.astype(jnp.float32), gram_one)
    basis_half = (scale * single).astype(jnp.bfloat16).reshape(devices, half_rows, rank_cols)
    returned = lax.all_to_all(basis_half, "expert", split_axis=0, concat_axis=0, tiled=True)
    basis_block = returned.reshape(clusters, block_rows, rank_cols)
    chosen = jnp.dot(
        member_table.T,
        basis_block.reshape(clusters, block_rows * rank_cols),
        preferred_element_type=jnp.float32,
    ).astype(jnp.bfloat16)
    gathered = lax.all_to_all(
        chosen.reshape(devices, block_rows, rank_cols),
        "expert",
        split_axis=0,
        concat_axis=0,
        tiled=True,
    ).reshape(width, rank_cols)
    coef = jnp.dot(weights, gathered, preferred_element_type=jnp.float32).astype(jnp.bfloat16)
    return (coef[None], basis_block)


def solution(mesh):
    placed = (
        P(("groups", "expert"), None, None),
        P(("groups", "expert"), None, None),
        P(("groups", "expert"), None, None),
        P("groups"),
    )
    return jax.shard_map(
        local,
        mesh=mesh,
        in_specs=placed,
        out_specs=(P(("groups", "expert"), None, None), P("groups", "expert", None)),
        check_vma=False,
    )
```

profile of v0, /device:TPU:9, one launch (start us, length us, event | category | flops | bytes accessed | tf_op | source)
XLA Modules:
  0.0 255.3 jit_solution(18358480194426241653)
XLA Ops:
  0.6 1.3 copy-done
  1.9 7.0 %fusion.7 = bf16[4096,256]{0,1:T(8,128)(2,1)} fusion(bf16[1,768,4096]{2,1,0:T(8,128)(2,1)} %param.4, bf16[1,768,768]{2,1,0:T(8,128)(2,1)S(1)} %copy-done, bf16[1,768,256]{2,1,0:T(8,128)(2,1)} %param.6), kind=kOutput, calls=%fused_computation.9 | convolution fusion | flops 1913847808 | bytes 9961472 | tf_op jit(solution)/shard_map/dot_general | solution.py:35
  8.9 3.3 %copy.21 = bf16[4096,256]{1,0:T(8,128)(2,1)S(1)} copy(bf16[4096,256]{0,1:T(8,128)(2,1)} %fusion.7) | data formatting | bytes 4194304 | tf_op jit(solution)/shard_map/reshape | solution.py:43
  12.2 54.3 %all_to_all.20 = bf16[16,256,256]{2,1,0:T(8,128)(2,1)S(1)} all-to-all(bf16[16,256,256]{2,1,0:T(8,128)(2,1)S(1)} %bitcast.83), channel_id=1, replica_groups=mesh['groups'=2,'expert'=16] {'expert'}, dimensions={0} | all-to-all | bytes 4194304 | tf_op jit(solution)/shard_map/all_to_all | solution.py:42
  66.5 1.2 copy.25
  68.1 0.5 reshape.50
  68.6 29.8 %all_to_all.21 = bf16[16,128,256]{2,1,0:T(8,128)(2,1)S(1)} all-to-all(bf16[16,128,256]{2,1,0:T(8,128)(2,1)S(1)} %reshape.50), channel_id=1, replica_groups=mesh['groups'=2,'expert'=16] {'expert'}, dimensions={0} | all-to-all | bytes 2097152 | tf_op jit(solution)/shard_map/all_to_all | solution.py:58
  98.3 0.5 convolution_bitcast_fusion
  99.0 1.5 collective-permute-done
  100.7 11.7 %cholesky.50 = f32[128,128]{1,0:T(8,128)S(1)} custom-call(f32[128,128]{1,0:T(8,128)S(1)} %cholesky.118), custom_call_target="Cholesky" | custom-call | tf_op jit(solution)/shard_map/jit(cholesky)/cholesky | solution.py:24
  112.4 9.8 %custom-call.15 = f32[1,128,128]{1,2,0:T(8,128)S(1)} custom-call(f32[1,128,128]{2,1,0:T(8,128)S(1)} %get-tuple-element.27), custom_call_target="InvertDiagBlocksLowerTriangular" | custom-call | tf_op jit(solution)/shard_map/jit(cholesky)/cholesky | solution.py:24
  122.8 11.7 %cholesky.105 = f32[128,128]{1,0:T(8,128)S(1)} custom-call(f32[128,128]{1,0:T(8,128)S(1)} %slice_subtract_fusion), custom_call_target="Cholesky" | custom-call | tf_op jit(solution)/shard_map/jit(cholesky)/cholesky | solution.py:24
  134.5 0.7 compare_reduce_fusion
  136.7 4.1 %while.1 = (s32[]{:T(128)}, f32[256,256]{1,0:T(8,128)S(1)}, s32[2,2]{1,0:T(2,128)S(1)}, f32[2,128,128]{2,1,0:T(8,128)S(1)}, s32[]{:T(128)}) while((s32[]{:T(128)}, f32[256,256]{1,0:T(8,128)S(1)}, s32[2,2]{1,0:T(2,128)S(1)}, f32[2,128,128]{2,1,0:T(8,128)S(1)}, s32[]{:T(128)}) %tuple.29), condition=%wide.while_cond, body=%wide.while_body.sunk | while | flops 2 | bytes 131189 | solution.py:25
  136.7 0.6 fusion.44
  137.3 1.4 bitcast_dynamic-update-slice_fusion.2
  138.8 0.6 fusion.44
  139.4 1.4 bitcast_dynamic-update-slice_fusion.2
  140.8 19.9 %custom-call.16 = f32[2,128,128]{1,2,0:T(8,128)S(1)} custom-call(f32[2,128,128]{2,1,0:T(8,128)S(1)} %get-tuple-element.9), custom_call_target="InvertDiagBlocksLowerTriangular" | custom-call | tf_op jit(solution)/shard_map/jit(_solve_triangular)/triangular_solve | solution.py:25
  160.7 0.6 fusion.21
  161.3 1.8 convolution_subtract_fusion
  163.2 1.1 fusion.27
  164.4 0.5 copy.24
  164.9 29.6 %all_to_all.22 = bf16[16,128,256]{2,1,0:T(8,128)(2,1)S(1)} all-to-all(bf16[16,128,256]{2,1,0:T(8,128)(2,1)S(1)} %bitcast.89), channel_id=1, replica_groups=mesh['groups'=2,'expert'=16] {'expert'}, dimensions={0} | all-to-all | bytes 2097152 | tf_op jit(solution)/shard_map/all_to_all | solution.py:70
  194.6 0.5 reshape_reshape.3
  195.1 0.8 convolution_convert_fusion
  195.8 1.8 copy.26
  197.6 4.5 %all-to-all-start.3 = ((bf16[16,256,256]{2,1,0:T(8,128)(2,1)}), bf16[16,256,256]{2,1,0:T(8,128)(2,1)}, u32[]{:S(2)}, u32[]{:S(2)}) async-start(bf16[16,256,256]{2,1,0:T(8,128)(2,1)} %bitcast.82), calls=%async_computation.3 | async-start | bytes 4194304 | tf_op jit(solution)/shard_map/all_to_all | solution.py:77
  202.1 46.1 %all-to-all-done.3 = bf16[16,256,256]{2,1,0:T(8,128)(2,1)} async-done(((bf16[16,256,256]{2,1,0:T(8,128)(2,1)}), bf16[16,256,256]{2,1,0:T(8,128)(2,1)}, u32[]{:S(2)}, u32[]{:S(2)}) %all-to-all-start.3) | async-done | bytes 2097184 | tf_op jit(solution)/shard_map/all_to_all | solution.py:77
  248.1 5.3 %fusion.14 = bf16[1,768,256]{1,2,0:T(8,128)(2,1)S(1)} fusion(bf16[4096,256]{1,0:T(8,128)(2,1)} %bitcast.18, bf16[1,768,4096]{2,1,0:T(8,128)(2,1)} %param.4), kind=kOutput, calls=%fused_computation.15 | convolution fusion | flops 1610809344 | bytes 8781824 | tf_op jit(solution)/shard_map/dot_general | solution.py:84
  253.4 0.9 copy.18
  254.3 1.0 copy.39
  (21 shorter events, 1.6 us)
Async XLA Ops:
  0.6 1.3 copy-start
  66.5 1.2 copy-start.1
  98.9 1.6 collective-permute-start
  197.6 50.5 %all-to-all-start.3 = ((bf16[16,256,256]{2,1,0:T(8,128)(2,1)}), bf16[16,256,256]{2,1,0:T(8,128)(2,1)}, u32[]{:S(2)}, u32[]{:S(2)}) async-start(bf16[16,256,256]{2,1,0:T(8,128)(2,1)} %bitcast.82), calls=%async_computation.3 | async-start | bytes 4194304 | tf_op jit(solution)/shard_map/all_to_all | solution.py:77
where the time goes:
time: 257 us; the launch traced here: 255 us
  blocking collectives  114 us (44%)
  other arithmetic  54.2 us (21%)
  waiting for transfers between devices  47.6 us (19%)
  matrix products  18 us (7%)
  local copies, waits for them, and re-layouts  15.1 us (6%)
  starting transfers between devices  4.53 us (2%)
    all_to_all x1, blocking collectives, local(): lax.all_to_all(partial_sketch.reshape(devices, block_rows, rank_cols), 'e...  54.3 us
    all_to_all x1, waiting for transfers between devices, local(): lax.all_to_all(chosen.reshape(devices, block_rows, rank_cols), 'expert',...  46.1 us
    another operation x6, other arithmetic, orthonormal_rows(): factor = jnp.linalg.cholesky(total_gram)  34 us
    all_to_all x1, blocking collectives, local(): lax.all_to_all(cluster_rows.reshape(devices, half_rows, rank_cols), 'expe...  29.8 us
    all_to_all x1, blocking collectives, local(): lax.all_to_all(basis_half, 'expert', split_axis=0, concat_axis=0, tiled=T...  29.6 us
    another operation x3, other arithmetic, orthonormal_rows(): return jax.scipy.linalg.solve_triangular(factor, rows.T, lower=True).T  19.9 us
    dot_general x1, matrix products, local(): lax.dot_general(weights, weighted, (((0,), (0,)), ((), ())), preferred_el...  7.01 us
    unnamed x8, local copies, waits for them, and re-layouts  6.12 us
  transfers between devices with their start and end apart: 2, of which 2 were waited for; matrix products, arithmetic and copies ran while one was open for 0% of the time, Pallas kernels for 0%

commit v1 on v0

v1 whole, which is shorter than its diff:
```python
import functools
import math

import jax
import jax.numpy as jnp
from jax import lax
from jax.experimental import pallas as pl
from jax.experimental.pallas import tpu as pltpu
from jax.sharding import PartitionSpec as P

F32 = jnp.float32
BF16 = jnp.bfloat16
VMEM_LIMIT = 48 * 1024 * 1024
PANEL = 8
BLOCK = 64


def dot(a, b, dims):
    return lax.dot_general(a, b, (dims, ((), ())), preferred_element_type=F32)


def params():
    return pltpu.CompilerParams(vmem_limit_bytes=VMEM_LIMIT)


def partial_kernel(cov_ref, sketch_ref, weights_ref, out_ref, weighted):
    @pl.when(pl.program_id(0) == 0)
    def _():
        weighted[...] = dot(sketch_ref[...], cov_ref[...], ((0,), (1,))).astype(BF16)

    product = dot(weighted[...], weights_ref[...], ((1,), (0,))).astype(BF16)
    rows = out_ref.shape[2]
    for piece in range(out_ref.shape[0]):
        out_ref[piece] = product[:, piece * rows : (piece + 1) * rows]


def partial_blocks(cov, sketch, weights, devices):
    hidden, width = weights.shape
    rank = sketch.shape[1]
    rows = width // devices
    columns = min(width, 512)
    return pl.pallas_call(
        partial_kernel,
        grid=(width // columns,),
        in_specs=[
            pl.BlockSpec((hidden, hidden), lambda i: (0, 0)),
            pl.BlockSpec((hidden, rank), lambda i: (0, 0)),
            pl.BlockSpec((hidden, columns), lambda i: (0, i)),
        ],
        out_specs=pl.BlockSpec((columns // rows, rank, rows), lambda i: (i, 0, 0)),
        out_shape=jax.ShapeDtypeStruct((devices, rank, rows), BF16),
        scratch_shapes=[pltpu.VMEM((rank, hidden), BF16)],
        compiler_params=params(),
        cost_estimate=pl.CostEstimate(
            flops=2 * hidden * rank * (hidden + width),
            bytes_accessed=2 * (hidden * (width + hidden + rank) + rank * width),
            transcendentals=0,
        ),
    )(cov, sketch, weights)


def cluster_kernel(member_ref, base_ref, recv_ref, rows_ref, chosen_ref, keep_ref, send_ref, total):
    devices = recv_ref.shape[0]
    clusters = rows_ref.shape[0]
    half = rows_ref.shape[1] // 2
    total[...] = jnp.zeros_like(total)

    @pl.loop(0, devices)
    def _(e):
        c = member_ref[e]
        total[c] = total[c] + recv_ref[e].astype(F32)

    @pl.loop(0, clusters)
    def _(c):
        rows_ref[c] = total[c].astype(BF16)

    @pl.loop(0, devices)
    def _(e):
        chosen_ref[e] = rows_ref[member_ref[e]]

    def gram(slot):
        block = rows_ref[base_ref[0] ^ slot]
        full = dot(block, block, ((1,), (1,)))
        return full[:half, :half], full[half:, :half], full[half:, half:]

    kept = keep_ref.shape[0]

    @pl.loop(0, kept)
    def _(k):
        keep_ref[k, 0], keep_ref[k, 1], keep_ref[k, 2] = gram(k)
        send_ref[k, 0], send_ref[k, 1], send_ref[k, 2] = gram(k + kept)


def cluster_sums(members, base, received):
    devices, rank, rows = received.shape
    clusters = devices // 2
    half = rank // 2
    smem = pl.BlockSpec(memory_space=pltpu.SMEM)
    vmem = pl.BlockSpec(memory_space=pltpu.VMEM)
    gram = jax.ShapeDtypeStruct((clusters // 2, 3, half, half), F32)
    return pl.pallas_call(
        cluster_kernel,
        in_specs=[smem, smem, vmem],
        out_specs=[vmem] * 4,
        out_shape=[
            jax.ShapeDtypeStruct((clusters, rank, rows), BF16),
            jax.ShapeDtypeStruct((devices, rank, rows), BF16),
            gram,
            gram,
        ],
        scratch_shapes=[pltpu.VMEM((clusters, rank, rows), F32)],
        compiler_params=params(),
    )(members, base, received)


def stacked(x, axis, order):
    high = x.astype(BF16)
    rest = x - high.astype(F32)
    middle = rest.astype(BF16)
    low = (rest - middle.astype(F32)).astype(BF16)
    return jnp.concatenate([(high, middle, low)[i] for i in order], axis=axis)


def stack_left(x, axis):
    return stacked(x, axis, (0, 0, 1, 0, 2, 1))


def stack_right(x, axis):
    return stacked(x, axis, (0, 1, 0, 2, 0, 1))


def block_inverse(square):
    size = square.shape[0]
    lanes = 128
    groups = size // 8
    row = lax.broadcasted_iota(jnp.int32, (size, size), 0)
    col = lax.broadcasted_iota(jnp.int32, (size, size), 1)
    parts = [square, jnp.where(row == col, 1.0, 0.0)]
    if lanes > 2 * size:
        parts.append(jnp.zeros((size, lanes - 2 * size), F32))
    table = jnp.concatenate(parts, axis=1)
    tiles = [table[8 * g : 8 * g + 8, :] for g in range(groups)]
    sub = lax.broadcasted_iota(jnp.int32, (8, lanes), 0)
    pivots = [jnp.ones((8, lanes), F32) for _ in range(groups)]

    def spread(x):
        return jnp.broadcast_to(x, (8, lanes))

    for k in range(0, size, PANEL):
        first = k // 8
        columns = [
            [spread(tiles[g][:, k + i : k + i + 1]) for g in range(first, groups)]
            for i in range(PANEL)
        ]
        s = {}
        for m in range(PANEL):
            for i in range(m, PANEL):
                q = k + i
                s[m, i] = spread(columns[m][q // 8 - first][q % 8 : q % 8 + 1, :])
        rows = [spread(tiles[(k + i) // 8][(k + i) % 8 : (k + i) % 8 + 1, :]) for i in range(PANEL)]
        inverse = []
        for m in range(PANEL):
            inverse.append(1.0 / s[m, m])
            for i in range(m + 1, PANEL):
                factor = s[m, i] * inverse[m]
                for t in range(i, PANEL):
                    s[i, t] = s[i, t] - factor * s[m, t]
                rows[i] = rows[i] - factor * rows[m]
        factors = []
        for m in range(PANEL):
            column = []
            for g in range(groups - first):
                x = columns[m][g]
                for t in range(m):
                    x = x - factors[t][g] * s[t, m]
                column.append(x * inverse[m])
            factors.append(column)
        for g in range(first, groups):
            tile = tiles[g]
            for m in range(PANEL):
                x = factors[m][g - first]
                if 8 * g <= k + m:
                    x = jnp.where(sub + 8 * g > k + m, x, 0.0)
                tile = tile - x * rows[m]
            tiles[g] = tile
        for m in range(PANEL):
            q = k + m
            pivots[q // 8] = jnp.where(sub == q % 8, s[m, m], pivots[q // 8])
    out = [tiles[g] * lax.rsqrt(pivots[g]) for g in range(groups)]
    return jnp.concatenate(out, axis=0)[:, size : 2 * size]


def inverse_kernel(scale, gram_ref, out_ref, work):
    half = gram_ref.shape[1]
    n = 2 * half
    row = lax.broadcasted_iota(jnp.int32, (n, n), 0)
    col = lax.broadcasted_iota(jnp.int32, (n, n), 1)
    work[:half, :half] = gram_ref[0]
    work[half:, :half] = gram_ref[1]
    work[:half, half:n] = gram_ref[1].T
    work[half:, half:n] = gram_ref[2]
    work[:, n:] = jnp.where(row == col, 1.0, 0.0)
    for top in range(0, n, BLOCK):
        left = top // 128 * 128
        bottom = top + BLOCK
        square = work[top:bottom, left : left + 128][:, top - left : bottom - left]
        scaled = dot(
            stack_left(block_inverse(square), 1), stack_right(work[top:bottom, :], 0), ((1,), (0,))
        )
        work[top:bottom, n:] = scaled[:, n:]
        if bottom < n:
            start = bottom // 128 * 128
            change = dot(
                stack_left(scaled[:, start:n], 0), stack_right(scaled, 0), ((0,), (0,))
            )
            work[bottom:, :] = work[bottom:, :] - change[bottom - start :, :]
    out_ref[0] = (scale * work[:half, n : n + half]).astype(out_ref.dtype)
    out_ref[1] = (scale * work[half:, n : n + half]).astype(out_ref.dtype)
    out_ref[2] = (scale * work[half:, n + half :]).astype(out_ref.dtype)


def inverse_factor(gram, scale):
    half = gram.shape[1]
    return pl.pallas_call(
        functools.partial(inverse_kernel, scale),
        out_shape=jax.ShapeDtypeStruct(gram.shape, BF16),
        scratch_shapes=[pltpu.VMEM((2 * half, 4 * half), F32)],
        compiler_params=params(),
    )(gram)


def basis_kernel(base_ref, rows_ref, inverse_ref, out_ref):
    half = inverse_ref.shape[2]

    @pl.loop(0, rows_ref.shape[0])
    def _(c):
        slot = base_ref[0] ^ c
        block = rows_ref[c]
        top = dot(inverse_ref[slot, 0], block[:half], ((1,), (0,)))
        bottom = dot(inverse_ref[slot, 1], block[:half], ((1,), (0,))) + dot(
            inverse_ref[slot, 2], block[half:], ((1,), (0,))
        )
        out_ref[c, :, :half] = top.T.astype(BF16)
        out_ref[c, :, half:] = bottom.T.astype(BF16)


def basis_rows(base, rows_t, inverses):
    clusters, rank, rows = rows_t.shape
    vmem = pl.BlockSpec(memory_space=pltpu.VMEM)
    return pl.pallas_call(
        basis_kernel,
        in_specs=[pl.BlockSpec(memory_space=pltpu.SMEM), vmem, vmem],
        out_specs=vmem,
        out_shape=jax.ShapeDtypeStruct((clusters, rows, rank), BF16),
        compiler_params=params(),
    )(base, rows_t, inverses)


def coef_kernel(slot_ref, weights_ref, gathered_ref, inverse_ref, out_ref, total):
    step = pl.program_id(0)
    rows = gathered_ref.shape[2]

    @pl.when(step == 0)
    def _():
        total[...] = jnp.zeros_like(total)

    block = weights_ref[...]
    for piece in range(gathered_ref.shape[0]):
        total[...] += dot(
            block[:, piece * rows : (piece + 1) * rows], gathered_ref[piece], ((1,), (1,))
        )

    @pl.when(step == pl.num_programs(0) - 1)
    def _():
        half = inverse_ref.shape[2]
        high = total[...].astype(BF16)
        low = (total[...] - high.astype(F32)).astype(BF16)
        slot = slot_ref[0]
        first, below, second = (inverse_ref[slot, i] for i in range(3))

        def times(cols, factor):
            return dot(high[:, cols], factor, ((1,), (1,))) + dot(low[:, cols], factor, ((1,), (1,)))

        left, right = slice(0, half), slice(half, 2 * half)
        out_ref[:, left] = times(left, first).astype(BF16)
        out_ref[:, right] = (times(left, below) + times(right, second)).astype(BF16)


def coefficients(slot, weights, gathered, inverses):
    hidden, width = weights.shape
    devices, rank, rows = gathered.shape
    columns = min(width, 512)
    return pl.pallas_call(
        coef_kernel,
        grid=(width // columns,),
        in_specs=[
            pl.BlockSpec(memory_space=pltpu.SMEM),
            pl.BlockSpec((hidden, columns), lambda i: (0, i)),
            pl.BlockSpec((columns // rows, rank, rows), lambda i: (i, 0, 0)),
            pl.BlockSpec(inverses.shape, lambda i: (0, 0, 0, 0)),
        ],
        out_specs=pl.BlockSpec((hidden, rank), lambda i: (0, 0)),
        out_shape=jax.ShapeDtypeStruct((hidden, rank), BF16),
        scratch_shapes=[pltpu.VMEM((hidden, rank), F32)],
        compiler_params=params(),
    )(slot, weights, gathered, inverses)


def swap(block, bit):
    count = lax.axis_size("expert")
    return lax.ppermute(block, "expert", [(i, i ^ (1 << bit)) for i in range(count)])


def exchange(blocks):
    return lax.all_to_all(blocks, "expert", split_axis=0, concat_axis=0, tiled=True)


def local(down_proj, cov_factor, sketch, membership):
    devices = lax.axis_size("expert")
    weights = down_proj[0]
    width = weights.shape[1]
    bits = devices.bit_length() - 1
    me = lax.axis_index("expert")
    base = sum(((me >> s) & 1) << (bits - 2 - s) for s in range(bits - 1)).astype(jnp.int32)
    slot = (membership[me] ^ base).reshape(1)
    base = base.reshape(1)

    received = exchange(partial_blocks(cov_factor[0], sketch[0], weights, devices))
    rows_t, chosen, keep, send = cluster_sums(membership, base, received)
    gathered = exchange(chosen)

    total = keep + swap(send, 0)
    for bit in range(1, bits - 1):
        kept = total.shape[0] // 2
        total = total[:kept] + swap(total[kept:], bit)
    total = total + swap(total, bits - 1)
    inverses = inverse_factor(total[0], math.sqrt(width))[None]
    for bit in reversed(range(bits - 1)):
        inverses = jnp.concatenate([inverses, swap(inverses, bit)], axis=0)

    basis = basis_rows(base, rows_t, inverses)
    coef = coefficients(slot, weights, gathered, inverses)
    return (coef[None], basis)


def solution(mesh):
    placed = (
        P(("groups", "expert"), None, None),
        P(("groups", "expert"), None, None),
        P(("groups", "expert"), None, None),
        P("groups"),
    )
    return jax.shard_map(
        local,
        mesh=mesh,
        in_specs=placed,
        out_specs=(P(("groups", "expert"), None, None), P("groups", "expert", None)),
        check_vma=False,
    )
```

time: 257 us -> 173 us (0.67)
  blocking collectives: 114 us -> 0 us
  other arithmetic: 54.2 us -> 1.32 us
  waiting for transfers between devices: 47.6 us -> 96 us
  Pallas kernels: 0 us -> 32.7 us
  starting transfers between devices: 4.53 us -> 29.5 us
  matrix products: 18 us -> 0 us
  local copies, waits for them, and re-layouts: 15.1 us -> 8.65 us
    all_to_all x3 -> x0, blocking collectives: 114 us -> none  [the longest x1 54.3 us: local(): lax.all_to_all(partial_sketch.reshape(devices, block_rows, rank_cols), 'e...]
    another operation x9 -> x0, other arithmetic: 54 us -> none  [the longest x6 34 us: orthonormal_rows(): factor = jnp.linalg.cholesky(total_gram)]
    ppermute x1 -> x7, waiting for transfers between devices: 1.5 us -> 50 us  [swap(): lax.ppermute(block, 'expert', [(i, i ^ 1 << bit) for i in range(count)])]
    pallas_call x0 -> x5, Pallas kernels: none -> 32.7 us  [the longest x1 9.5 us: inverse_factor(): pl.pallas_call(functools.partial(inverse_kernel, scale), out_shape=jax.Sh...]
    ppermute x1 -> x7, starting transfers between devices: 0.07 us -> 16.4 us  [swap(): lax.ppermute(block, 'expert', [(i, i ^ 1 << bit) for i in range(count)])]
    dot_general x5 -> x0, matrix products: 14 us -> none  [the longest x1 7.01 us: local(): lax.dot_general(weights, weighted, (((0,), (0,)), ((), ())), preferred_el...]
    all_to_all x1 -> x2, starting transfers between devices: 4.46 us -> 13.1 us  [exchange(): lax.all_to_all(blocks, 'expert', split_axis=0, concat_axis=0, tiled=True)]
    another operation x10 -> x0, local copies, waits for them, and re-layouts: 4.63 us -> none
  transfers between devices with their start and end apart: 2 -> 9, of which waited for: 2 -> 8; matrix products, arithmetic and copies ran while one was open for 0% -> 1% of each run, Pallas kernels for 0% -> 8%
where the time goes in v1:
time: 173 us; the launch traced here: 170 us
  waiting for transfers between devices  96 us (55%)
  Pallas kernels  32.7 us (19%)
  starting transfers between devices  29.5 us (17%)
  local copies, waits for them, and re-layouts  8.65 us (5%)
    ppermute x7, waiting for transfers between devices, swap(): lax.ppermute(block, 'expert', [(i, i ^ 1 << bit) for i in range(count)])  50 us
    all_to_all x2, waiting for transfers between devices, exchange(): lax.all_to_all(blocks, 'expert', split_axis=0, concat_axis=0, tiled=True)  46 us
    ppermute x7, starting transfers between devices, swap(): lax.ppermute(block, 'expert', [(i, i ^ 1 << bit) for i in range(count)])  16.4 us
    all_to_all x2, starting transfers between devices, exchange(): lax.all_to_all(blocks, 'expert', split_axis=0, concat_axis=0, tiled=True)  13.1 us
    pallas_call x1, Pallas kernels, inverse_factor(): pl.pallas_call(functools.partial(inverse_kernel, scale), out_shape=jax.Sh...  9.5 us
    pallas_call x1, Pallas kernels, partial_blocks(): pl.pallas_call(partial_kernel, grid=(width // columns,), in_specs=[pl.Blo...  8.33 us
    pallas_call x1, Pallas kernels, coefficients(): pl.pallas_call(coef_kernel, grid=(width // columns,), in_specs=[pl.BlockS...  8.04 us
    unnamed x16, local copies, waits for them, and re-layouts  8.02 us
  transfers between devices with their start and end apart: 9, of which 8 were waited for; matrix products, arithmetic and copies ran while one was open for 1% of the time, Pallas kernels for 8%

profile of v1, /device:TPU:9, one launch (start us, length us, event | category | flops | bytes accessed | tf_op | source)
XLA Modules:
  0.0 169.5 jit_solution(7426767514458715415)
XLA Ops:
  0.6 1.3 copy-done.1
  1.9 1.0 copy-done.4
  2.9 8.3 %shard_map.59 = bf16[16,256,256]{2,1,0:T(8,128)(2,1)} custom-call(bf16[768,768]{1,0:T(8,128)(2,1)S(1)} %bitcast.14, bf16[768,256]{1,0:T(8,128)(2,1)S(1)} %bitcast.15, bf16[768,4096]{1,0:T(8,128)(2,1)} %bitcast.16), custom_call_target="tpu_custom_call" | custom-call | flops 1912602624 | bytes 9961472 | tf_op jit(solution)/shard_map/pallas_call | solution.py:42
  11.2 6.7 %all-to-all-start = ((bf16[16,256,256]{2,1,0:T(8,128)(2,1)}), bf16[16,256,256]{2,1,0:T(8,128)(2,1)S(1)}, u32[]{:S(2)}, u32[]{:S(2)}) async-start(bf16[16,256,256]{2,1,0:T(8,128)(2,1)} %shard_map.59), calls=%async_computation | async-start | bytes 4194304 | tf_op jit(solution)/shard_map/all_to_all | solution.py:315
  18.0 46.0 %all-to-all-done.recv_ref = bf16[16,256,256]{2,1,0:T(8,128)(2,1)S(1)} async-done(((bf16[16,256,256]{2,1,0:T(8,128)(2,1)}), bf16[16,256,256]{2,1,0:T(8,128)(2,1)S(1)}, u32[]{:S(2)}, u32[]{:S(2)}) %all-to-all-start) | async-done | bytes 2097184 | tf_op jit(solution)/shard_map/all_to_all | solution.py:315
  64.0 1.3 copy-done.7
  65.3 3.5 %shard_map.60 = (bf16[8,256,256]{2,1,0:T(8,128)(2,1)S(1)}, bf16[16,256,256]{2,1,0:T(8,128)(2,1)S(1)}, f32[4,3,128,128]{3,2,1,0:T(8,128)S(1)}, f32[4,3,128,128]{3,2,1,0:T(8,128)S(1)}) custom-call(s32[16]{0:T(128)S(1)} %copy-done.5, s32[1]{0:T(128)} %bitcast.3.base_ref, bf16[16,256,256]{2,1,0:T(8,128)(2,1)} %copy-done.7), custom_call_target="tpu_custom_call" | custom-call | tf_op jit(solution)/shard_map/pallas_call | solution.py:101
  68.8 1.3 copy-done
  70.2 1.0 copy-done.2
  71.2 0.9 copy-done.6
  72.0 6.3 %all-to-all-start.1 = ((bf16[16,256,256]{2,1,0:T(8,128)(2,1)}), bf16[16,256,256]{2,1,0:T(8,128)(2,1)S(1)}, u32[]{:S(2)}, u32[]{:S(2)}) async-start(bf16[16,256,256]{2,1,0:T(8,128)(2,1)} %copy-done), calls=%async_computation.1 | async-start | bytes 4194304 | tf_op jit(solution)/shard_map/all_to_all | solution.py:315
  78.4 0.4 collective-permute-start
  78.8 2.2 %collective-permute-done = f32[4,3,128,128]{3,2,1,0:T(8,128)S(1)} collective-permute-done((f32[4,3,128,128]{3,2,1,0:T(8,128)}, f32[4,3,128,128]{3,2,1,0:T(8,128)S(1)}, u32[]{:S(2)}, u32[]{:S(2)}) %collective-permute-start) | collective-permute-done | bytes 786464 | tf_op jit(solution)/shard_map/ppermute | solution.py:311
  80.9 0.1 add.24
  81.0 1.2 collective-permute-start.1
  82.3 19.0 %collective-permute-done.1 = f32[2,3,128,128]{3,2,1,0:T(8,128)S(1)} collective-permute-done((f32[2,3,128,128]{3,2,1,0:T(8,128)S(1)}, f32[2,3,128,128]{3,2,1,0:T(8,128)S(1)}, u32[]{:S(2)}, u32[]{:S(2)}) %collective-permute-start.1) | collective-permute-done | bytes 393248 | tf_op jit(solution)/shard_map/ppermute | solution.py:311
  101.4 4.9 %collective-permute-start.2 = (f32[1,3,128,128]{3,2,1,0:T(8,128)S(1)}, f32[1,3,128,128]{3,2,1,0:T(8,128)S(1)}, u32[]{:S(2)}, u32[]{:S(2)}) collective-permute-start(f32[1,3,128,128]{3,2,1,0:T(8,128)S(1)} %slice.19), channel_id=1, source_target_pairs={{0,4},{1,5},{2,6},{3,7},{4,0},{5,1},{6,2},{7,3},{8,12},{9,13},{10,... | collective-permute-start | bytes 589832 | tf_op jit(solution)/shard_map/ppermute | solution.py:311
  106.3 11.7 %collective-permute-done.2 = f32[1,3,128,128]{3,2,1,0:T(8,128)S(1)} collective-permute-done((f32[1,3,128,128]{3,2,1,0:T(8,128)S(1)}, f32[1,3,128,128]{3,2,1,0:T(8,128)S(1)}, u32[]{:S(2)}, u32[]{:S(2)}) %collective-permute-start.2) | collective-permute-done | bytes 196640 | tf_op jit(solution)/shard_map/ppermute | solution.py:311
  117.9 2.5 %collective-permute-start.3 = (f32[1,3,128,128]{3,2,1,0:T(8,128)S(1)}, f32[1,3,128,128]{3,2,1,0:T(8,128)S(1)}, u32[]{:S(2)}, u32[]{:S(2)}) collective-permute-start(f32[1,3,128,128]{3,2,1,0:T(8,128)S(1)} %slice_add_fusion.1), channel_id=1, source_target_pairs={{0,8},{1,9},{2,10},{3,11},{4,12},{5,13},{6,14},{7,15},{8,0},{9,1},... | collective-permute-start | bytes 589832 | tf_op jit(solution)/shard_map/ppermute | solution.py:311
  120.5 11.7 %collective-permute-done.3 = f32[1,3,128,128]{3,2,1,0:T(8,128)S(1)} collective-permute-done((f32[1,3,128,128]{3,2,1,0:T(8,128)S(1)}, f32[1,3,128,128]{3,2,1,0:T(8,128)S(1)}, u32[]{:S(2)}, u32[]{:S(2)}) %collective-permute-start.3) | collective-permute-done | bytes 196640 | tf_op jit(solution)/shard_map/ppermute | solution.py:311
  132.2 9.5 %shard_map.61 = bf16[3,128,128]{2,1,0:T(8,128)(2,1)S(1)} custom-call(f32[3,128,128]{2,1,0:T(8,128)S(1)} %add_bitcast_fusion.gram_ref), custom_call_target="tpu_custom_call" | custom-call | tf_op jit(solution)/shard_map/pallas_call | solution.py:224
  141.7 3.0 %collective-permute-start.4 = (bf16[1,3,128,128]{3,2,1,0:T(8,128)(2,1)S(1)}, bf16[1,3,128,128]{3,2,1,0:T(8,128)(2,1)S(1)}, u32[]{:S(2)}, u32[]{:S(2)}) collective-permute-start(bf16[1,3,128,128]{3,2,1,0:T(8,128)(2,1)S(1)} %bitcast.10), channel_id=1, source_target_pairs={{0,4},{1,5},{2,6},{3,7},{4,0},{5,1},{6,2},{7,3},{8,12},{9,13},{10,... | collective-permute-start | bytes 294920 | tf_op jit(solution)/shard_map/ppermute | solution.py:311
  144.8 2.0 %collective-permute-done.4 = bf16[1,3,128,128]{3,2,1,0:T(8,128)(2,1)S(1)} collective-permute-done((bf16[1,3,128,128]{3,2,1,0:T(8,128)(2,1)S(1)}, bf16[1,3,128,128]{3,2,1,0:T(8,128)(2,1)S(1)}, u32[]{:S(2)}, u32[]{:S(2)}) %collective-permute-start.4) | collective-permute-done | bytes 98336 | tf_op jit(solution)/shard_map/ppermute | solution.py:311
  146.8 1.3 collective-permute-start.5
  148.2 3.2 %collective-permute-done.5 = bf16[2,3,128,128]{3,2,1,0:T(8,128)(2,1)S(1)} collective-permute-done((bf16[2,3,128,128]{3,2,1,0:T(8,128)(2,1)S(1)}, bf16[2,3,128,128]{3,2,1,0:T(8,128)(2,1)S(1)}, u32[]{:S(2)}, u32[]{:S(2)}) %collective-permute-start.5) | collective-permute-done | bytes 196640 | tf_op jit(solution)/shard_map/ppermute | solution.py:311
  151.5 3.0 %collective-permute-start.6 = (bf16[4,3,128,128]{3,2,1,0:T(8,128)(2,1)S(1)}, bf16[4,3,128,128]{3,2,1,0:T(8,128)(2,1)}, u32[]{:S(2)}, u32[]{:S(2)}) collective-permute-start(bf16[4,3,128,128]{3,2,1,0:T(8,128)(2,1)S(1)} %pad_maximum_fusion.1), channel_id=1, source_target_pairs={{0,1},{1,0},{2,3},{3,2},{4,5},{5,4},{6,7},{7,6},{8,9},{9,8},{10,11... | collective-permute-start | bytes 1179656 | tf_op jit(solution)/shard_map/ppermute | solution.py:311
  154.4 0.6 dynamic_slice.3
  155.6 0.2 collective-permute-done.6
  155.9 1.1 pad_maximum_fusion.inverse_ref
  157.0 1.2 copy-done.3
  158.2 3.3 %shard_map.63 = bf16[8,256,256]{2,1,0:T(8,128)(2,1)} custom-call(s32[1]{0:T(128)} %bitcast.3.base_ref, bf16[8,256,256]{2,1,0:T(8,128)(2,1)S(1)} %copy-done.3, bf16[8,3,128,128]{3,2,1,0:T(8,128)(2,1)S(1)} %pad_maximum_fusion.inverse_ref), custom_call_target="tpu_custom_call" | custom-call | tf_op jit(solution)/shard_map/pallas_call | solution.py:250
  161.5 8.0 %shard_map.62 = bf16[768,256]{1,0:T(8,128)(2,1)} custom-call(s32[1]{0:T(128)} %bitcast.1.slot_ref, bf16[768,4096]{1,0:T(8,128)(2,1)} %bitcast.17, bf16[16,256,256]{2,1,0:T(8,128)(2,1)S(1)} %all-to-all-done.1.gathered_ref, bf16[8,3,128,128]{3,2,1,0:T(8,128)(2,1)S(1)} %pad_maximum_fusion.inverse_ref), custom_call_target="tpu_custom_call" | custom-call | tf_op jit(solution)/shard_map/pallas_call | solution.py:293
  (17 shorter events, 0.2 us)
Async XLA Ops:
  0.6 1.3 copy-start.1
  1.9 1.0 copy-start.4
  11.2 54.1 %copy-start.5 = (s32[16]{0:T(128)S(1)}, s32[16]{0:T(128)}, u32[]{:S(2)}) copy-start(s32[16]{0:T(128)} %member_ref.1) | copy-start | bytes 196
  11.2 52.7 %all-to-all-start = ((bf16[16,256,256]{2,1,0:T(8,128)(2,1)}), bf16[16,256,256]{2,1,0:T(8,128)(2,1)S(1)}, u32[]{:S(2)}, u32[]{:S(2)}) async-start(bf16[16,256,256]{2,1,0:T(8,128)(2,1)} %shard_map.59), calls=%async_computation | async-start | bytes 4194304 | tf_op jit(solution)/shard_map/all_to_all | solution.py:315
  64.0 1.3 copy-start.7
  68.8 1.3 copy-start
  70.2 1.0 copy-start.2
  71.2 0.9 copy-start.6
  72.0 89.4 %all-to-all-start.1 = ((bf16[16,256,256]{2,1,0:T(8,128)(2,1)}), bf16[16,256,256]{2,1,0:T(8,128)(2,1)S(1)}, u32[]{:S(2)}, u32[]{:S(2)}) async-start(bf16[16,256,256]{2,1,0:T(8,128)(2,1)} %copy-done), calls=%async_computation.1 | async-start | bytes 4194304 | tf_op jit(solution)/shard_map/all_to_all | solution.py:315
  78.4 2.5 %collective-permute-start = (f32[4,3,128,128]{3,2,1,0:T(8,128)}, f32[4,3,128,128]{3,2,1,0:T(8,128)S(1)}, u32[]{:S(2)}, u32[]{:S(2)}) collective-permute-start(f32[4,3,128,128]{3,2,1,0:T(8,128)} %copy-done.6), channel_id=1, source_target_pairs={{0,1},{1,0},{2,3},{3,2},{4,5},{5,4},{6,7},{7,6},{8,9},{9,8},{10,11... | collective-permute-start | bytes 2359304 | tf_op jit(solution)/shard_map/ppermute | solution.py:311
  81.0 20.2 %collective-permute-start.1 = (f32[2,3,128,128]{3,2,1,0:T(8,128)S(1)}, f32[2,3,128,128]{3,2,1,0:T(8,128)S(1)}, u32[]{:S(2)}, u32[]{:S(2)}) collective-permute-start(f32[2,3,128,128]{3,2,1,0:T(8,128)S(1)} %slice.17), channel_id=1, source_target_pairs={{0,2},{1,3},{2,0},{3,1},{4,6},{5,7},{6,4},{7,5},{8,10},{9,11},{10,... | collective-permute-start | bytes 1179656 | tf_op jit(solution)/shard_map/ppermute | solution.py:311
  101.4 16.6 %collective-permute-start.2 = (f32[1,3,128,128]{3,2,1,0:T(8,128)S(1)}, f32[1,3,128,128]{3,2,1,0:T(8,128)S(1)}, u32[]{:S(2)}, u32[]{:S(2)}) collective-permute-start(f32[1,3,128,128]{3,2,1,0:T(8,128)S(1)} %slice.19), channel_id=1, source_target_pairs={{0,4},{1,5},{2,6},{3,7},{4,0},{5,1},{6,2},{7,3},{8,12},{9,13},{10,... | collective-permute-start | bytes 589832 | tf_op jit(solution)/shard_map/ppermute | solution.py:311
  117.9 14.3 %collective-permute-start.3 = (f32[1,3,128,128]{3,2,1,0:T(8,128)S(1)}, f32[1,3,128,128]{3,2,1,0:T(8,128)S(1)}, u32[]{:S(2)}, u32[]{:S(2)}) collective-permute-start(f32[1,3,128,128]{3,2,1,0:T(8,128)S(1)} %slice_add_fusion.1), channel_id=1, source_target_pairs={{0,8},{1,9},{2,10},{3,11},{4,12},{5,13},{6,14},{7,15},{8,0},{9,1},... | collective-permute-start | bytes 589832 | tf_op jit(solution)/shard_map/ppermute | solution.py:311
  141.7 5.0 %collective-permute-start.4 = (bf16[1,3,128,128]{3,2,1,0:T(8,128)(2,1)S(1)}, bf16[1,3,128,128]{3,2,1,0:T(8,128)(2,1)S(1)}, u32[]{:S(2)}, u32[]{:S(2)}) collective-permute-start(bf16[1,3,128,128]{3,2,1,0:T(8,128)(2,1)S(1)} %bitcast.10), channel_id=1, source_target_pairs={{0,4},{1,5},{2,6},{3,7},{4,0},{5,1},{6,2},{7,3},{8,12},{9,13},{10,... | collective-permute-start | bytes 294920 | tf_op jit(solution)/shard_map/ppermute | solution.py:311
  146.8 4.6 %collective-permute-start.5 = (bf16[2,3,128,128]{3,2,1,0:T(8,128)(2,1)S(1)}, bf16[2,3,128,128]{3,2,1,0:T(8,128)(2,1)S(1)}, u32[]{:S(2)}, u32[]{:S(2)}) collective-permute-start(bf16[2,3,128,128]{3,2,1,0:T(8,128)(2,1)S(1)} %pad_maximum_fusion.2), channel_id=1, source_target_pairs={{0,2},{1,3},{2,0},{3,1},{4,6},{5,7},{6,4},{7,5},{8,10},{9,11},{10,... | collective-permute-start | bytes 589832 | tf_op jit(solution)/shard_map/ppermute | solution.py:311
  151.5 4.4 %collective-permute-start.6 = (bf16[4,3,128,128]{3,2,1,0:T(8,128)(2,1)S(1)}, bf16[4,3,128,128]{3,2,1,0:T(8,128)(2,1)}, u32[]{:S(2)}, u32[]{:S(2)}) collective-permute-start(bf16[4,3,128,128]{3,2,1,0:T(8,128)(2,1)S(1)} %pad_maximum_fusion.1), channel_id=1, source_target_pairs={{0,1},{1,0},{2,3},{3,2},{4,5},{5,4},{6,7},{7,6},{8,9},{9,8},{10,11... | collective-permute-start | bytes 1179656 | tf_op jit(solution)/shard_map/ppermute | solution.py:311
  157.0 1.2 copy-start.3

commit v2 on v1

v2 whole, which is shorter than its diff:
```python
import functools
import math

import jax
import jax.numpy as jnp
from jax import lax
from jax.experimental import pallas as pl
from jax.experimental.pallas import tpu as pltpu
from jax.sharding import PartitionSpec as P

F32 = jnp.float32
BF16 = jnp.bfloat16
MIB = 1024 * 1024
PANEL = 8
BLOCK = 64
AHEAD = 6
PLAN = {"sum": (1, 1), "last": (0, 2), "invert": (2, 2), "share": (1, 1)}
VMEM = pl.BlockSpec(memory_space=pltpu.VMEM)
SMEM = pl.BlockSpec(memory_space=pltpu.SMEM)
HBM = pl.BlockSpec(memory_space=pltpu.MemorySpace.HBM)


def dot(a, b, dims):
    return lax.dot_general(a, b, (dims, ((), ())), preferred_element_type=F32)


def params(mib=24):
    return pltpu.CompilerParams(vmem_limit_bytes=mib * MIB)


def base_cluster(me, devices):
    last = devices.bit_length() - 2
    return sum(((me >> s) & 1) << (last - 1 - s) for s in range(last))


def weight_copies(me, weights_hbm, weights, sems, rows, half, far):
    quarter = half // 2
    columns = quarter * rows
    own = me // half
    first = (1 - own if far else own) * 2
    copies = []
    for part in range(2):
        start = (first + (me % half // quarter ^ part)) * columns
        copies.append(
            pltpu.make_async_copy(
                weights_hbm.at[:, pl.ds(pl.multiple_of(start, columns), columns)],
                weights.at[part],
                sems.at[part],
            )
        )
    return copies


def slot_blocks(me, weighted, weights, copy, part, product, outs):
    count = product.shape[0]
    rows = product.shape[2]
    copy.wait()
    wide = dot(weighted, weights[part], ((1,), (0,))).astype(BF16)
    for b in range(count):
        product[b] = wide[:, b * rows : (b + 1) * rows]
    for t in range(count):
        outs[part * count + t][...] = product[me % count ^ t]


def far_partial_kernel(half, ids_ref, cov_hbm, sketch_hbm, weights_hbm, *refs):
    outs, weighted_ref = refs[:half], refs[half]
    cov, sketch, weights, product, in_sems, sems = refs[half + 1 :]
    me = ids_ref[0]
    cov_copy = pltpu.make_async_copy(cov_hbm, cov, in_sems.at[0])
    sketch_copy = pltpu.make_async_copy(sketch_hbm, sketch, in_sems.at[1])
    copies = weight_copies(me, weights_hbm, weights, sems, product.shape[2], half, True)
    cov_copy.start()
    sketch_copy.start()
    copies[0].start()
    cov_copy.wait()
    sketch_copy.wait()
    copies[1].start()
    weighted = dot(sketch[...], cov[...], ((0,), (1,))).astype(BF16)
    weighted_ref[...] = weighted
    for part in range(2):
        slot_blocks(me, weighted, weights, copies[part], part, product, outs)


def near_partial_kernel(half, ids_ref, weighted_ref, weights_hbm, *refs):
    outs = refs[:half]
    weights, product, sems = refs[half:]
    me = ids_ref[0]
    copies = weight_copies(me, weights_hbm, weights, sems, product.shape[2], half, False)
    for copy in copies:
        copy.start()
    for part in range(2):
        slot_blocks(me, weighted_ref[...], weights, copies[part], part, product, outs)


def partial_blocks(ids, cov, sketch, weights, devices):
    hidden, width = weights.shape
    rank = sketch.shape[1]
    rows = width // devices
    half = devices // 2
    block = jax.ShapeDtypeStruct((rank, rows), BF16)
    scratch = [
        pltpu.VMEM((2, hidden, width // 4), BF16),
        pltpu.VMEM((half // 2, rank, rows), BF16),
    ]
    sems = pltpu.SemaphoreType.DMA((2,))
    *far, weighted = pl.pallas_call(
        functools.partial(far_partial_kernel, half),
        in_specs=[SMEM, HBM, HBM, HBM],
        out_specs=[VMEM] * (half + 1),
        out_shape=[block] * half + [jax.ShapeDtypeStruct((rank, hidden), BF16)],
        scratch_shapes=[pltpu.VMEM(cov.shape, BF16), pltpu.VMEM(sketch.shape, BF16)]
        + scratch
        + [sems, sems],
        compiler_params=params(62),
    )(ids, cov, sketch, weights)
    near = pl.pallas_call(
        functools.partial(near_partial_kernel, half),
        in_specs=[SMEM, VMEM, HBM],
        out_specs=[VMEM] * half,
        out_shape=[block] * half,
        scratch_shapes=scratch + [sems],
        compiler_params=params(),
    )(ids, weighted, weights)
    return [*near, *far]


def cluster_kernel(devices, ids_ref, member_ref, *refs):
    received, refs = refs[:devices], refs[devices:]
    rows_ref, keep_ref, send_ref = refs[:3]
    blocks, total = refs[3 : 3 + devices], refs[-1]
    me = ids_ref[0]
    base = base_cluster(me, devices)
    half = rows_ref.shape[1] // 2
    total[...] = jnp.zeros_like(total)
    for s in range(devices):
        c = member_ref[me ^ s]
        total[c] = total[c] + received[s][...].astype(F32)
    rows_ref[...] = total[...].astype(BF16)
    for s in range(devices):
        blocks[s][...] = rows_ref[member_ref[me ^ s]]
    kept = keep_ref.shape[0]

    @pl.loop(0, kept)
    def _(k):
        for out_ref, slot in ((send_ref, k + kept), (keep_ref, k)):
            block = rows_ref[base ^ slot]
            full = dot(block, block, ((1,), (1,)))
            out_ref[k, 0] = full[:half, :half]
            out_ref[k, 1] = full[half:, :half]
            out_ref[k, 2] = full[half:, half:]


def cluster_sums(ids, members, received):
    devices = len(received)
    clusters = devices // 2
    rank, rows = received[0].shape
    gram = jax.ShapeDtypeStruct((clusters // 2, 3, rank // 2, rank // 2), F32)
    block = jax.ShapeDtypeStruct((rank, rows), BF16)
    rows_t, keep, send, *blocks = pl.pallas_call(
        functools.partial(cluster_kernel, devices),
        in_specs=[SMEM, SMEM] + [VMEM] * devices,
        out_specs=[VMEM] * (devices + 3),
        out_shape=[jax.ShapeDtypeStruct((clusters, rank, rows), BF16), gram, gram]
        + [block] * devices,
        scratch_shapes=[pltpu.VMEM((clusters, rank, rows), F32)],
        compiler_params=params(),
    )(ids, members, *received)
    return rows_t, keep, send, blocks


def stacked(x, axis, order):
    high = x.astype(BF16)
    rest = x - high.astype(F32)
    middle = rest.astype(BF16)
    low = (rest - middle.astype(F32)).astype(BF16)
    return jnp.concatenate([(high, middle, low)[i] for i in order], axis=axis)


def stack_left(x, axis):
    return stacked(x, axis, (0, 0, 1, 0, 2, 1))


def stack_right(x, axis):
    return stacked(x, axis, (0, 1, 0, 2, 0, 1))


def block_inverse(square):
    size = square.shape[0]
    lanes = 128
    groups = size // 8
    row = lax.broadcasted_iota(jnp.int32, (size, size), 0)
    col = lax.broadcasted_iota(jnp.int32, (size, size), 1)
    parts = [square, jnp.where(row == col, 1.0, 0.0)]
    if lanes > 2 * size:
        parts.append(jnp.zeros((size, lanes - 2 * size), F32))
    table = jnp.concatenate(parts, axis=1)
    tiles = [table[8 * g : 8 * g + 8, :] for g in range(groups)]
    sub = lax.broadcasted_iota(jnp.int32, (8, lanes), 0)
    pivots = [jnp.ones((8, lanes), F32) for _ in range(groups)]

    def spread(x):
        return jnp.broadcast_to(x, (8, lanes))

    for k in range(0, size, PANEL):
        first = k // 8
        columns = [
            [spread(tiles[g][:, k + i : k + i + 1]) for g in range(first, groups)]
            for i in range(PANEL)
        ]
        s = {}
        for m in range(PANEL):
            for i in range(m, PANEL):
                q = k + i
                s[m, i] = spread(columns[m][q // 8 - first][q % 8 : q % 8 + 1, :])
        rows = [spread(tiles[(k + i) // 8][(k + i) % 8 : (k + i) % 8 + 1, :]) for i in range(PANEL)]
        inverse = []
        for m in range(PANEL):
            inverse.append(1.0 / s[m, m])
            for i in range(m + 1, PANEL):
                factor = s[m, i] * inverse[m]
                for t in range(i, PANEL):
                    s[i, t] = s[i, t] - factor * s[m, t]
                rows[i] = rows[i] - factor * rows[m]
        factors = []
        for m in range(PANEL):
            column = []
            for g in range(groups - first):
                x = columns[m][g]
                for t in range(m):
                    x = x - factors[t][g] * s[t, m]
                column.append(x * inverse[m])
            factors.append(column)
        for g in range(first, groups):
            tile = tiles[g]
            for m in range(PANEL):
                x = factors[m][g - first]
                if 8 * g <= k + m:
                    x = jnp.where(sub + 8 * g > k + m, x, 0.0)
                tile = tile - x * rows[m]
            tiles[g] = tile
        for m in range(PANEL):
            q = k + m
            pivots[q // 8] = jnp.where(sub == q % 8, s[m, m], pivots[q // 8])
    out = [tiles[g] * lax.rsqrt(pivots[g]) for g in range(groups)]
    return jnp.concatenate(out, axis=0)[:, size : 2 * size]


def invert(work):
    n = work.shape[0]
    for top in range(0, n, BLOCK):
        left = top // 128 * 128
        bottom = top + BLOCK
        square = work[top:bottom, left : left + 128][:, top - left : bottom - left]
        scaled = dot(
            stack_left(block_inverse(square), 1), stack_right(work[top:bottom, :], 0), ((1,), (0,))
        )
        work[top:bottom, n:] = scaled[:, n:]
        if bottom < n:
            start = bottom // 128 * 128
            change = dot(stack_left(scaled[:, start:n], 0), stack_right(scaled, 0), ((0,), (0,)))
            work[bottom:, :] = work[bottom:, :] - change[bottom - start :, :]


def identity(n):
    row = lax.broadcasted_iota(jnp.int32, (n, n), 0)
    col = lax.broadcasted_iota(jnp.int32, (n, n), 1)
    return jnp.where(row == col, 1.0, 0.0)


def inverse_kernel(scale, gram_ref, rows_t_ref, out_ref, rows_ref, work):
    for c in range(rows_ref.shape[0]):
        rows_ref[c] = rows_t_ref[c].T
    half = gram_ref.shape[1]
    n = 2 * half
    work[:half, :half] = gram_ref[0]
    work[half:, :half] = gram_ref[1]
    work[:half, half:n] = gram_ref[1].T
    work[half:, half:n] = gram_ref[2]
    work[:, n:] = identity(n)
    invert(work)
    out_ref[0] = (scale * work[:half, n : n + half]).astype(BF16)
    out_ref[1] = (scale * work[half:, n : n + half]).astype(BF16)
    out_ref[2] = (scale * work[half:, n + half :]).astype(BF16)


def inverse_factor(gram, rows_t, scale):
    half = gram.shape[1]
    clusters, rank, rows = rows_t.shape
    return pl.pallas_call(
        functools.partial(inverse_kernel, scale),
        in_specs=[VMEM] * 2,
        out_specs=[VMEM] * 2,
        out_shape=[
            jax.ShapeDtypeStruct(gram.shape, BF16),
            jax.ShapeDtypeStruct((clusters, rows, rank), BF16),
        ],
        scratch_shapes=[pltpu.VMEM((2 * half, 4 * half), F32)],
        compiler_params=params(),
    )(gram, rows_t)


def basis_kernel(ids_ref, rows_ref, near_ref, far_ref, out_hbm, out, sems):
    half = out.shape[2] // 2
    count = near_ref.shape[0]
    base = base_cluster(ids_ref[0], 4 * count)

    def copy(k):
        return pltpu.make_async_copy(out.at[k], out_hbm.at[base ^ k], sems.at[k])

    for k in range(2 * count):
        refs, i = (near_ref, k) if k < count else (far_ref, k - count)
        block = rows_ref[base ^ k]
        out[k, :, :half] = dot(block[:, :half], refs[i, 0], ((1,), (1,))).astype(BF16)
        out[k, :, half:] = (
            dot(block[:, :half], refs[i, 1], ((1,), (1,)))
            + dot(block[:, half:], refs[i, 2], ((1,), (1,)))
        ).astype(BF16)
        copy(k).start()
    for k in range(2 * count):
        copy(k).wait()


def basis_rows(ids, rows, near, far):
    return pl.pallas_call(
        basis_kernel,
        in_specs=[SMEM] + [VMEM] * 3,
        out_specs=HBM,
        out_shape=jax.ShapeDtypeStruct(rows.shape, BF16),
        scratch_shapes=[pltpu.VMEM(rows.shape, BF16), pltpu.SemaphoreType.DMA((rows.shape[0],))],
        compiler_params=params(),
    )(ids, rows, near, far)


def column_block(ref, index, rows):
    if rows % 128 == 0:
        return ref[:, pl.ds(pl.multiple_of(index * rows, rows), rows)]
    share = 128 // rows
    wide = ref[:, pl.ds(pl.multiple_of(index // share * 128, 128), 128)]
    block = wide[:, :rows]
    for i in range(1, share):
        block = jnp.where(index % share == i, wide[:, i * rows : (i + 1) * rows], block)
    return block


def first_product_kernel(ids_ref, weights_hbm, *refs):
    *blocks, out_ref, weights, sem = refs
    me = ids_ref[0]
    rows = blocks[0].shape[1]
    copy = pltpu.make_async_copy(weights_hbm, weights, sem)
    copy.start()
    copy.wait()
    total = None
    for s, block in enumerate(blocks):
        term = dot(column_block(weights, me ^ s, rows), block[...], ((1,), (1,)))
        total = term if total is None else total + term
    out_ref[...] = total


def coef_kernel(ids_ref, member_ref, weights_hbm, first_ref, near_ref, far_ref, *refs):
    *blocks, out_hbm, weights, out, sem, out_sem = refs
    me = ids_ref[0]
    slot = member_ref[me] ^ base_cluster(me, member_ref.shape[0])
    rows = blocks[0].shape[1]
    count = len(blocks)
    columns = count * rows
    start = (me // count ^ 3) * columns
    copy = pltpu.make_async_copy(
        weights_hbm.at[:, pl.ds(pl.multiple_of(start, columns), columns)], weights, sem
    )
    copy.start()
    copy.wait()
    total = first_ref[...]
    for t, block in enumerate(blocks):
        total = total + dot(
            column_block(weights, me % count ^ t, rows), block[...], ((1,), (1,))
        )
    high = total.astype(BF16)
    low = (total - high.astype(F32)).astype(BF16)
    near = slot < near_ref.shape[0]
    inside = lax.rem(slot, near_ref.shape[0])
    half = out.shape[1] // 2

    def times(i, part):
        factor = jnp.where(near, near_ref[inside, i], far_ref[inside, i])
        return dot(high[:, part], factor, ((1,), (1,))) + dot(low[:, part], factor, ((1,), (1,)))

    left, right = slice(0, half), slice(half, 2 * half)
    out[:, left] = times(0, left).astype(BF16)
    out[:, right] = (times(1, left) + times(2, right)).astype(BF16)
    out_copy = pltpu.make_async_copy(out, out_hbm, out_sem)
    out_copy.start()
    out_copy.wait()


def first_product(ids, weights, blocks):
    rank = blocks[0].shape[0]
    return pl.pallas_call(
        first_product_kernel,
        in_specs=[SMEM, HBM] + [VMEM] * len(blocks),
        out_specs=VMEM,
        out_shape=jax.ShapeDtypeStruct((weights.shape[0], rank), F32),
        scratch_shapes=[pltpu.VMEM(weights.shape, BF16), pltpu.SemaphoreType.DMA],
        compiler_params=params(),
    )(ids, weights, *blocks)


def coefficients(ids, members, weights, first, near, far, blocks):
    hidden = weights.shape[0]
    rank, rows = blocks[0].shape
    return pl.pallas_call(
        coef_kernel,
        in_specs=[SMEM, SMEM, HBM] + [VMEM] * (len(blocks) + 3),
        out_specs=HBM,
        out_shape=jax.ShapeDtypeStruct((hidden, rank), BF16),
        scratch_shapes=[
            pltpu.VMEM((hidden, len(blocks) * rows), BF16),
            pltpu.VMEM((hidden, rank), BF16),
            pltpu.SemaphoreType.DMA,
            pltpu.SemaphoreType.DMA,
        ],
        compiler_params=params(),
    )(ids, members, weights, first, near, far, *blocks)


def swap(block, distance):
    count = lax.axis_size("expert")
    return lax.ppermute(block, "expert", [(i, i ^ distance) for i in range(count)])


def tied(value, values, keys):
    value, *others = lax.optimization_barrier((value, *[values[k] for k in keys]))
    values.update(zip(keys, others))
    return value


def halves(keep, other):
    cut = keep.shape[0] // 2
    return keep[:cut] + other[:cut], keep[cut:] + other[cut:]


def local(down_proj, cov_factor, sketch, membership):
    devices = lax.axis_size("expert")
    weights = down_proj[0]
    width = weights.shape[1]
    last = devices.bit_length() - 2
    half, quarter = devices // 2, devices // 4
    me = lax.axis_index("expert")
    ids = me.astype(jnp.int32).reshape(1)

    blocks = partial_blocks(ids, cov_factor[0], sketch[0], weights, devices)
    order = [half]
    for s in range(1, half):
        order += [half + s, s]
    got = {0: blocks[0]}
    for k, s in enumerate(order):
        block = blocks[s]
        if k >= AHEAD:
            block = tied(block, got, order[k - AHEAD : k - AHEAD + 1])
        got[s] = swap(block, s)

    rows_t, keep, send, blocks = cluster_sums(ids, membership, [got[s] for s in range(devices)])

    crossing, inner = list(range(half, devices)), list(range(1, half))
    values = {0: blocks[0]}
    unit = max(1, devices // 16)

    def start(across, within, gate):
        keys = []
        for queue, count in ((crossing, across), (inner, within)):
            for _ in range(min(count * unit, len(queue))):
                s = queue.pop(0)
                block = blocks[s]
                if gate is not None:
                    block, gate = lax.optimization_barrier((block, gate))
                values[s] = swap(block, s)
                keys.append(s)
        return keys, gate

    other = swap(send, 1)
    waiting, _ = start(1, 1, None)
    for bit in range(1, last):
        keep, send = halves(keep, other)
        if bit > 1:
            send = tied(send, values, waiting)
            waiting, send = start(*PLAN["sum"], send)
        other = swap(send, 1 << bit)
    gram = tied(keep + other, values, waiting)
    waiting, gram = start(*PLAN["last"], gram)
    gram = gram + swap(gram, half)
    gram = tied(gram, values, waiting)
    waiting, gram = start(*PLAN["invert"], gram)
    inverse, rows = inverse_factor(gram[0], rows_t, math.sqrt(width))
    near = tied(inverse[None], values, waiting)
    for bit in reversed(range(1, last)):
        waiting, near = start(*PLAN["share"], near)
        near = jnp.concatenate([near, swap(near, 1 << bit)], axis=0)
        near = tied(near, values, waiting)
    far = swap(near, 1)
    start(devices, devices, near)

    first = first_product(ids, weights, [values[s] for s in range(half + quarter)])
    basis = basis_rows(ids, rows, near, far)
    coef = coefficients(
        ids, membership, weights, first, near, far, [values[s] for s in range(half + quarter, devices)]
    )
    return (coef[None], basis)


def solution(mesh):
    placed = (
        P(("groups", "expert"), None, None),
        P(("groups", "expert"), None, None),
        P(("groups", "expert"), None, None),
        P("groups"),
    )
    return jax.shard_map(
        local,
        mesh=mesh,
        in_specs=placed,
        out_specs=(P(("groups", "expert"), None, None), P("groups", "expert", None)),
        check_vma=False,
    )
```

time: 173 us -> 152 us (0.88); the launches traced: 170 us -> 152 us
  waiting for transfers between devices: 96 us -> 62.3 us
  starting transfers between devices: 29.5 us -> 59.9 us
  Pallas kernels: 32.7 us -> 24.5 us
  local copies, waits for them, and re-layouts: 8.65 us -> 3.82 us
    all_to_all x2 -> x0, waiting for transfers between devices: 46 us -> none  [exchange(): lax.all_to_all(blocks, 'expert', split_axis=0, concat_axis=0, tiled=True)]
    ppermute x7 -> x37, starting transfers between devices: 16.4 us -> 59.9 us  [swap(): lax.ppermute(block, 'expert', [(i, i ^ distance) for i in range(count)])]
    all_to_all x2 -> x0, starting transfers between devices: 13.1 us -> none  [exchange(): lax.all_to_all(blocks, 'expert', split_axis=0, concat_axis=0, tiled=True)]
    ppermute x7 -> x37, waiting for transfers between devices: 50 us -> 62.3 us  [swap(): lax.ppermute(block, 'expert', [(i, i ^ distance) for i in range(count)])]
    pallas_call x5 -> x7, Pallas kernels: 32.7 us -> 24.5 us  [the longest x1 9.56 us: inverse_factor(): pl.pallas_call(functools.partial(inverse_kernel, scale), in_specs=[VMEM]...]
    unnamed x16 -> x22, local copies, waits for them, and re-layouts: 8.02 us -> 3.82 us
  transfers between devices with their start and end apart: 9 -> 37, of which waited for: 8 -> 21; matrix products, arithmetic and copies ran while one was open for 1% -> 0% of each run, Pallas kernels for 8% -> 10%
where the time goes in v2:
time: 152 us
  waiting for transfers between devices  62.3 us (41%)
  starting transfers between devices  59.9 us (39%)
  Pallas kernels  24.5 us (16%)
  local copies, waits for them, and re-layouts  3.82 us (3%)
    ppermute x37, waiting for transfers between devices, swap(): lax.ppermute(block, 'expert', [(i, i ^ distance) for i in range(count)])  62.3 us
    ppermute x37, starting transfers between devices, swap(): lax.ppermute(block, 'expert', [(i, i ^ distance) for i in range(count)])  59.9 us
    pallas_call x1, Pallas kernels, inverse_factor(): pl.pallas_call(functools.partial(inverse_kernel, scale), in_specs=[VMEM]...  9.56 us
    pallas_call x1, Pallas kernels, partial_blocks(): pl.pallas_call(functools.partial(far_partial_kernel, half), in_specs=[SME...  4.43 us
    unnamed x22, local copies, waits for them, and re-layouts  3.82 us
    pallas_call x1, Pallas kernels, coefficients(): pl.pallas_call(coef_kernel, in_specs=[SMEM, SMEM, HBM] + [VMEM] * (len(bl...  3.05 us
  transfers between devices with their start and end apart: 37, of which 21 were waited for; matrix products, arithmetic and copies ran while one was open for 0% of the time, Pallas kernels for 10%

profile of v2, /device:TPU:9, one launch (start us, length us, event | category | flops | bytes accessed | tf_op | source)
XLA Modules:
  0.0 151.9 jit_solution(5456572960427954588)
XLA Ops:
  0.6 4.4 %shard_map.59 = (bf16[256,256]{1,0:T(8,128)(2,1)}, bf16[256,256]{1,0:T(8,128)(2,1)}, bf16[256,256]{1,0:T(8,128)(2,1)}, bf16[256,256]{1,0:T(8,128)(2,1)}, bf16[25...) custom-call(s32[1]{0:T(128)} %bitcast.ids_ref, ...), custom_call_target="tpu_custom_call" | custom-call | tf_op jit(solution)/shard_map/pallas_call | solution.py:106
  5.1 2.9 %collective-permute-start.8 = (bf16[256,256]{1,0:T(8,128)(2,1)}, bf16[256,256]{1,0:T(8,128)(2,1)S(1)}, u32[]{:S(2)}, u32[]{:S(2)}) collective-permute-start(bf16[256,256]{1,0:T(8,128)(2,1)} %get-tuple-element.121), channel_id=1, source_target_pairs={{0,9},{1,8},{2,11},{3,10},{4,13},{5,12},{6,15},{7,14},{8,1},{9,0},... | collective-permute-start | bytes 393224 | tf_op jit(solution)/shard_map/ppermute | solution.py:427
  8.1 2.8 %copy-done = bf16[1,768,4096]{2,1,0:T(8,128)(2,1)S(1)} copy-done((bf16[1,768,4096]{2,1,0:T(8,128)(2,1)S(1)}, bf16[1,768,4096]{2,1,0:T(8,128)(2,1)}, u32[]{:S(2)}) %copy-start) | copy-done | bytes 6291480
  14.1 2.9 %collective-permute-start.9 = (bf16[256,256]{1,0:T(8,128)(2,1)S(1)}, bf16[256,256]{1,0:T(8,128)(2,1)S(1)}, u32[]{:S(2)}, u32[]{:S(2)}) collective-permute-start(bf16[256,256]{1,0:T(8,128)(2,1)S(1)} %copy-done.8), channel_id=1, source_target_pairs={{0,10},{1,11},{2,8},{3,9},{4,14},{5,15},{6,12},{7,13},{8,2},{9,3},... | collective-permute-start | bytes 393224 | tf_op jit(solution)/shard_map/ppermute | solution.py:427
  17.7 6.2 %collective-permute-start.1 = (bf16[256,256]{1,0:T(8,128)(2,1)S(1)}, bf16[256,256]{1,0:T(8,128)(2,1)S(1)}, u32[]{:S(2)}, u32[]{:S(2)}) collective-permute-start(bf16[256,256]{1,0:T(8,128)(2,1)S(1)} %get-tuple-element.106), channel_id=1, source_target_pairs={{0,2},{1,3},{2,0},{3,1},{4,6},{5,7},{6,4},{7,5},{8,10},{9,11},{10,... | collective-permute-start | bytes 393224 | tf_op jit(solution)/shard_map/ppermute | solution.py:427
  28.3 3.3 %collective-permute-start.4 = (bf16[256,256]{1,0:T(8,128)(2,1)S(1)}, bf16[256,256]{1,0:T(8,128)(2,1)S(1)}, u32[]{:S(2)}, u32[]{:S(2)}) collective-permute-start(bf16[256,256]{1,0:T(8,128)(2,1)S(1)} %get-tuple-element.114), channel_id=1, source_target_pairs={{0,4},{1,5},{2,6},{3,7},{4,0},{5,1},{6,2},{7,3},{8,12},{9,13},{10,... | collective-permute-start | bytes 393224 | tf_op jit(solution)/shard_map/ppermute | solution.py:427
  31.6 2.2 %collective-permute-done.10.refs_11_ = bf16[256,256]{1,0:T(8,128)(2,1)S(1)} collective-permute-done((bf16[256,256]{1,0:T(8,128)(2,1)S(1)}, bf16[256,256]{1,0:T(8,128)(2,1)S(1)}, u32[]{:S(2)}, u32[]{:S(2)}) %collective-permute-start.10) | collective-permute-done | bytes 131104 | tf_op jit(solution)/shard_map/ppermute | solution.py:427
  33.8 2.7 %collective-permute-start.13 = (bf16[256,256]{1,0:T(8,128)(2,1)S(1)}, bf16[256,256]{1,0:T(8,128)(2,1)S(1)}, u32[]{:S(2)}, u32[]{:S(2)}) collective-permute-start(bf16[256,256]{1,0:T(8,128)(2,1)S(1)} %copy-done.4), channel_id=1, source_target_pairs={{0,14},{1,15},{2,12},{3,13},{4,10},{5,11},{6,8},{7,9},{8,6},{9,7},... | collective-permute-start | bytes 393224 | tf_op jit(solution)/shard_map/ppermute | solution.py:427
  36.8 3.2 %collective-permute-start.5 = (bf16[256,256]{1,0:T(8,128)(2,1)S(1)}, bf16[256,256]{1,0:T(8,128)(2,1)S(1)}, u32[]{:S(2)}, u32[]{:S(2)}) collective-permute-start(bf16[256,256]{1,0:T(8,128)(2,1)S(1)} %get-tuple-element.116), channel_id=1, source_target_pairs={{0,5},{1,4},{2,7},{3,6},{4,1},{5,0},{6,3},{7,2},{8,13},{9,12},{10,... | collective-permute-start | bytes 393224 | tf_op jit(solution)/shard_map/ppermute | solution.py:427
  40.0 3.2 %collective-permute-start.14 = (bf16[256,256]{1,0:T(8,128)(2,1)S(1)}, bf16[256,256]{1,0:T(8,128)(2,1)S(1)}, u32[]{:S(2)}, u32[]{:S(2)}) collective-permute-start(bf16[256,256]{1,0:T(8,128)(2,1)S(1)} %copy-done.3), channel_id=1, source_target_pairs={{0,15},{1,14},{2,13},{3,12},{4,11},{5,10},{6,9},{7,8},{8,7},{9,6},... | collective-permute-start | bytes 393224 | tf_op jit(solution)/shard_map/ppermute | solution.py:427
  46.0 2.7 %collective-permute-done.13.refs_14_ = bf16[256,256]{1,0:T(8,128)(2,1)S(1)} collective-permute-done((bf16[256,256]{1,0:T(8,128)(2,1)S(1)}, bf16[256,256]{1,0:T(8,128)(2,1)S(1)}, u32[]{:S(2)}, u32[]{:S(2)}) %collective-permute-start.13) | collective-permute-done | bytes 131104 | tf_op jit(solution)/shard_map/ppermute | solution.py:427
  49.6 6.8 %collective-permute-done.14.refs_15_ = bf16[256,256]{1,0:T(8,128)(2,1)S(1)} collective-permute-done((bf16[256,256]{1,0:T(8,128)(2,1)S(1)}, bf16[256,256]{1,0:T(8,128)(2,1)S(1)}, u32[]{:S(2)}, u32[]{:S(2)}) %collective-permute-start.14) | collective-permute-done | bytes 131104 | tf_op jit(solution)/shard_map/ppermute | solution.py:427
  56.7 3.0 %collective-permute-done.7.refs_7_ = bf16[256,256]{1,0:T(8,128)(2,1)S(1)} collective-permute-done((bf16[256,256]{1,0:T(8,128)(2,1)S(1)}, bf16[256,256]{1,0:T(8,128)(2,1)S(1)}, u32[]{:S(2)}, u32[]{:S(2)}) %collective-permute-start.7) | collective-permute-done | bytes 131104 | tf_op jit(solution)/shard_map/ppermute | solution.py:427
  59.7 2.3 %shard_map.61 = (bf16[8,256,256]{2,1,0:T(8,128)(2,1)S(1)}, f32[4,3,128,128]{3,2,1,0:T(8,128)S(1)}, f32[4,3,128,128]{3,2,1,0:T(8,128)S(1)}, bf16[256,256]{1,0:T(8...) custom-call(s32[1]{0:T(128)} %bitcast.ids_ref, ...), custom_call_target="tpu_custom_call" | custom-call | tf_op jit(solution)/shard_map/pallas_call | solution.py:159
  66.9 8.1 %collective-permute-done.16 = f32[2,3,128,128]{3,2,1,0:T(8,128)S(1)} collective-permute-done((f32[2,3,128,128]{3,2,1,0:T(8,128)S(1)}, f32[2,3,128,128]{3,2,1,0:T(8,128)S(1)}, u32[]{:S(2)}, u32[]{:S(2)}) %collective-permute-start.16) | collective-permute-done | bytes 393248 | tf_op jit(solution)/shard_map/ppermute | solution.py:427
  75.6 3.9 %collective-permute-start.20 = (bf16[256,256]{1,0:T(8,128)(2,1)S(1)}, bf16[256,256]{1,0:T(8,128)(2,1)S(1)}, u32[]{:S(2)}, u32[]{:S(2)}) collective-permute-start(bf16[256,256]{1,0:T(8,128)(2,1)S(1)} %get-tuple-element.146), channel_id=1, source_target_pairs={{0,9},{1,8},{2,11},{3,10},{4,13},{5,12},{6,15},{7,14},{8,1},{9,0},... | collective-permute-start | bytes 393224 | tf_op jit(solution)/shard_map/ppermute | solution.py:427
  80.3 5.5 %collective-permute-done.20.refs_9_ = bf16[256,256]{1,0:T(8,128)(2,1)S(1)} collective-permute-done((bf16[256,256]{1,0:T(8,128)(2,1)S(1)}, bf16[256,256]{1,0:T(8,128)(2,1)S(1)}, u32[]{:S(2)}, u32[]{:S(2)}) %collective-permute-start.20) | collective-permute-done | bytes 131104 | tf_op jit(solution)/shard_map/ppermute | solution.py:427
  87.4 2.3 %collective-permute-start.23 = (bf16[256,256]{1,0:T(8,128)(2,1)S(1)}, bf16[256,256]{1,0:T(8,128)(2,1)S(1)}, u32[]{:S(2)}, u32[]{:S(2)}) collective-permute-start(bf16[256,256]{1,0:T(8,128)(2,1)S(1)} %get-tuple-element.154), channel_id=1, source_target_pairs={{0,3},{1,2},{2,1},{3,0},{4,7},{5,6},{6,5},{7,4},{8,11},{9,10},{10,... | collective-permute-start | bytes 393224 | tf_op jit(solution)/shard_map/ppermute | solution.py:427
  89.7 5.8 %collective-permute-done.22 = f32[1,3,128,128]{3,2,1,0:T(8,128)S(1)} collective-permute-done((f32[1,3,128,128]{3,2,1,0:T(8,128)S(1)}, f32[1,3,128,128]{3,2,1,0:T(8,128)S(1)}, u32[]{:S(2)}, u32[]{:S(2)}) %collective-permute-start.22) | collective-permute-done | bytes 196640 | tf_op jit(solution)/shard_map/ppermute | solution.py:427
  95.7 2.3 %collective-permute-start.27 = (bf16[256,256]{1,0:T(8,128)(2,1)S(1)}, bf16[256,256]{1,0:T(8,128)(2,1)S(1)}, u32[]{:S(2)}, u32[]{:S(2)}) collective-permute-start(bf16[256,256]{1,0:T(8,128)(2,1)S(1)} %get-tuple-element.171), channel_id=1, source_target_pairs={{0,5},{1,4},{2,7},{3,6},{4,1},{5,0},{6,3},{7,2},{8,13},{9,12},{10,... | collective-permute-start | bytes 393224 | tf_op jit(solution)/shard_map/ppermute | solution.py:427
  98.0 3.4 %collective-permute-start.26 = (bf16[256,256]{1,0:T(8,128)(2,1)S(1)}, bf16[256,256]{1,0:T(8,128)(2,1)S(1)}, u32[]{:S(2)}, u32[]{:S(2)}) collective-permute-start(bf16[256,256]{1,0:T(8,128)(2,1)S(1)} %get-tuple-element.170), channel_id=1, source_target_pairs={{0,11},{1,10},{2,9},{3,8},{4,15},{5,14},{6,13},{7,12},{8,3},{9,2},... | collective-permute-start | bytes 393224 | tf_op jit(solution)/shard_map/ppermute | solution.py:427
  101.8 9.6 %shard_map.62 = (bf16[3,128,128]{2,1,0:T(8,128)(2,1)S(1)}, bf16[8,256,256]{2,1,0:T(8,128)(2,1)S(1)}) custom-call(f32[3,128,128]{2,1,0:T(8,128)S(1)} %bitcast.13, bf16[8,256,256]{2,1,0:T(8,128)(2,1)S(1)} %get-tuple-element.167.rows_t_ref), custom_call_target="tpu_custom_call" | custom-call | tf_op jit(solution)/shard_map/pallas_call | solution.py:289
  115.4 2.3 %collective-permute-start.30 = (bf16[256,256]{1,0:T(8,128)(2,1)S(1)}, bf16[256,256]{1,0:T(8,128)(2,1)S(1)}, u32[]{:S(2)}, u32[]{:S(2)}) collective-permute-start(bf16[256,256]{1,0:T(8,128)(2,1)S(1)} %get-tuple-element.180), channel_id=1, source_target_pairs={{0,12},{1,13},{2,14},{3,15},{4,8},{5,9},{6,10},{7,11},{8,4},{9,5},... | collective-permute-start | bytes 393224 | tf_op jit(solution)/shard_map/ppermute | solution.py:427
  117.7 3.6 %collective-permute-done.31.refs_7_ = bf16[256,256]{1,0:T(8,128)(2,1)S(1)} collective-permute-done((bf16[256,256]{1,0:T(8,128)(2,1)S(1)}, bf16[256,256]{1,0:T(8,128)(2,1)S(1)}, u32[]{:S(2)}, u32[]{:S(2)}) %collective-permute-start.31) | collective-permute-done | bytes 131104 | tf_op jit(solution)/shard_map/ppermute | solution.py:427
  121.3 2.2 %collective-permute-done.30.refs_0_ = bf16[256,256]{1,0:T(8,128)(2,1)S(1)} collective-permute-done((bf16[256,256]{1,0:T(8,128)(2,1)S(1)}, bf16[256,256]{1,0:T(8,128)(2,1)S(1)}, u32[]{:S(2)}, u32[]{:S(2)}) %collective-permute-start.30) | collective-permute-done | bytes 131104 | tf_op jit(solution)/shard_map/ppermute | solution.py:427
  123.5 3.5 %collective-permute-start.33 = (bf16[256,256]{1,0:T(8,128)(2,1)S(1)}, bf16[256,256]{1,0:T(8,128)(2,1)S(1)}, u32[]{:S(2)}, u32[]{:S(2)}) collective-permute-start(bf16[256,256]{1,0:T(8,128)(2,1)S(1)} %get-tuple-element.190), channel_id=1, source_target_pairs={{0,13},{1,12},{2,15},{3,14},{4,9},{5,8},{6,11},{7,10},{8,5},{9,4},... | collective-permute-start | bytes 393224 | tf_op jit(solution)/shard_map/ppermute | solution.py:427
  127.1 2.2 %collective-permute-done.32 = bf16[2,3,128,128]{3,2,1,0:T(8,128)(2,1)S(1)} collective-permute-done((bf16[2,3,128,128]{3,2,1,0:T(8,128)(2,1)S(1)}, bf16[2,3,128,128]{3,2,1,0:T(8,128)(2,1)S(1)}, u32[]{:S(2)}, u32[]{:S(2)}) %collective-permute-start.32) | collective-permute-done | bytes 196640 | tf_op jit(solution)/shard_map/ppermute | solution.py:427
  129.3 3.3 %collective-permute-done.33.refs_1_ = bf16[256,256]{1,0:T(8,128)(2,1)S(1)} collective-permute-done((bf16[256,256]{1,0:T(8,128)(2,1)S(1)}, bf16[256,256]{1,0:T(8,128)(2,1)S(1)}, u32[]{:S(2)}, u32[]{:S(2)}) %collective-permute-start.33) | collective-permute-done | bytes 131104 | tf_op jit(solution)/shard_map/ppermute | solution.py:427
  132.6 3.6 %collective-permute-start.36 = (bf16[256,256]{1,0:T(8,128)(2,1)S(1)}, bf16[256,256]{1,0:T(8,128)(2,1)S(1)}, u32[]{:S(2)}, u32[]{:S(2)}) collective-permute-start(bf16[256,256]{1,0:T(8,128)(2,1)S(1)} %get-tuple-element.196), channel_id=1, source_target_pairs={{0,15},{1,14},{2,13},{3,12},{4,11},{5,10},{6,9},{7,8},{8,7},{9,6},... | collective-permute-start | bytes 393224 | tf_op jit(solution)/shard_map/ppermute | solution.py:427
  139.8 6.1 %collective-permute-done.36.refs_3_ = bf16[256,256]{1,0:T(8,128)(2,1)S(1)} collective-permute-done((bf16[256,256]{1,0:T(8,128)(2,1)S(1)}, bf16[256,256]{1,0:T(8,128)(2,1)S(1)}, u32[]{:S(2)}, u32[]{:S(2)}) %collective-permute-start.36) | collective-permute-done | bytes 131104 | tf_op jit(solution)/shard_map/ppermute | solution.py:427
  145.9 2.7 %collective-permute-done.35.refs_2_ = bf16[256,256]{1,0:T(8,128)(2,1)S(1)} collective-permute-done((bf16[256,256]{1,0:T(8,128)(2,1)S(1)}, bf16[256,256]{1,0:T(8,128)(2,1)S(1)}, u32[]{:S(2)}, u32[]{:S(2)}) %collective-permute-start.35) | collective-permute-done | bytes 131104 | tf_op jit(solution)/shard_map/ppermute | solution.py:427
  148.7 3.0 %shard_map.64 = bf16[768,256]{1,0:T(8,128)(2,1)} custom-call(s32[1]{0:T(128)} %bitcast.ids_ref, s32[16]{0:T(128)S(1)} %copy-done.2, bf16[768,4096]{1,0:T(8,128)(2,1)S(1)} %bitcast.12, f32[768,256]{1,0:T(8,128)S(1)} %shard_map.63.first_ref, bf16[4,3,128,128]{3,2,1,0:T(8,128)(2,1)S(1)} %pad_maximum_fusion.near_ref, ...), custom_call_target="tpu_custom_call" | custom-call | tf_op jit(solution)/shard_map/pallas_call | solution.py:410
  (78 shorter events, 28.5 us)
Async XLA Ops:
  5.1 12.6 %collective-permute-start.8 = (bf16[256,256]{1,0:T(8,128)(2,1)}, bf16[256,256]{1,0:T(8,128)(2,1)S(1)}, u32[]{:S(2)}, u32[]{:S(2)}) collective-permute-start(bf16[256,256]{1,0:T(8,128)(2,1)} %get-tuple-element.121), channel_id=1, source_target_pairs={{0,9},{1,8},{2,11},{3,10},{4,13},{5,12},{6,15},{7,14},{8,1},{9,0},... | collective-permute-start | bytes 393224 | tf_op jit(solution)/shard_map/ppermute | solution.py:427
  8.0 17.6 %collective-permute-start.2 = (bf16[256,256]{1,0:T(8,128)(2,1)}, bf16[256,256]{1,0:T(8,128)(2,1)S(1)}, u32[]{:S(2)}, u32[]{:S(2)}) collective-permute-start(bf16[256,256]{1,0:T(8,128)(2,1)} %get-tuple-element.110), channel_id=1, source_target_pairs={{0,8},{1,9},{2,10},{3,11},{4,12},{5,13},{6,14},{7,15},{8,0},{9,1},... | collective-permute-start | bytes 393224 | tf_op jit(solution)/shard_map/ppermute | solution.py:427
  13.6 12.0 %collective-permute-start = (bf16[256,256]{1,0:T(8,128)(2,1)S(1)}, bf16[256,256]{1,0:T(8,128)(2,1)S(1)}, u32[]{:S(2)}, u32[]{:S(2)}) collective-permute-start(bf16[256,256]{1,0:T(8,128)(2,1)S(1)} %get-tuple-element.103), channel_id=1, source_target_pairs={{0,1},{1,0},{2,3},{3,2},{4,5},{5,4},{6,7},{7,6},{8,9},{9,8},{10,11... | collective-permute-start | bytes 393224 | tf_op jit(solution)/shard_map/ppermute | solution.py:427
  14.1 14.2 %collective-permute-start.9 = (bf16[256,256]{1,0:T(8,128)(2,1)S(1)}, bf16[256,256]{1,0:T(8,128)(2,1)S(1)}, u32[]{:S(2)}, u32[]{:S(2)}) collective-permute-start(bf16[256,256]{1,0:T(8,128)(2,1)S(1)} %copy-done.8), channel_id=1, source_target_pairs={{0,10},{1,11},{2,8},{3,9},{4,14},{5,15},{6,12},{7,13},{8,2},{9,3},... | collective-permute-start | bytes 393224 | tf_op jit(solution)/shard_map/ppermute | solution.py:427
  17.1 16.7 %collective-permute-start.10 = (bf16[256,256]{1,0:T(8,128)(2,1)S(1)}, bf16[256,256]{1,0:T(8,128)(2,1)S(1)}, u32[]{:S(2)}, u32[]{:S(2)}) collective-permute-start(bf16[256,256]{1,0:T(8,128)(2,1)S(1)} %copy-done.7), channel_id=1, source_target_pairs={{0,11},{1,10},{2,9},{3,8},{4,15},{5,14},{6,13},{7,12},{8,3},{9,2},... | collective-permute-start | bytes 393224 | tf_op jit(solution)/shard_map/ppermute | solution.py:427
  17.7 16.1 %collective-permute-start.1 = (bf16[256,256]{1,0:T(8,128)(2,1)S(1)}, bf16[256,256]{1,0:T(8,128)(2,1)S(1)}, u32[]{:S(2)}, u32[]{:S(2)}) collective-permute-start(bf16[256,256]{1,0:T(8,128)(2,1)S(1)} %get-tuple-element.106), channel_id=1, source_target_pairs={{0,2},{1,3},{2,0},{3,1},{4,6},{5,7},{6,4},{7,5},{8,10},{9,11},{10,... | collective-permute-start | bytes 393224 | tf_op jit(solution)/shard_map/ppermute | solution.py:427
  25.6 11.2 %collective-permute-start.11 = (bf16[256,256]{1,0:T(8,128)(2,1)S(1)}, bf16[256,256]{1,0:T(8,128)(2,1)S(1)}, u32[]{:S(2)}, u32[]{:S(2)}) collective-permute-start(bf16[256,256]{1,0:T(8,128)(2,1)S(1)} %copy-done.6), channel_id=1, source_target_pairs={{0,12},{1,13},{2,14},{3,15},{4,8},{5,9},{6,10},{7,11},{8,4},{9,5},... | collective-permute-start | bytes 393224 | tf_op jit(solution)/shard_map/ppermute | solution.py:427
  25.6 14.4 %collective-permute-start.3 = (bf16[256,256]{1,0:T(8,128)(2,1)S(1)}, bf16[256,256]{1,0:T(8,128)(2,1)S(1)}, u32[]{:S(2)}, u32[]{:S(2)}) collective-permute-start(bf16[256,256]{1,0:T(8,128)(2,1)S(1)} %get-tuple-element.111), channel_id=1, source_target_pairs={{0,3},{1,2},{2,1},{3,0},{4,7},{5,6},{6,5},{7,4},{8,11},{9,10},{10,... | collective-permute-start | bytes 393224 | tf_op jit(solution)/shard_map/ppermute | solution.py:427
  28.3 15.0 %collective-permute-start.4 = (bf16[256,256]{1,0:T(8,128)(2,1)S(1)}, bf16[256,256]{1,0:T(8,128)(2,1)S(1)}, u32[]{:S(2)}, u32[]{:S(2)}) collective-permute-start(bf16[256,256]{1,0:T(8,128)(2,1)S(1)} %get-tuple-element.114), channel_id=1, source_target_pairs={{0,4},{1,5},{2,6},{3,7},{4,0},{5,1},{6,2},{7,3},{8,12},{9,13},{10,... | collective-permute-start | bytes 393224 | tf_op jit(solution)/shard_map/ppermute | solution.py:427
  33.8 10.2 %collective-permute-start.12 = (bf16[256,256]{1,0:T(8,128)(2,1)S(1)}, bf16[256,256]{1,0:T(8,128)(2,1)S(1)}, u32[]{:S(2)}, u32[]{:S(2)}) collective-permute-start(bf16[256,256]{1,0:T(8,128)(2,1)S(1)} %copy-done.5), channel_id=1, source_target_pairs={{0,13},{1,12},{2,15},{3,14},{4,9},{5,8},{6,11},{7,10},{8,5},{9,4},... | collective-permute-start | bytes 393224 | tf_op jit(solution)/shard_map/ppermute | solution.py:427
  33.8 14.9 %collective-permute-start.13 = (bf16[256,256]{1,0:T(8,128)(2,1)S(1)}, bf16[256,256]{1,0:T(8,128)(2,1)S(1)}, u32[]{:S(2)}, u32[]{:S(2)}) collective-permute-start(bf16[256,256]{1,0:T(8,128)(2,1)S(1)} %copy-done.4), channel_id=1, source_target_pairs={{0,14},{1,15},{2,12},{3,13},{4,10},{5,11},{6,8},{7,9},{8,6},{9,7},... | collective-permute-start | bytes 393224 | tf_op jit(solution)/shard_map/ppermute | solution.py:427
  36.8 12.8 %collective-permute-start.5 = (bf16[256,256]{1,0:T(8,128)(2,1)S(1)}, bf16[256,256]{1,0:T(8,128)(2,1)S(1)}, u32[]{:S(2)}, u32[]{:S(2)}) collective-permute-start(bf16[256,256]{1,0:T(8,128)(2,1)S(1)} %get-tuple-element.116), channel_id=1, source_target_pairs={{0,5},{1,4},{2,7},{3,6},{4,1},{5,0},{6,3},{7,2},{8,13},{9,12},{10,... | collective-permute-start | bytes 393224 | tf_op jit(solution)/shard_map/ppermute | solution.py:427
  40.0 16.3 %collective-permute-start.14 = (bf16[256,256]{1,0:T(8,128)(2,1)S(1)}, bf16[256,256]{1,0:T(8,128)(2,1)S(1)}, u32[]{:S(2)}, u32[]{:S(2)}) collective-permute-start(bf16[256,256]{1,0:T(8,128)(2,1)S(1)} %copy-done.3), channel_id=1, source_target_pairs={{0,15},{1,14},{2,13},{3,12},{4,11},{5,10},{6,9},{7,8},{8,7},{9,6},... | collective-permute-start | bytes 393224 | tf_op jit(solution)/shard_map/ppermute | solution.py:427
  43.2 13.4 %collective-permute-start.6 = (bf16[256,256]{1,0:T(8,128)(2,1)S(1)}, bf16[256,256]{1,0:T(8,128)(2,1)S(1)}, u32[]{:S(2)}, u32[]{:S(2)}) collective-permute-start(bf16[256,256]{1,0:T(8,128)(2,1)S(1)} %get-tuple-element.117), channel_id=1, source_target_pairs={{0,6},{1,7},{2,4},{3,5},{4,2},{5,3},{6,0},{7,1},{8,14},{9,15},{10,... | collective-permute-start | bytes 393224 | tf_op jit(solution)/shard_map/ppermute | solution.py:427
  44.0 15.7 %collective-permute-start.7 = (bf16[256,256]{1,0:T(8,128)(2,1)S(1)}, bf16[256,256]{1,0:T(8,128)(2,1)S(1)}, u32[]{:S(2)}, u32[]{:S(2)}) collective-permute-start(bf16[256,256]{1,0:T(8,128)(2,1)S(1)} %get-tuple-element.118), channel_id=1, source_target_pairs={{0,7},{1,6},{2,5},{3,4},{4,3},{5,2},{6,1},{7,0},{8,15},{9,14},{10,... | collective-permute-start | bytes 393224 | tf_op jit(solution)/shard_map/ppermute | solution.py:427
  64.6 10.4 %collective-permute-start.16 = (f32[2,3,128,128]{3,2,1,0:T(8,128)S(1)}, f32[2,3,128,128]{3,2,1,0:T(8,128)S(1)}, u32[]{:S(2)}, u32[]{:S(2)}) collective-permute-start(f32[2,3,128,128]{3,2,1,0:T(8,128)S(1)} %get-tuple-element.199), channel_id=1, source_target_pairs={{0,2},{1,3},{2,0},{3,1},{4,6},{5,7},{6,4},{7,5},{8,10},{9,11},{10,... | collective-permute-start | bytes 1179656 | tf_op jit(solution)/shard_map/ppermute | solution.py:427
  65.1 9.9 %collective-permute-start.17 = (bf16[256,256]{1,0:T(8,128)(2,1)S(1)}, bf16[256,256]{1,0:T(8,128)(2,1)S(1)}, u32[]{:S(2)}, u32[]{:S(2)}) collective-permute-start(bf16[256,256]{1,0:T(8,128)(2,1)S(1)} %get-tuple-element.138), channel_id=1, source_target_pairs={{0,8},{1,9},{2,10},{3,11},{4,12},{5,13},{6,14},{7,15},{8,0},{9,1},... | collective-permute-start | bytes 393224 | tf_op jit(solution)/shard_map/ppermute | solution.py:427
  66.0 9.0 %collective-permute-start.18 = (bf16[256,256]{1,0:T(8,128)(2,1)S(1)}, bf16[256,256]{1,0:T(8,128)(2,1)S(1)}, u32[]{:S(2)}, u32[]{:S(2)}) collective-permute-start(bf16[256,256]{1,0:T(8,128)(2,1)S(1)} %get-tuple-element.139), channel_id=1, source_target_pairs={{0,1},{1,0},{2,3},{3,2},{4,5},{5,4},{6,7},{7,6},{8,9},{9,8},{10,11... | collective-permute-start | bytes 393224 | tf_op jit(solution)/shard_map/ppermute | solution.py:427
  75.6 10.2 %collective-permute-start.20 = (bf16[256,256]{1,0:T(8,128)(2,1)S(1)}, bf16[256,256]{1,0:T(8,128)(2,1)S(1)}, u32[]{:S(2)}, u32[]{:S(2)}) collective-permute-start(bf16[256,256]{1,0:T(8,128)(2,1)S(1)} %get-tuple-element.146), channel_id=1, source_target_pairs={{0,9},{1,8},{2,11},{3,10},{4,13},{5,12},{6,15},{7,14},{8,1},{9,0},... | collective-permute-start | bytes 393224 | tf_op jit(solution)/shard_map/ppermute | solution.py:427
  85.8 9.7 %collective-permute-start.22 = (f32[1,3,128,128]{3,2,1,0:T(8,128)S(1)}, f32[1,3,128,128]{3,2,1,0:T(8,128)S(1)}, u32[]{:S(2)}, u32[]{:S(2)}) collective-permute-start(f32[1,3,128,128]{3,2,1,0:T(8,128)S(1)} %fusion), channel_id=1, source_target_pairs={{0,8},{1,9},{2,10},{3,11},{4,12},{5,13},{6,14},{7,15},{8,0},{9,1},... | collective-permute-start | bytes 589832 | tf_op jit(solution)/shard_map/ppermute | solution.py:427
  87.4 8.2 %collective-permute-start.24 = (bf16[256,256]{1,0:T(8,128)(2,1)S(1)}, bf16[256,256]{1,0:T(8,128)(2,1)S(1)}, u32[]{:S(2)}, u32[]{:S(2)}) collective-permute-start(bf16[256,256]{1,0:T(8,128)(2,1)S(1)} %get-tuple-element.155), channel_id=1, source_target_pairs={{0,4},{1,5},{2,6},{3,7},{4,0},{5,1},{6,2},{7,3},{8,12},{9,13},{10,... | collective-permute-start | bytes 393224 | tf_op jit(solution)/shard_map/ppermute | solution.py:427
  87.4 8.2 %collective-permute-start.23 = (bf16[256,256]{1,0:T(8,128)(2,1)S(1)}, bf16[256,256]{1,0:T(8,128)(2,1)S(1)}, u32[]{:S(2)}, u32[]{:S(2)}) collective-permute-start(bf16[256,256]{1,0:T(8,128)(2,1)S(1)} %get-tuple-element.154), channel_id=1, source_target_pairs={{0,3},{1,2},{2,1},{3,0},{4,7},{5,6},{6,5},{7,4},{8,11},{9,10},{10,... | collective-permute-start | bytes 393224 | tf_op jit(solution)/shard_map/ppermute | solution.py:427
  95.6 15.8 %collective-permute-start.28 = (bf16[256,256]{1,0:T(8,128)(2,1)S(1)}, bf16[256,256]{1,0:T(8,128)(2,1)S(1)}, u32[]{:S(2)}, u32[]{:S(2)}) collective-permute-start(bf16[256,256]{1,0:T(8,128)(2,1)S(1)} %get-tuple-element.172), channel_id=1, source_target_pairs={{0,6},{1,7},{2,4},{3,5},{4,2},{5,3},{6,0},{7,1},{8,14},{9,15},{10,... | collective-permute-start | bytes 393224 | tf_op jit(solution)/shard_map/ppermute | solution.py:427
  95.7 15.7 %collective-permute-start.27 = (bf16[256,256]{1,0:T(8,128)(2,1)S(1)}, bf16[256,256]{1,0:T(8,128)(2,1)S(1)}, u32[]{:S(2)}, u32[]{:S(2)}) collective-permute-start(bf16[256,256]{1,0:T(8,128)(2,1)S(1)} %get-tuple-element.171), channel_id=1, source_target_pairs={{0,5},{1,4},{2,7},{3,6},{4,1},{5,0},{6,3},{7,2},{8,13},{9,12},{10,... | collective-permute-start | bytes 393224 | tf_op jit(solution)/shard_map/ppermute | solution.py:427
  98.0 13.4 %collective-permute-start.26 = (bf16[256,256]{1,0:T(8,128)(2,1)S(1)}, bf16[256,256]{1,0:T(8,128)(2,1)S(1)}, u32[]{:S(2)}, u32[]{:S(2)}) collective-permute-start(bf16[256,256]{1,0:T(8,128)(2,1)S(1)} %get-tuple-element.170), channel_id=1, source_target_pairs={{0,11},{1,10},{2,9},{3,8},{4,15},{5,14},{6,13},{7,12},{8,3},{9,2},... | collective-permute-start | bytes 393224 | tf_op jit(solution)/shard_map/ppermute | solution.py:427
  101.4 11.1 %collective-permute-start.25 = (bf16[256,256]{1,0:T(8,128)(2,1)S(1)}, bf16[256,256]{1,0:T(8,128)(2,1)S(1)}, u32[]{:S(2)}, u32[]{:S(2)}) collective-permute-start(bf16[256,256]{1,0:T(8,128)(2,1)S(1)} %get-tuple-element.169), channel_id=1, source_target_pairs={{0,10},{1,11},{2,8},{3,9},{4,14},{5,15},{6,12},{7,13},{8,2},{9,3},... | collective-permute-start | bytes 393224 | tf_op jit(solution)/shard_map/ppermute | solution.py:427
  114.5 6.8 %collective-permute-start.31 = (bf16[256,256]{1,0:T(8,128)(2,1)S(1)}, bf16[256,256]{1,0:T(8,128)(2,1)S(1)}, u32[]{:S(2)}, u32[]{:S(2)}) collective-permute-start(bf16[256,256]{1,0:T(8,128)(2,1)S(1)} %get-tuple-element.181), channel_id=1, source_target_pairs={{0,7},{1,6},{2,5},{3,4},{4,3},{5,2},{6,1},{7,0},{8,15},{9,14},{10,... | collective-permute-start | bytes 393224 | tf_op jit(solution)/shard_map/ppermute | solution.py:427
  115.4 8.2 %collective-permute-start.30 = (bf16[256,256]{1,0:T(8,128)(2,1)S(1)}, bf16[256,256]{1,0:T(8,128)(2,1)S(1)}, u32[]{:S(2)}, u32[]{:S(2)}) collective-permute-start(bf16[256,256]{1,0:T(8,128)(2,1)S(1)} %get-tuple-element.180), channel_id=1, source_target_pairs={{0,12},{1,13},{2,14},{3,15},{4,8},{5,9},{6,10},{7,11},{8,4},{9,5},... | collective-permute-start | bytes 393224 | tf_op jit(solution)/shard_map/ppermute | solution.py:427
  123.5 9.1 %collective-permute-start.33 = (bf16[256,256]{1,0:T(8,128)(2,1)S(1)}, bf16[256,256]{1,0:T(8,128)(2,1)S(1)}, u32[]{:S(2)}, u32[]{:S(2)}) collective-permute-start(bf16[256,256]{1,0:T(8,128)(2,1)S(1)} %get-tuple-element.190), channel_id=1, source_target_pairs={{0,13},{1,12},{2,15},{3,14},{4,9},{5,8},{6,11},{7,10},{8,5},{9,4},... | collective-permute-start | bytes 393224 | tf_op jit(solution)/shard_map/ppermute | solution.py:427
  132.6 5.8 %collective-permute-start.34 = (bf16[4,3,128,128]{3,2,1,0:T(8,128)(2,1)S(1)}, bf16[4,3,128,128]{3,2,1,0:T(8,128)(2,1)S(1)}, u32[]{:S(2)}, u32[]{:S(2)}) collective-permute-start(bf16[4,3,128,128]{3,2,1,0:T(8,128)(2,1)S(1)} %pad_maximum_fusion.near_ref), channel_id=1, source_target_pairs={{0,1},{1,0},{2,3},{3,2},{4,5},{5,4},{6,7},{7,6},{8,9},{9,8},{10,11... | collective-permute-start | bytes 1179656 | tf_op jit(solution)/shard_map/ppermute | solution.py:427
  132.6 13.3 %collective-permute-start.36 = (bf16[256,256]{1,0:T(8,128)(2,1)S(1)}, bf16[256,256]{1,0:T(8,128)(2,1)S(1)}, u32[]{:S(2)}, u32[]{:S(2)}) collective-permute-start(bf16[256,256]{1,0:T(8,128)(2,1)S(1)} %get-tuple-element.196), channel_id=1, source_target_pairs={{0,15},{1,14},{2,13},{3,12},{4,11},{5,10},{6,9},{7,8},{8,7},{9,6},... | collective-permute-start | bytes 393224 | tf_op jit(solution)/shard_map/ppermute | solution.py:427
  136.2 12.4 %collective-permute-start.35 = (bf16[256,256]{1,0:T(8,128)(2,1)S(1)}, bf16[256,256]{1,0:T(8,128)(2,1)S(1)}, u32[]{:S(2)}, u32[]{:S(2)}) collective-permute-start(bf16[256,256]{1,0:T(8,128)(2,1)S(1)} %get-tuple-element.195), channel_id=1, source_target_pairs={{0,14},{1,15},{2,12},{3,13},{4,10},{5,11},{6,8},{7,9},{8,6},{9,7},... | collective-permute-start | bytes 393224 | tf_op jit(solution)/shard_map/ppermute | solution.py:427
  (16 other events, 381.0 us)

commit v3 on v2

--- a/solution.py
+++ b/solution.py
@@ -13,8 +13,7 @@
 MIB = 1024 * 1024
 PANEL = 8
 BLOCK = 64
-AHEAD = 6
-PLAN = {"sum": (1, 1), "last": (0, 2), "invert": (2, 2), "share": (1, 1)}
+BUSY = {"invert": 40, "basis": 0, "product": 0, "late": 1}
 VMEM = pl.BlockSpec(memory_space=pltpu.VMEM)
 SMEM = pl.BlockSpec(memory_space=pltpu.SMEM)
 HBM = pl.BlockSpec(memory_space=pltpu.MemorySpace.HBM)
@@ -22,6 +21,10 @@
 
 def dot(a, b, dims):
     return lax.dot_general(a, b, (dims, ((), ())), preferred_element_type=F32)
+
+
+def busy(microseconds):
+    return pl.CostEstimate(flops=0, bytes_accessed=int(3.5e6 * microseconds), transcendentals=0)
 
 
 def params(mib=24):
@@ -59,12 +62,12 @@
     for b in range(count):
         product[b] = wide[:, b * rows : (b + 1) * rows]
     for t in range(count):
-        outs[part * count + t][...] = product[me % count ^ t]
+        outs[(part * count + t) // 2][t % 2] = product[me % count ^ t]
 
 
 def far_partial_kernel(half, ids_ref, cov_hbm, sketch_hbm, weights_hbm, *refs):
-    outs, weighted_ref = refs[:half], refs[half]
-    cov, sketch, weights, product, in_sems, sems = refs[half + 1 :]
+    *outs, weighted_ref = refs[: half // 2 + 1]
+    cov, sketch, weights, product, in_sems, sems = refs[half // 2 + 1 :]
     me = ids_ref[0]
     cov_copy = pltpu.make_async_copy(cov_hbm, cov, in_sems.at[0])
     sketch_copy = pltpu.make_async_copy(sketch_hbm, sketch, in_sems.at[1])
@@ -82,8 +85,7 @@
 
 
 def near_partial_kernel(half, ids_ref, weighted_ref, weights_hbm, *refs):
-    outs = refs[:half]
-    weights, product, sems = refs[half:]
+    *outs, weights, product, sems = refs
     me = ids_ref[0]
     copies = weight_copies(me, weights_hbm, weights, sems, product.shape[2], half, False)
     for copy in copies:
@@ -97,7 +99,7 @@
     rank = sketch.shape[1]
     rows = width // devices
     half = devices // 2
-    block = jax.ShapeDtypeStruct((rank, rows), BF16)
+    pair = jax.ShapeDtypeStruct((2, rank, rows), BF16)
     scratch = [
         pltpu.VMEM((2, hidden, width // 4), BF16),
         pltpu.VMEM((half // 2, rank, rows), BF16),
@@ -106,8 +108,8 @@
     *far, weighted = pl.pallas_call(
         functools.partial(far_partial_kernel, half),
         in_specs=[SMEM, HBM, HBM, HBM],
-        out_specs=[VMEM] * (half + 1),
-        out_shape=[block] * half + [jax.ShapeDtypeStruct((rank, hidden), BF16)],
+        out_specs=[VMEM] * (half // 2 + 1),
+        out_shape=[pair] * (half // 2) + [jax.ShapeDtypeStruct((rank, hidden), BF16)],
         scratch_shapes=[pltpu.VMEM(cov.shape, BF16), pltpu.VMEM(sketch.shape, BF16)]
         + scratch
         + [sems, sems],
@@ -116,28 +118,30 @@
     near = pl.pallas_call(
         functools.partial(near_partial_kernel, half),
         in_specs=[SMEM, VMEM, HBM],
-        out_specs=[VMEM] * half,
-        out_shape=[block] * half,
+        out_specs=[VMEM] * (half // 2),
+        out_shape=[pair] * (half // 2),
         scratch_shapes=scratch + [sems],
         compiler_params=params(),
     )(ids, weighted, weights)
     return [*near, *far]
 
 
-def cluster_kernel(devices, ids_ref, member_ref, *refs):
-    received, refs = refs[:devices], refs[devices:]
+def cluster_kernel(pairs, ids_ref, member_ref, *refs):
+    received, passed, refs = refs[:pairs], refs[pairs : 2 * pairs], refs[2 * pairs :]
     rows_ref, keep_ref, send_ref = refs[:3]
-    blocks, total = refs[3 : 3 + devices], refs[-1]
+    outs, total = refs[3 : 3 + pairs], refs[-1]
     me = ids_ref[0]
-    base = base_cluster(me, devices)
+    base = base_cluster(me, 2 * pairs)
     half = rows_ref.shape[1] // 2
     total[...] = jnp.zeros_like(total)
-    for s in range(devices):
-        c = member_ref[me ^ s]
-        total[c] = total[c] + received[s][...].astype(F32)
+    for q in range(pairs):
+        for i, ref in enumerate((received[q], passed[q])):
+            c = member_ref[me ^ (2 * q + i)]
+            total[c] = total[c] + ref[i].astype(F32)
     rows_ref[...] = total[...].astype(BF16)
-    for s in range(devices):
-        blocks[s][...] = rows_ref[member_ref[me ^ s]]
+    for q in range(pairs):
+        for i in range(2):
+            outs[q][i] = rows_ref[member_ref[me ^ (2 * q + i)]]
     kept = keep_ref.shape[0]
 
     @pl.loop(0, kept)
@@ -150,22 +154,20 @@
             out_ref[k, 2] = full[half:, half:]
 
 
-def cluster_sums(ids, members, received):
-    devices = len(received)
-    clusters = devices // 2
-    rank, rows = received[0].shape
-    gram = jax.ShapeDtypeStruct((clusters // 2, 3, rank // 2, rank // 2), F32)
-    block = jax.ShapeDtypeStruct((rank, rows), BF16)
-    rows_t, keep, send, *blocks = pl.pallas_call(
-        functools.partial(cluster_kernel, devices),
-        in_specs=[SMEM, SMEM] + [VMEM] * devices,
-        out_specs=[VMEM] * (devices + 3),
-        out_shape=[jax.ShapeDtypeStruct((clusters, rank, rows), BF16), gram, gram]
-        + [block] * devices,
-        scratch_shapes=[pltpu.VMEM((clusters, rank, rows), F32)],
-        compiler_params=params(),
-    )(ids, members, *received)
-    return rows_t, keep, send, blocks
+def cluster_sums(ids, members, received, passed):
+    pairs = len(received)
+    _, rank, rows = received[0].shape
+    gram = jax.ShapeDtypeStruct((pairs // 2, 3, rank // 2, rank // 2), F32)
+    pair = jax.ShapeDtypeStruct((2, rank, rows), BF16)
+    rows_t, keep, send, *outs = pl.pallas_call(
+        functools.partial(cluster_kernel, pairs),
+        in_specs=[SMEM, SMEM] + [VMEM] * (2 * pairs),
+        out_specs=[VMEM] * (pairs + 3),
+        out_shape=[jax.ShapeDtypeStruct((pairs, rank, rows), BF16), gram, gram] + [pair] * pairs,
+        scratch_shapes=[pltpu.VMEM((pairs, rank, rows), F32)],
+        compiler_params=params(),
+    )(ids, members, *received, *passed)
+    return rows_t, keep, send, outs
 
 
 def stacked(x, axis, order):
@@ -296,6 +298,7 @@
         ],
         scratch_shapes=[pltpu.VMEM((2 * half, 4 * half), F32)],
         compiler_params=params(),
+        cost_estimate=busy(BUSY["invert"]),
     )(gram, rows_t)
 
 
@@ -328,6 +331,7 @@
         out_shape=jax.ShapeDtypeStruct(rows.shape, BF16),
         scratch_shapes=[pltpu.VMEM(rows.shape, BF16), pltpu.SemaphoreType.DMA((rows.shape[0],))],
         compiler_params=params(),
+        cost_estimate=busy(BUSY["basis"]),
     )(ids, rows, near, far)
 
 
@@ -342,47 +346,51 @@
     return block
 
 
-def first_product_kernel(ids_ref, weights_hbm, *refs):
-    *blocks, out_ref, weights, sem = refs
+def slots_of(pairs):
+    return [2 * q + i for q in pairs for i in range(2)]
+
+
+def add_products(total, columns, refs, places):
+    for column, (ref, block) in zip(columns, places):
+        term = dot(column, refs[ref][block], ((1,), (1,)))
+        total = term if total is None else total + term
+    return total
+
+
+def first_product_kernel(early, late, places, ids_ref, weights_hbm, *refs):
+    *refs, out_ref, late_ref, weights, sem = refs
     me = ids_ref[0]
-    rows = blocks[0].shape[1]
+    rows = refs[0].shape[2]
     copy = pltpu.make_async_copy(weights_hbm, weights, sem)
     copy.start()
     copy.wait()
-    total = None
-    for s, block in enumerate(blocks):
-        term = dot(column_block(weights, me ^ s, rows), block[...], ((1,), (1,)))
-        total = term if total is None else total + term
-    out_ref[...] = total
-
-
-def coef_kernel(ids_ref, member_ref, weights_hbm, first_ref, near_ref, far_ref, *refs):
-    *blocks, out_hbm, weights, out, sem, out_sem = refs
+    columns = [column_block(weights, me ^ s, rows) for s in slots_of(early)]
+    out_ref[...] = add_products(None, columns, refs, places)
+    for k, s in enumerate(slots_of(late)):
+        late_ref[:, k * rows : (k + 1) * rows] = column_block(weights, me ^ s, rows)
+
+
+def late_product_kernel(places, weights_ref, first_ref, *refs):
+    *refs, high_ref, low_ref = refs
+    rows = refs[0].shape[2]
+    columns = [weights_ref[:, k * rows : (k + 1) * rows] for k in range(len(places))]
+    total = add_products(first_ref[...], columns, refs, places)
+    high = total.astype(BF16)
+    high_ref[...] = high
+    low_ref[...] = (total - high.astype(F32)).astype(BF16)
+
+
+def coef_kernel(ids_ref, member_ref, high_ref, low_ref, near_ref, far_ref, out_hbm, out, out_sem):
     me = ids_ref[0]
     slot = member_ref[me] ^ base_cluster(me, member_ref.shape[0])
-    rows = blocks[0].shape[1]
-    count = len(blocks)
-    columns = count * rows
-    start = (me // count ^ 3) * columns
-    copy = pltpu.make_async_copy(
-        weights_hbm.at[:, pl.ds(pl.multiple_of(start, columns), columns)], weights, sem
-    )
-    copy.start()
-    copy.wait()
-    total = first_ref[...]
-    for t, block in enumerate(blocks):
-        total = total + dot(
-            column_block(weights, me % count ^ t, rows), block[...], ((1,), (1,))
-        )
-    high = total.astype(BF16)
-    low = (total - high.astype(F32)).astype(BF16)
     near = slot < near_ref.shape[0]
     inside = lax.rem(slot, near_ref.shape[0])
     half = out.shape[1] // 2
 
     def times(i, part):
         factor = jnp.where(near, near_ref[inside, i], far_ref[inside, i])
-        return dot(high[:, part], factor, ((1,), (1,))) + dot(low[:, part], factor, ((1,), (1,)))
+        high, low = high_ref[:, part], low_ref[:, part]
+        return dot(high, factor, ((1,), (1,))) + dot(low, factor, ((1,), (1,)))
 
     left, right = slice(0, half), slice(half, 2 * half)
     out[:, left] = times(0, left).astype(BF16)
@@ -392,34 +400,44 @@
     out_copy.wait()
 
 
-def first_product(ids, weights, blocks):
-    rank = blocks[0].shape[0]
+def first_product(ids, weights, early, late, arrays, places):
+    hidden, width = weights.shape
+    _, rank, rows = arrays[0].shape
     return pl.pallas_call(
-        first_product_kernel,
-        in_specs=[SMEM, HBM] + [VMEM] * len(blocks),
-        out_specs=VMEM,
-        out_shape=jax.ShapeDtypeStruct((weights.shape[0], rank), F32),
+        functools.partial(first_product_kernel, early, late, places),
+        in_specs=[SMEM, HBM] + [VMEM] * len(arrays),
+        out_specs=[VMEM] * 2,
+        out_shape=[
+            jax.ShapeDtypeStruct((hidden, rank), F32),
+            jax.ShapeDtypeStruct((hidden, 2 * len(late) * rows), BF16),
+        ],
         scratch_shapes=[pltpu.VMEM(weights.shape, BF16), pltpu.SemaphoreType.DMA],
         compiler_params=params(),
-    )(ids, weights, *blocks)
-
-
-def coefficients(ids, members, weights, first, near, far, blocks):
-    hidden = weights.shape[0]
-    rank, rows = blocks[0].shape
+        cost_estimate=busy(BUSY["product"]),
+    )(ids, weights, *arrays)
+
+
+def late_product(late_weights, first, arrays, places):
+    return pl.pallas_call(
+        functools.partial(late_product_kernel, places),
+        in_specs=[VMEM] * (len(arrays) + 2),
+        out_specs=[VMEM] * 2,
+        out_shape=[jax.ShapeDtypeStruct(first.shape, BF16)] * 2,
+        compiler_params=params(),
+        cost_estimate=busy(BUSY["late"]),
+    )(late_weights, first, *arrays)
+
+
+def coefficients(ids, members, product, near, far):
+    out = product[0].shape
     return pl.pallas_call(
         coef_kernel,
-        in_specs=[SMEM, SMEM, HBM] + [VMEM] * (len(blocks) + 3),
+        in_specs=[SMEM, SMEM] + [VMEM] * 4,
         out_specs=HBM,
-        out_shape=jax.ShapeDtypeStruct((hidden, rank), BF16),
-        scratch_shapes=[
-            pltpu.VMEM((hidden, len(blocks) * rows), BF16),
-            pltpu.VMEM((hidden, rank), BF16),
-            pltpu.SemaphoreType.DMA,
-            pltpu.SemaphoreType.DMA,
-        ],
-        compiler_params=params(),
-    )(ids, members, weights, first, near, far, *blocks)
+        out_shape=jax.ShapeDtypeStruct(out, BF16),
+        scratch_shapes=[pltpu.VMEM(out, BF16), pltpu.SemaphoreType.DMA],
+        compiler_params=params(),
+    )(ids, members, *product, near, far)
 
 
 def swap(block, distance):
@@ -443,66 +461,94 @@
     weights = down_proj[0]
     width = weights.shape[1]
     last = devices.bit_length() - 2
-    half, quarter = devices // 2, devices // 4
+    half = devices // 2
     me = lax.axis_index("expert")
     ids = me.astype(jnp.int32).reshape(1)
 
+    pairs = devices // 2
+    middle = pairs // 2
     blocks = partial_blocks(ids, cov_factor[0], sketch[0], weights, devices)
-    order = [half]
-    for s in range(1, half):
-        order += [half + s, s]
     got = {0: blocks[0]}
-    for k, s in enumerate(order):
-        block = blocks[s]
-        if k >= AHEAD:
-            block = tied(block, got, order[k - AHEAD : k - AHEAD + 1])
-        got[s] = swap(block, s)
-
-    rows_t, keep, send, blocks = cluster_sums(ids, membership, [got[s] for s in range(devices)])
-
-    crossing, inner = list(range(half, devices)), list(range(1, half))
+    far = list(range(middle, pairs))
+    near = list(range(1, middle))
+    share = -(-len(near) // max(1, len(far) - 2))
+    for q in far[:2] + near:
+        got[q] = swap(blocks[q], 2 * q)
+    for k, q in enumerate(far[2:]):
+        block = tied(blocks[q], got, [far[k]] + near[k * share : (k + 1) * share])
+        got[q] = swap(block, 2 * q)
+    every = range(pairs)
+    rows_t, keep, send, blocks = cluster_sums(
+        ids, membership, [got[q] for q in every], [swap(got[q], 1) for q in every]
+    )
+
+    even = [q for q in range(pairs - 1, middle - 1, -1) if q % 2 == 0]
+    last_pairs = [q for q in range(middle, pairs) if q % 2]
+    inner = list(range(1, middle))
+    inner_parts = [q for q in inner if q % 2 == 0], [q for q in inner if q % 4 == 1], [q for q in inner if q % 4 == 3]
     values = {0: blocks[0]}
-    unit = max(1, devices // 16)
-
-    def start(across, within, gate):
-        keys = []
-        for queue, count in ((crossing, across), (inner, within)):
-            for _ in range(min(count * unit, len(queue))):
-                s = queue.pop(0)
-                block = blocks[s]
-                if gate is not None:
-                    block, gate = lax.optimization_barrier((block, gate))
-                values[s] = swap(block, s)
-                keys.append(s)
-        return keys, gate
-
+    passed = {}
+
+    def start(keys, gate):
+        for q in keys:
+            block, gate = lax.optimization_barrier((blocks[q], gate))
+            values[q] = swap(block, 2 * q)
+        return gate
+
+    def pass_on(keys):
+        pair = values[keys[0]] if len(keys) == 1 else jnp.concatenate([values[q] for q in keys])
+        passed[tuple(keys)] = swap(pair, 1)
+
+    def blocks_for(keys):
+        groups = [g for g in passed if set(g) <= set(keys)]
+        arrays = [values[q] for q in keys] + [passed[g] for g in groups]
+        places = []
+        for k, q in enumerate(keys):
+            (n, g), = ((n, g) for n, g in enumerate(groups) if q in g)
+            places += [(k, 0), (len(keys) + n, 2 * g.index(q) + 1)]
+        return arrays, places
+
+    cut = len(even) // 2
+    send = start(even[:cut] + inner_parts[0], send)
+    send = start(even[cut:], send)
     other = swap(send, 1)
-    waiting, _ = start(1, 1, None)
     for bit in range(1, last):
         keep, send = halves(keep, other)
-        if bit > 1:
-            send = tied(send, values, waiting)
-            waiting, send = start(*PLAN["sum"], send)
+        if bit == 2:
+            send = tied(send, values, even[:cut] + inner_parts[0])
+            send = start(inner_parts[1] + inner_parts[2], send)
         other = swap(send, 1 << bit)
-    gram = tied(keep + other, values, waiting)
-    waiting, gram = start(*PLAN["last"], gram)
+    gram = tied(keep + other, values, even[cut:] + inner_parts[1])
     gram = gram + swap(gram, half)
-    gram = tied(gram, values, waiting)
-    waiting, gram = start(*PLAN["invert"], gram)
+    gram = tied(gram, values, inner_parts[2])
+
+    cut = len(last_pairs) // 2
+    gram = start(last_pairs[:cut], gram)
+    early = [q for q in every if q not in last_pairs]
+    for q in early:
+        if (q,) not in passed:
+            values[q], gram = lax.optimization_barrier((values[q], gram))
+            pass_on([q])
     inverse, rows = inverse_factor(gram[0], rows_t, math.sqrt(width))
-    near = tied(inverse[None], values, waiting)
+    near = tied(inverse[None], passed, list(passed))
+    first, late_weights = first_product(ids, weights, early, last_pairs, *blocks_for(early))
+    near = start(last_pairs[cut:], near)
+    pieces = [near]
     for bit in reversed(range(1, last)):
-        waiting, near = start(*PLAN["share"], near)
-        near = jnp.concatenate([near, swap(near, 1 << bit)], axis=0)
-        near = tied(near, values, waiting)
+        if len(pieces) > 2:
+            pieces = [jnp.concatenate(pieces, axis=0)]
+        pieces += [swap(piece, 1 << bit) for piece in pieces]
+        if bit == last - 1:
+            pieces[1] = tied(pieces[1], values, last_pairs[:cut])
+    near = jnp.concatenate(pieces, axis=0)
+    near, first = lax.optimization_barrier((near, first))
+    near = tied(near, values, last_pairs[cut:])
+    for q in last_pairs:
+        pass_on([q])
     far = swap(near, 1)
-    start(devices, devices, near)
-
-    first = first_product(ids, weights, [values[s] for s in range(half + quarter)])
+    product = late_product(late_weights, first, *blocks_for(last_pairs))
     basis = basis_rows(ids, rows, near, far)
-    coef = coefficients(
-        ids, membership, weights, first, near, far, [values[s] for s in range(half + quarter, devices)]
-    )
+    coef = coefficients(ids, membership, product, near, far)
     return (coef[None], basis)
 
 

time: 152 us -> 140 us (0.921); the launches traced: 152 us -> 137 us
  starting transfers between devices: 59.9 us -> 40.4 us
  waiting for transfers between devices: 62.3 us -> 67.6 us
    ppermute x37 -> x38, starting transfers between devices: 59.9 us -> 40.4 us  [swap(): lax.ppermute(block, 'expert', [(i, i ^ distance) for i in range(count)])]
    ppermute x37 -> x38, waiting for transfers between devices: 62.3 us -> 67.6 us  [swap(): lax.ppermute(block, 'expert', [(i, i ^ distance) for i in range(count)])]
    pallas_call x3 -> x4, Pallas kernels: 7.43 us -> 6.97 us  [the longest x1 2.33 us: cluster_sums(): pl.pallas_call(functools.partial(cluster_kernel, pairs), in_specs=[SMEM,...]
    unnamed x22 -> x16, local copies, waits for them, and re-layouts: 3.82 us -> 3.81 us
  transfers between devices with their start and end apart: 37 -> 38, of which waited for: 21 -> 18; matrix products, arithmetic and copies ran while one was open for 0% -> 0% of each run, Pallas kernels for 10% -> 10%
where the time goes in v3:
time: 140 us; the launch traced here: 137 us
  waiting for transfers between devices  67.6 us (48%)
  starting transfers between devices  40.4 us (29%)
  Pallas kernels  24.1 us (17%)
  local copies, waits for them, and re-layouts  3.81 us (3%)
    ppermute x38, waiting for transfers between devices, swap(): lax.ppermute(block, 'expert', [(i, i ^ distance) for i in range(count)])  67.6 us
    ppermute x38, starting transfers between devices, swap(): lax.ppermute(block, 'expert', [(i, i ^ distance) for i in range(count)])  40.4 us
    pallas_call x1, Pallas kernels, inverse_factor(): pl.pallas_call(functools.partial(inverse_kernel, scale), in_specs=[VMEM]...  9.56 us
    pallas_call x1, Pallas kernels, partial_blocks(): pl.pallas_call(functools.partial(far_partial_kernel, half), in_specs=[SME...  4.45 us
    unnamed x16, local copies, waits for them, and re-layouts  3.81 us
  transfers between devices with their start and end apart: 38, of which 18 were waited for; matrix products, arithmetic and copies ran while one was open for 0% of the time, Pallas kernels for 10%

profile of v3, /device:TPU:9, one launch (start us, length us, event | category | flops | bytes accessed | tf_op | source)
XLA Modules:
  0.0 137.1 jit_solution(17758557068400081842)
XLA Ops:
  0.6 4.4 %shard_map.59 = (bf16[2,256,256]{2,1,0:T(8,128)(2,1)}, bf16[2,256,256]{2,1,0:T(8,128)(2,1)}, bf16[2,256,256]{2,1,0:T(8,128)(2,1)}, bf16[2,256,256]{2,1,0:T(8,128)(2,1)}, bf16[256,768]{1,0:T(8,128)(2,1)}) custom-call(s32[1]{0:T(128)} %bitcast.ids_ref, bf16[768,768]{1,0:T(8,128)(2,1)} %bitcast.16, bf16[768,256]{1,0:T(8,128)(2,1)} %bitcast.17, ...), custom_call_target="tpu_custom_call" | custom-call | tf_op jit(solution)/shard_map/pallas_call | solution.py:108
  5.1 2.4 %collective-permute-start = (bf16[2,256,256]{2,1,0:T(8,128)(2,1)}, bf16[2,256,256]{2,1,0:T(8,128)(2,1)S(1)}, u32[]{:S(2)}, u32[]{:S(2)}) collective-permute-start(bf16[2,256,256]{2,1,0:T(8,128)(2,1)} %get-tuple-element.85), channel_id=1, source_target_pairs={{0,8},{1,9},{2,10},{3,11},{4,12},{5,13},{6,14},{7,15},{8,0},{9,1},... | collective-permute-start | bytes 786440 | tf_op jit(solution)/shard_map/ppermute | solution.py:445
  7.5 2.8 %copy-done = bf16[1,768,4096]{2,1,0:T(8,128)(2,1)S(1)} copy-done((bf16[1,768,4096]{2,1,0:T(8,128)(2,1)S(1)}, bf16[1,768,4096]{2,1,0:T(8,128)(2,1)}, u32[]{:S(2)}) %copy-start) | copy-done | bytes 6291480
  11.3 1.7 %shard_map.60 = (bf16[2,256,256]{2,1,0:T(8,128)(2,1)S(1)}, bf16[2,256,256]{2,1,0:T(8,128)(2,1)S(1)}, bf16[2,256,256]{2,1,0:T(8,128)(2,1)S(1)}, bf16[2,256,256]{2,1,0:T(8,128)(2,1)S(1)}) custom-call(s32[1]{0:T(128)} %bitcast.ids_ref, bf16[256,768]{1,0:T(8,128)(2,1)S(1)} %copy-done.1, bf16[768,4096]{1,0:T(8,128)(2,1)S(1)} %bitcast.8), custom_call_target="tpu_custom_call" | custom-call | tf_op jit(solution)/shard_map/pallas_call | solution.py:118
  14.5 2.2 %collective-permute-start.4 = (bf16[2,256,256]{2,1,0:T(8,128)(2,1)S(1)}, bf16[2,256,256]{2,1,0:T(8,128)(2,1)S(1)}, u32[]{:S(2)}, u32[]{:S(2)}) collective-permute-start(bf16[2,256,256]{2,1,0:T(8,128)(2,1)S(1)} %get-tuple-element.92), channel_id=1, source_target_pairs={{0,6},{1,7},{2,4},{3,5},{4,2},{5,3},{6,0},{7,1},{8,14},{9,15},{10,... | collective-permute-start | bytes 786440 | tf_op jit(solution)/shard_map/ppermute | solution.py:445
  16.7 2.6 %collective-permute-done.refs_4_ = bf16[2,256,256]{2,1,0:T(8,128)(2,1)S(1)} collective-permute-done((bf16[2,256,256]{2,1,0:T(8,128)(2,1)}, bf16[2,256,256]{2,1,0:T(8,128)(2,1)S(1)}, u32[]{:S(2)}, u32[]{:S(2)}) %collective-permute-start) | collective-permute-done | bytes 262176 | tf_op jit(solution)/shard_map/ppermute | solution.py:445
  20.0 7.0 %collective-permute-done.2.refs_2_ = bf16[2,256,256]{2,1,0:T(8,128)(2,1)S(1)} collective-permute-done((bf16[2,256,256]{2,1,0:T(8,128)(2,1)S(1)}, bf16[2,256,256]{2,1,0:T(8,128)(2,1)S(1)}, u32[]{:S(2)}, u32[]{:S(2)}) %collective-permute-start.2) | collective-permute-done | bytes 262176 | tf_op jit(solution)/shard_map/ppermute | solution.py:445
  27.0 2.6 %collective-permute-start.5 = (bf16[2,256,256]{2,1,0:T(8,128)(2,1)S(1)}, bf16[2,256,256]{2,1,0:T(8,128)(2,1)S(1)}, u32[]{:S(2)}, u32[]{:S(2)}) collective-permute-start(bf16[2,256,256]{2,1,0:T(8,128)(2,1)S(1)} %copy-done.4), channel_id=1, source_target_pairs={{0,12},{1,13},{2,14},{3,15},{4,8},{5,9},{6,10},{7,11},{8,4},{9,5},... | collective-permute-start | bytes 786440 | tf_op jit(solution)/shard_map/ppermute | solution.py:445
  31.1 9.4 %collective-permute-done.4.refs_3_ = bf16[2,256,256]{2,1,0:T(8,128)(2,1)S(1)} collective-permute-done((bf16[2,256,256]{2,1,0:T(8,128)(2,1)S(1)}, bf16[2,256,256]{2,1,0:T(8,128)(2,1)S(1)}, u32[]{:S(2)}, u32[]{:S(2)}) %collective-permute-start.4) | collective-permute-done | bytes 262176 | tf_op jit(solution)/shard_map/ppermute | solution.py:445
  40.5 1.4 %collective-permute-start.6 = (bf16[2,256,256]{2,1,0:T(8,128)(2,1)S(1)}, bf16[2,256,256]{2,1,0:T(8,128)(2,1)S(1)}, u32[]{:S(2)}, u32[]{:S(2)}) collective-permute-start(bf16[2,256,256]{2,1,0:T(8,128)(2,1)S(1)} %copy-done.3), channel_id=1, source_target_pairs={{0,14},{1,15},{2,12},{3,13},{4,10},{5,11},{6,8},{7,9},{8,6},{9,7},... | collective-permute-start | bytes 786440 | tf_op jit(solution)/shard_map/ppermute | solution.py:445
  42.0 1.8 %collective-permute-start.11 = (bf16[2,256,256]{2,1,0:T(8,128)(2,1)S(1)}, bf16[2,256,256]{2,1,0:T(8,128)(2,1)S(1)}, u32[]{:S(2)}, u32[]{:S(2)}) collective-permute-start(bf16[2,256,256]{2,1,0:T(8,128)(2,1)S(1)} %collective-permute-done.refs_4_), channel_id=1, source_target_pairs={{0,1},{1,0},{2,3},{3,2},{4,5},{5,4},{6,7},{7,6},{8,9},{9,8},{10,11... | collective-permute-start | bytes 786440 | tf_op jit(solution)/shard_map/ppermute | solution.py:445
  44.4 10.0 %collective-permute-done.6.refs_7_ = bf16[2,256,256]{2,1,0:T(8,128)(2,1)S(1)} collective-permute-done((bf16[2,256,256]{2,1,0:T(8,128)(2,1)S(1)}, bf16[2,256,256]{2,1,0:T(8,128)(2,1)S(1)}, u32[]{:S(2)}, u32[]{:S(2)}) %collective-permute-start.6) | collective-permute-done | bytes 262176 | tf_op jit(solution)/shard_map/ppermute | solution.py:445
  54.4 1.3 collective-permute-start.14
  56.9 2.3 %shard_map.61 = (bf16[8,256,256]{2,1,0:T(8,128)(2,1)S(1)}, f32[4,3,128,128]{3,2,1,0:T(8,128)S(1)}, f32[4,3,128,128]{3,2,1,0:T(8,128)S(1)}, bf16[2,256,256]{2,1,0...) custom-call(s32[1]{0:T(128)} %bitcast.ids_ref, ...), custom_call_target="tpu_custom_call" | custom-call | tf_op jit(solution)/shard_map/pallas_call | solution.py:162
  59.7 1.9 %collective-permute-done.15 = f32[4,3,128,128]{3,2,1,0:T(8,128)S(1)} collective-permute-done((f32[4,3,128,128]{3,2,1,0:T(8,128)S(1)}, f32[4,3,128,128]{3,2,1,0:T(8,128)S(1)}, u32[]{:S(2)}, u32[]{:S(2)}) %collective-permute-start.15) | collective-permute-done | bytes 786464 | tf_op jit(solution)/shard_map/ppermute | solution.py:445
  61.7 1.4 collective-permute-start.16
  64.3 7.8 %collective-permute-done.16 = f32[2,3,128,128]{3,2,1,0:T(8,128)S(1)} collective-permute-done((f32[2,3,128,128]{3,2,1,0:T(8,128)S(1)}, f32[2,3,128,128]{3,2,1,0:T(8,128)S(1)}, u32[]{:S(2)}, u32[]{:S(2)}) %collective-permute-start.16) | collective-permute-done | bytes 393248 | tf_op jit(solution)/shard_map/ppermute | solution.py:445
  72.1 6.1 %collective-permute-start.19 = (f32[1,3,128,128]{3,2,1,0:T(8,128)S(1)}, f32[1,3,128,128]{3,2,1,0:T(8,128)S(1)}, u32[]{:S(2)}, u32[]{:S(2)}) collective-permute-start(f32[1,3,128,128]{3,2,1,0:T(8,128)S(1)} %slice_add_fusion.2), channel_id=1, source_target_pairs={{0,4},{1,5},{2,6},{3,7},{4,0},{5,1},{6,2},{7,3},{8,12},{9,13},{10,... | collective-permute-start | bytes 589832 | tf_op jit(solution)/shard_map/ppermute | solution.py:445
  80.6 3.8 %collective-permute-done.19 = f32[1,3,128,128]{3,2,1,0:T(8,128)S(1)} collective-permute-done((f32[1,3,128,128]{3,2,1,0:T(8,128)S(1)}, f32[1,3,128,128]{3,2,1,0:T(8,128)S(1)}, u32[]{:S(2)}, u32[]{:S(2)}) %collective-permute-start.19) | collective-permute-done | bytes 196640 | tf_op jit(solution)/shard_map/ppermute | solution.py:445
  84.5 3.0 %collective-permute-done.20.refs_4_ = bf16[2,256,256]{2,1,0:T(8,128)(2,1)S(1)} collective-permute-done((bf16[2,256,256]{2,1,0:T(8,128)(2,1)S(1)}, bf16[2,256,256]{2,1,0:T(8,128)(2,1)S(1)}, u32[]{:S(2)}, u32[]{:S(2)}) %collective-permute-start.20) | collective-permute-done | bytes 262176 | tf_op jit(solution)/shard_map/ppermute | solution.py:445
  87.6 9.7 %collective-permute-done.22 = f32[1,3,128,128]{3,2,1,0:T(8,128)S(1)} collective-permute-done((f32[1,3,128,128]{3,2,1,0:T(8,128)S(1)}, f32[1,3,128,128]{3,2,1,0:T(8,128)S(1)}, u32[]{:S(2)}, u32[]{:S(2)}) %collective-permute-start.22) | collective-permute-done | bytes 196640 | tf_op jit(solution)/shard_map/ppermute | solution.py:445
  97.4 3.4 %collective-permute-start.29 = (bf16[2,256,256]{2,1,0:T(8,128)(2,1)S(1)}, bf16[2,256,256]{2,1,0:T(8,128)(2,1)S(1)}, u32[]{:S(2)}, u32[]{:S(2)}) collective-permute-start(bf16[2,256,256]{2,1,0:T(8,128)(2,1)S(1)} %collective-permute-done.17.refs_5_), channel_id=1, source_target_pairs={{0,1},{1,0},{2,3},{3,2},{4,5},{5,4},{6,7},{7,6},{8,9},{9,8},{10,11... | collective-permute-start | bytes 786440 | tf_op jit(solution)/shard_map/ppermute | solution.py:445
  102.3 3.8 %collective-permute-start.31 = (bf16[2,256,256]{2,1,0:T(8,128)(2,1)S(1)}, bf16[2,256,256]{2,1,0:T(8,128)(2,1)S(1)}, u32[]{:S(2)}, u32[]{:S(2)}) collective-permute-start(bf16[2,256,256]{2,1,0:T(8,128)(2,1)S(1)} %get-tuple-element.150), channel_id=1, source_target_pairs={{0,10},{1,11},{2,8},{3,9},{4,14},{5,15},{6,12},{7,13},{8,2},{9,3},... | collective-permute-start | bytes 786440 | tf_op jit(solution)/shard_map/ppermute | solution.py:445
  106.1 9.6 %shard_map.62 = (bf16[3,128,128]{2,1,0:T(8,128)(2,1)S(1)}, bf16[8,256,256]{2,1,0:T(8,128)(2,1)S(1)}) custom-call(f32[3,128,128]{2,1,0:T(8,128)S(1)} %bitcast.12, bf16[8,256,256]{2,1,0:T(8,128)(2,1)S(1)} %get-tuple-element.138.rows_t_ref), custom_call_target="tpu_custom_call" | custom-call | bytes 140000000 | tf_op jit(solution)/shard_map/pallas_call | solution.py:291
  117.3 1.9 %collective-permute-done.30 = bf16[1,3,128,128]{3,2,1,0:T(8,128)(2,1)S(1)} collective-permute-done((bf16[1,3,128,128]{3,2,1,0:T(8,128)(2,1)S(1)}, bf16[1,3,128,128]{3,2,1,0:T(8,128)(2,1)S(1)}, u32[]{:S(2)}, u32[]{:S(2)}) %collective-permute-start.30) | collective-permute-done | bytes 98336 | tf_op jit(solution)/shard_map/ppermute | solution.py:445
  119.8 2.2 %shard_map.63 = (f32[768,256]{1,0:T(8,128)S(1)}, bf16[768,1024]{1,0:T(8,128)(2,1)S(1)}) custom-call(s32[1]{0:T(128)} %bitcast.ids_ref, bf16[768,4096]{1,0:T(8,128)(2,1)S(1)} %bitcast.11, bf16[2,256,256]{2,1,0:T(8,128)(2,1)S(1)} %get-tuple-element.121.refs_0_, bf16[2,256,256]{2,1,0:T(8,128)(2,1)S(1)} %collective-permute-done.21.refs_1_, ...), custom_call_target="tpu_custom_call" | custom-call | tf_op jit(solution)/shard_map/pallas_call | solution.py:406
  122.1 1.4 %collective-permute-done.32 = bf16[1,3,128,128]{3,2,1,0:T(8,128)(2,1)S(1)} collective-permute-done((bf16[1,3,128,128]{3,2,1,0:T(8,128)(2,1)S(1)}, bf16[1,3,128,128]{3,2,1,0:T(8,128)(2,1)S(1)}, u32[]{:S(2)}, u32[]{:S(2)}) %collective-permute-start.32) | collective-permute-done | bytes 98336 | tf_op jit(solution)/shard_map/ppermute | solution.py:445
  123.5 1.5 %collective-permute-done.33 = bf16[1,3,128,128]{3,2,1,0:T(8,128)(2,1)S(1)} collective-permute-done((bf16[1,3,128,128]{3,2,1,0:T(8,128)(2,1)S(1)}, bf16[1,3,128,128]{3,2,1,0:T(8,128)(2,1)S(1)}, u32[]{:S(2)}, u32[]{:S(2)}) %collective-permute-start.33) | collective-permute-done | bytes 98336 | tf_op jit(solution)/shard_map/ppermute | solution.py:445
  125.1 4.5 %collective-permute-done.34.refs_1_ = bf16[2,256,256]{2,1,0:T(8,128)(2,1)S(1)} collective-permute-done((bf16[2,256,256]{2,1,0:T(8,128)(2,1)S(1)}, bf16[2,256,256]{2,1,0:T(8,128)(2,1)S(1)}, u32[]{:S(2)}, u32[]{:S(2)}) %collective-permute-start.34) | collective-permute-done | bytes 262176 | tf_op jit(solution)/shard_map/ppermute | solution.py:445
  129.6 1.5 %collective-permute-start.37 = (bf16[4,3,128,128]{3,2,1,0:T(8,128)(2,1)S(1)}, bf16[4,3,128,128]{3,2,1,0:T(8,128)(2,1)S(1)}, u32[]{:S(2)}, u32[]{:S(2)}) collective-permute-start(bf16[4,3,128,128]{3,2,1,0:T(8,128)(2,1)S(1)} %pad_maximum_fusion.near_ref), channel_id=1, source_target_pairs={{0,1},{1,0},{2,3},{3,2},{4,5},{5,4},{6,7},{7,6},{8,9},{9,8},{10,11... | collective-permute-start | bytes 1179656 | tf_op jit(solution)/shard_map/ppermute | solution.py:445
  133.8 1.4 shard_map.66
  135.2 1.8 %shard_map.65 = bf16[768,256]{1,0:T(8,128)(2,1)} custom-call(s32[1]{0:T(128)} %bitcast.ids_ref, s32[16]{0:T(128)S(1)} %copy-done.2, bf16[768,256]{1,0:T(8,128)(2,1)S(1)} %get-tuple-element.158.high_ref, bf16[768,256]{1,0:T(8,128)(2,1)S(1)} %get-tuple-element.159.low_ref, bf16[4,3,128,128]{3,2,1,0:T(8,128)(2,1)S(1)} %pad_maximum_fusion.near_ref, ...), custom_call_target="tpu_custom_call" | custom-call | tf_op jit(solution)/shard_map/pallas_call | solution.py:433
  (74 shorter events, 17.3 us)
Async XLA Ops:
  5.1 14.3 %collective-permute-start = (bf16[2,256,256]{2,1,0:T(8,128)(2,1)}, bf16[2,256,256]{2,1,0:T(8,128)(2,1)S(1)}, u32[]{:S(2)}, u32[]{:S(2)}) collective-permute-start(bf16[2,256,256]{2,1,0:T(8,128)(2,1)} %get-tuple-element.85), channel_id=1, source_target_pairs={{0,8},{1,9},{2,10},{3,11},{4,12},{5,13},{6,14},{7,15},{8,0},{9,1},... | collective-permute-start | bytes 786440 | tf_op jit(solution)/shard_map/ppermute | solution.py:445
  13.0 7.0 %collective-permute-start.1 = (bf16[2,256,256]{2,1,0:T(8,128)(2,1)S(1)}, bf16[2,256,256]{2,1,0:T(8,128)(2,1)S(1)}, u32[]{:S(2)}, u32[]{:S(2)}) collective-permute-start(bf16[2,256,256]{2,1,0:T(8,128)(2,1)S(1)} %get-tuple-element.86), channel_id=1, source_target_pairs={{0,2},{1,3},{2,0},{3,1},{4,6},{5,7},{6,4},{7,5},{8,10},{9,11},{10,... | collective-permute-start | bytes 786440 | tf_op jit(solution)/shard_map/ppermute | solution.py:445
  14.3 12.7 %collective-permute-start.2 = (bf16[2,256,256]{2,1,0:T(8,128)(2,1)S(1)}, bf16[2,256,256]{2,1,0:T(8,128)(2,1)S(1)}, u32[]{:S(2)}, u32[]{:S(2)}) collective-permute-start(bf16[2,256,256]{2,1,0:T(8,128)(2,1)S(1)} %get-tuple-element.87), channel_id=1, source_target_pairs={{0,4},{1,5},{2,6},{3,7},{4,0},{5,1},{6,2},{7,3},{8,12},{9,13},{10,... | collective-permute-start | bytes 786440 | tf_op jit(solution)/shard_map/ppermute | solution.py:445
  14.5 16.3 %collective-permute-start.3 = (bf16[2,256,256]{2,1,0:T(8,128)(2,1)S(1)}, bf16[2,256,256]{2,1,0:T(8,128)(2,1)S(1)}, u32[]{:S(2)}, u32[]{:S(2)}) collective-permute-start(bf16[2,256,256]{2,1,0:T(8,128)(2,1)S(1)} %copy-done.5), channel_id=1, source_target_pairs={{0,10},{1,11},{2,8},{3,9},{4,14},{5,15},{6,12},{7,13},{8,2},{9,3},... | collective-permute-start | bytes 786440 | tf_op jit(solution)/shard_map/ppermute | solution.py:445
  14.5 26.0 %collective-permute-start.4 = (bf16[2,256,256]{2,1,0:T(8,128)(2,1)S(1)}, bf16[2,256,256]{2,1,0:T(8,128)(2,1)S(1)}, u32[]{:S(2)}, u32[]{:S(2)}) collective-permute-start(bf16[2,256,256]{2,1,0:T(8,128)(2,1)S(1)} %get-tuple-element.92), channel_id=1, source_target_pairs={{0,6},{1,7},{2,4},{3,5},{4,2},{5,3},{6,0},{7,1},{8,14},{9,15},{10,... | collective-permute-start | bytes 786440 | tf_op jit(solution)/shard_map/ppermute | solution.py:445
  19.4 22.6 %collective-permute-start.7 = (bf16[2,256,256]{2,1,0:T(8,128)(2,1)S(1)}, bf16[2,256,256]{2,1,0:T(8,128)(2,1)S(1)}, u32[]{:S(2)}, u32[]{:S(2)}) collective-permute-start(bf16[2,256,256]{2,1,0:T(8,128)(2,1)S(1)} %get-tuple-element.83.refs_0_), channel_id=1, source_target_pairs={{0,1},{1,0},{2,3},{3,2},{4,5},{5,4},{6,7},{7,6},{8,9},{9,8},{10,11... | collective-permute-start | bytes 786440 | tf_op jit(solution)/shard_map/ppermute | solution.py:445
  27.0 16.7 %collective-permute-start.5 = (bf16[2,256,256]{2,1,0:T(8,128)(2,1)S(1)}, bf16[2,256,256]{2,1,0:T(8,128)(2,1)S(1)}, u32[]{:S(2)}, u32[]{:S(2)}) collective-permute-start(bf16[2,256,256]{2,1,0:T(8,128)(2,1)S(1)} %copy-done.4), channel_id=1, source_target_pairs={{0,12},{1,13},{2,14},{3,15},{4,8},{5,9},{6,10},{7,11},{8,4},{9,5},... | collective-permute-start | bytes 786440 | tf_op jit(solution)/shard_map/ppermute | solution.py:445
  29.6 14.2 %collective-permute-start.8 = (bf16[2,256,256]{2,1,0:T(8,128)(2,1)S(1)}, bf16[2,256,256]{2,1,0:T(8,128)(2,1)S(1)}, u32[]{:S(2)}, u32[]{:S(2)}) collective-permute-start(bf16[2,256,256]{2,1,0:T(8,128)(2,1)S(1)} %collective-permute-done.1.refs_1_), channel_id=1, source_target_pairs={{0,1},{1,0},{2,3},{3,2},{4,5},{5,4},{6,7},{7,6},{8,9},{9,8},{10,11... | collective-permute-start | bytes 786440 | tf_op jit(solution)/shard_map/ppermute | solution.py:445
  30.8 13.5 %collective-permute-start.9 = (bf16[2,256,256]{2,1,0:T(8,128)(2,1)S(1)}, bf16[2,256,256]{2,1,0:T(8,128)(2,1)S(1)}, u32[]{:S(2)}, u32[]{:S(2)}) collective-permute-start(bf16[2,256,256]{2,1,0:T(8,128)(2,1)S(1)} %collective-permute-done.2.refs_2_), channel_id=1, source_target_pairs={{0,1},{1,0},{2,3},{3,2},{4,5},{5,4},{6,7},{7,6},{8,9},{9,8},{10,11... | collective-permute-start | bytes 786440 | tf_op jit(solution)/shard_map/ppermute | solution.py:445
  40.5 13.9 %collective-permute-start.6 = (bf16[2,256,256]{2,1,0:T(8,128)(2,1)S(1)}, bf16[2,256,256]{2,1,0:T(8,128)(2,1)S(1)}, u32[]{:S(2)}, u32[]{:S(2)}) collective-permute-start(bf16[2,256,256]{2,1,0:T(8,128)(2,1)S(1)} %copy-done.3), channel_id=1, source_target_pairs={{0,14},{1,15},{2,12},{3,13},{4,10},{5,11},{6,8},{7,9},{8,6},{9,7},... | collective-permute-start | bytes 786440 | tf_op jit(solution)/shard_map/ppermute | solution.py:445
  42.0 13.8 %collective-permute-start.11 = (bf16[2,256,256]{2,1,0:T(8,128)(2,1)S(1)}, bf16[2,256,256]{2,1,0:T(8,128)(2,1)S(1)}, u32[]{:S(2)}, u32[]{:S(2)}) collective-permute-start(bf16[2,256,256]{2,1,0:T(8,128)(2,1)S(1)} %collective-permute-done.refs_4_), channel_id=1, source_target_pairs={{0,1},{1,0},{2,3},{3,2},{4,5},{5,4},{6,7},{7,6},{8,9},{9,8},{10,11... | collective-permute-start | bytes 786440 | tf_op jit(solution)/shard_map/ppermute | solution.py:445
  43.8 12.0 %collective-permute-start.10 = (bf16[2,256,256]{2,1,0:T(8,128)(2,1)S(1)}, bf16[2,256,256]{2,1,0:T(8,128)(2,1)S(1)}, u32[]{:S(2)}, u32[]{:S(2)}) collective-permute-start(bf16[2,256,256]{2,1,0:T(8,128)(2,1)S(1)} %collective-permute-done.4.refs_3_), channel_id=1, source_target_pairs={{0,1},{1,0},{2,3},{3,2},{4,5},{5,4},{6,7},{7,6},{8,9},{9,8},{10,11... | collective-permute-start | bytes 786440 | tf_op jit(solution)/shard_map/ppermute | solution.py:445
  43.8 11.9 %collective-permute-start.12 = (bf16[2,256,256]{2,1,0:T(8,128)(2,1)S(1)}, bf16[2,256,256]{2,1,0:T(8,128)(2,1)S(1)}, u32[]{:S(2)}, u32[]{:S(2)}) collective-permute-start(bf16[2,256,256]{2,1,0:T(8,128)(2,1)S(1)} %collective-permute-done.3.refs_5_), channel_id=1, source_target_pairs={{0,1},{1,0},{2,3},{3,2},{4,5},{5,4},{6,7},{7,6},{8,9},{9,8},{10,11... | collective-permute-start | bytes 786440 | tf_op jit(solution)/shard_map/ppermute | solution.py:445
  44.3 11.5 %collective-permute-start.13 = (bf16[2,256,256]{2,1,0:T(8,128)(2,1)S(1)}, bf16[2,256,256]{2,1,0:T(8,128)(2,1)S(1)}, u32[]{:S(2)}, u32[]{:S(2)}) collective-permute-start(bf16[2,256,256]{2,1,0:T(8,128)(2,1)S(1)} %collective-permute-done.5.refs_6_), channel_id=1, source_target_pairs={{0,1},{1,0},{2,3},{3,2},{4,5},{5,4},{6,7},{7,6},{8,9},{9,8},{10,11... | collective-permute-start | bytes 786440 | tf_op jit(solution)/shard_map/ppermute | solution.py:445
  61.7 10.4 %collective-permute-start.16 = (f32[2,3,128,128]{3,2,1,0:T(8,128)S(1)}, f32[2,3,128,128]{3,2,1,0:T(8,128)S(1)}, u32[]{:S(2)}, u32[]{:S(2)}) collective-permute-start(f32[2,3,128,128]{3,2,1,0:T(8,128)S(1)} %get-tuple-element.163), channel_id=1, source_target_pairs={{0,2},{1,3},{2,0},{3,1},{4,6},{5,7},{6,4},{7,5},{8,10},{9,11},{10,... | collective-permute-start | bytes 1179656 | tf_op jit(solution)/shard_map/ppermute | solution.py:445
  63.0 9.1 %collective-permute-start.18 = (bf16[2,256,256]{2,1,0:T(8,128)(2,1)S(1)}, bf16[2,256,256]{2,1,0:T(8,128)(2,1)S(1)}, u32[]{:S(2)}, u32[]{:S(2)}) collective-permute-start(bf16[2,256,256]{2,1,0:T(8,128)(2,1)S(1)} %get-tuple-element.111), channel_id=1, source_target_pairs={{0,4},{1,5},{2,6},{3,7},{4,0},{5,1},{6,2},{7,3},{8,12},{9,13},{10,... | collective-permute-start | bytes 786440 | tf_op jit(solution)/shard_map/ppermute | solution.py:445
  63.0 9.1 %collective-permute-start.17 = (bf16[2,256,256]{2,1,0:T(8,128)(2,1)S(1)}, bf16[2,256,256]{2,1,0:T(8,128)(2,1)S(1)}, u32[]{:S(2)}, u32[]{:S(2)}) collective-permute-start(bf16[2,256,256]{2,1,0:T(8,128)(2,1)S(1)} %get-tuple-element.110), channel_id=1, source_target_pairs={{0,12},{1,13},{2,14},{3,15},{4,8},{5,9},{6,10},{7,11},{8,4},{9,5},... | collective-permute-start | bytes 786440 | tf_op jit(solution)/shard_map/ppermute | solution.py:445
  72.1 12.3 %collective-permute-start.19 = (f32[1,3,128,128]{3,2,1,0:T(8,128)S(1)}, f32[1,3,128,128]{3,2,1,0:T(8,128)S(1)}, u32[]{:S(2)}, u32[]{:S(2)}) collective-permute-start(f32[1,3,128,128]{3,2,1,0:T(8,128)S(1)} %slice_add_fusion.2), channel_id=1, source_target_pairs={{0,4},{1,5},{2,6},{3,7},{4,0},{5,1},{6,2},{7,3},{8,12},{9,13},{10,... | collective-permute-start | bytes 589832 | tf_op jit(solution)/shard_map/ppermute | solution.py:445
  78.2 9.2 %collective-permute-start.20 = (bf16[2,256,256]{2,1,0:T(8,128)(2,1)S(1)}, bf16[2,256,256]{2,1,0:T(8,128)(2,1)S(1)}, u32[]{:S(2)}, u32[]{:S(2)}) collective-permute-start(bf16[2,256,256]{2,1,0:T(8,128)(2,1)S(1)} %get-tuple-element.115), channel_id=1, source_target_pairs={{0,8},{1,9},{2,10},{3,11},{4,12},{5,13},{6,14},{7,15},{8,0},{9,1},... | collective-permute-start | bytes 786440 | tf_op jit(solution)/shard_map/ppermute | solution.py:445
  78.2 9.2 %collective-permute-start.21 = (bf16[2,256,256]{2,1,0:T(8,128)(2,1)S(1)}, bf16[2,256,256]{2,1,0:T(8,128)(2,1)S(1)}, u32[]{:S(2)}, u32[]{:S(2)}) collective-permute-start(bf16[2,256,256]{2,1,0:T(8,128)(2,1)S(1)} %get-tuple-element.116), channel_id=1, source_target_pairs={{0,2},{1,3},{2,0},{3,1},{4,6},{5,7},{6,4},{7,5},{8,10},{9,11},{10,... | collective-permute-start | bytes 786440 | tf_op jit(solution)/shard_map/ppermute | solution.py:445
  79.3 18.1 %collective-permute-start.23 = (bf16[2,256,256]{2,1,0:T(8,128)(2,1)S(1)}, bf16[2,256,256]{2,1,0:T(8,128)(2,1)S(1)}, u32[]{:S(2)}, u32[]{:S(2)}) collective-permute-start(bf16[2,256,256]{2,1,0:T(8,128)(2,1)S(1)} %get-tuple-element.118), channel_id=1, source_target_pairs={{0,6},{1,7},{2,4},{3,5},{4,2},{5,3},{6,0},{7,1},{8,14},{9,15},{10,... | collective-permute-start | bytes 786440 | tf_op jit(solution)/shard_map/ppermute | solution.py:445
  87.4 9.9 %collective-permute-start.22 = (f32[1,3,128,128]{3,2,1,0:T(8,128)S(1)}, f32[1,3,128,128]{3,2,1,0:T(8,128)S(1)}, u32[]{:S(2)}, u32[]{:S(2)}) collective-permute-start(f32[1,3,128,128]{3,2,1,0:T(8,128)S(1)} %fusion), channel_id=1, source_target_pairs={{0,8},{1,9},{2,10},{3,11},{4,12},{5,13},{6,14},{7,15},{8,0},{9,1},... | collective-permute-start | bytes 589832 | tf_op jit(solution)/shard_map/ppermute | solution.py:445
  97.4 4.6 %collective-permute-start.29 = (bf16[2,256,256]{2,1,0:T(8,128)(2,1)S(1)}, bf16[2,256,256]{2,1,0:T(8,128)(2,1)S(1)}, u32[]{:S(2)}, u32[]{:S(2)}) collective-permute-start(bf16[2,256,256]{2,1,0:T(8,128)(2,1)S(1)} %collective-permute-done.17.refs_5_), channel_id=1, source_target_pairs={{0,1},{1,0},{2,3},{3,2},{4,5},{5,4},{6,7},{7,6},{8,9},{9,8},{10,11... | collective-permute-start | bytes 786440 | tf_op jit(solution)/shard_map/ppermute | solution.py:445
  100.9 14.8 %collective-permute-start.27 = (bf16[2,256,256]{2,1,0:T(8,128)(2,1)S(1)}, bf16[2,256,256]{2,1,0:T(8,128)(2,1)S(1)}, u32[]{:S(2)}, u32[]{:S(2)}) collective-permute-start(bf16[2,256,256]{2,1,0:T(8,128)(2,1)S(1)} %collective-permute-done.23.refs_3_), channel_id=1, source_target_pairs={{0,1},{1,0},{2,3},{3,2},{4,5},{5,4},{6,7},{7,6},{8,9},{9,8},{10,11... | collective-permute-start | bytes 786440 | tf_op jit(solution)/shard_map/ppermute | solution.py:445
  101.3 14.4 %collective-permute-start.26 = (bf16[2,256,256]{2,1,0:T(8,128)(2,1)S(1)}, bf16[2,256,256]{2,1,0:T(8,128)(2,1)S(1)}, u32[]{:S(2)}, u32[]{:S(2)}) collective-permute-start(bf16[2,256,256]{2,1,0:T(8,128)(2,1)S(1)} %collective-permute-done.18.refs_2_), channel_id=1, source_target_pairs={{0,1},{1,0},{2,3},{3,2},{4,5},{5,4},{6,7},{7,6},{8,9},{9,8},{10,11... | collective-permute-start | bytes 786440 | tf_op jit(solution)/shard_map/ppermute | solution.py:445
  101.4 14.3 %collective-permute-start.25 = (bf16[2,256,256]{2,1,0:T(8,128)(2,1)S(1)}, bf16[2,256,256]{2,1,0:T(8,128)(2,1)S(1)}, u32[]{:S(2)}, u32[]{:S(2)}) collective-permute-start(bf16[2,256,256]{2,1,0:T(8,128)(2,1)S(1)} %collective-permute-done.21.refs_1_), channel_id=1, source_target_pairs={{0,1},{1,0},{2,3},{3,2},{4,5},{5,4},{6,7},{7,6},{8,9},{9,8},{10,11... | collective-permute-start | bytes 786440 | tf_op jit(solution)/shard_map/ppermute | solution.py:445
  101.9 13.7 %collective-permute-start.24 = (bf16[2,256,256]{2,1,0:T(8,128)(2,1)S(1)}, bf16[2,256,256]{2,1,0:T(8,128)(2,1)S(1)}, u32[]{:S(2)}, u32[]{:S(2)}) collective-permute-start(bf16[2,256,256]{2,1,0:T(8,128)(2,1)S(1)} %get-tuple-element.121.refs_0_), channel_id=1, source_target_pairs={{0,1},{1,0},{2,3},{3,2},{4,5},{5,4},{6,7},{7,6},{8,9},{9,8},{10,11... | collective-permute-start | bytes 786440 | tf_op jit(solution)/shard_map/ppermute | solution.py:445
  102.3 15.0 %collective-permute-start.31 = (bf16[2,256,256]{2,1,0:T(8,128)(2,1)S(1)}, bf16[2,256,256]{2,1,0:T(8,128)(2,1)S(1)}, u32[]{:S(2)}, u32[]{:S(2)}) collective-permute-start(bf16[2,256,256]{2,1,0:T(8,128)(2,1)S(1)} %get-tuple-element.150), channel_id=1, source_target_pairs={{0,10},{1,11},{2,8},{3,9},{4,14},{5,15},{6,12},{7,13},{8,2},{9,3},... | collective-permute-start | bytes 786440 | tf_op jit(solution)/shard_map/ppermute | solution.py:445
  115.8 13.8 %collective-permute-start.34 = (bf16[2,256,256]{2,1,0:T(8,128)(2,1)S(1)}, bf16[2,256,256]{2,1,0:T(8,128)(2,1)S(1)}, u32[]{:S(2)}, u32[]{:S(2)}) collective-permute-start(bf16[2,256,256]{2,1,0:T(8,128)(2,1)S(1)} %get-tuple-element.156), channel_id=1, source_target_pairs={{0,14},{1,15},{2,12},{3,13},{4,10},{5,11},{6,8},{7,9},{8,6},{9,7},... | collective-permute-start | bytes 786440 | tf_op jit(solution)/shard_map/ppermute | solution.py:445
  117.0 6.5 %collective-permute-start.32 = (bf16[1,3,128,128]{3,2,1,0:T(8,128)(2,1)S(1)}, bf16[1,3,128,128]{3,2,1,0:T(8,128)(2,1)S(1)}, u32[]{:S(2)}, u32[]{:S(2)}) collective-permute-start(bf16[1,3,128,128]{3,2,1,0:T(8,128)(2,1)S(1)} %bitcast.14), channel_id=1, source_target_pairs={{0,2},{1,3},{2,0},{3,1},{4,6},{5,7},{6,4},{7,5},{8,10},{9,11},{10,... | collective-permute-start | bytes 294920 | tf_op jit(solution)/shard_map/ppermute | solution.py:445
  119.2 5.8 %collective-permute-start.33 = (bf16[1,3,128,128]{3,2,1,0:T(8,128)(2,1)S(1)}, bf16[1,3,128,128]{3,2,1,0:T(8,128)(2,1)S(1)}, u32[]{:S(2)}, u32[]{:S(2)}) collective-permute-start(bf16[1,3,128,128]{3,2,1,0:T(8,128)(2,1)S(1)} %collective-permute-done.30), channel_id=1, source_target_pairs={{0,2},{1,3},{2,0},{3,1},{4,6},{5,7},{6,4},{7,5},{8,10},{9,11},{10,... | collective-permute-start | bytes 294920 | tf_op jit(solution)/shard_map/ppermute | solution.py:445
  129.6 4.2 %collective-permute-start.37 = (bf16[4,3,128,128]{3,2,1,0:T(8,128)(2,1)S(1)}, bf16[4,3,128,128]{3,2,1,0:T(8,128)(2,1)S(1)}, u32[]{:S(2)}, u32[]{:S(2)}) collective-permute-start(bf16[4,3,128,128]{3,2,1,0:T(8,128)(2,1)S(1)} %pad_maximum_fusion.near_ref), channel_id=1, source_target_pairs={{0,1},{1,0},{2,3},{3,2},{4,5},{5,4},{6,7},{7,6},{8,9},{9,8},{10,11... | collective-permute-start | bytes 1179656 | tf_op jit(solution)/shard_map/ppermute | solution.py:445
  (14 other events, 299.4 us)

commit v4 on v3

--- a/solution.py
+++ b/solution.py
@@ -13,7 +13,7 @@
 MIB = 1024 * 1024
 PANEL = 8
 BLOCK = 64
-BUSY = {"invert": 40, "basis": 0, "product": 0, "late": 1}
+BUSY = {"invert": 40, "basis": 2, "product": 0, "late": 1}
 VMEM = pl.BlockSpec(memory_space=pltpu.VMEM)
 SMEM = pl.BlockSpec(memory_space=pltpu.SMEM)
 HBM = pl.BlockSpec(memory_space=pltpu.MemorySpace.HBM)
@@ -128,11 +128,8 @@
 
 def cluster_kernel(pairs, ids_ref, member_ref, *refs):
     received, passed, refs = refs[:pairs], refs[pairs : 2 * pairs], refs[2 * pairs :]
-    rows_ref, keep_ref, send_ref = refs[:3]
-    outs, total = refs[3 : 3 + pairs], refs[-1]
+    rows_ref, outs, total = refs[0], refs[1 : 1 + pairs], refs[-1]
     me = ids_ref[0]
-    base = base_cluster(me, 2 * pairs)
-    half = rows_ref.shape[1] // 2
     total[...] = jnp.zeros_like(total)
     for q in range(pairs):
         for i, ref in enumerate((received[q], passed[q])):
@@ -142,10 +139,13 @@
     for q in range(pairs):
         for i in range(2):
             outs[q][i] = rows_ref[member_ref[me ^ (2 * q + i)]]
+
+
+def gram_kernel(ids_ref, rows_ref, keep_ref, send_ref):
+    half = rows_ref.shape[1] // 2
     kept = keep_ref.shape[0]
-
-    @pl.loop(0, kept)
-    def _(k):
+    base = base_cluster(ids_ref[0], 4 * kept)
+    for k in range(kept):
         for out_ref, slot in ((send_ref, k + kept), (keep_ref, k)):
             block = rows_ref[base ^ slot]
             full = dot(block, block, ((1,), (1,)))
@@ -159,14 +159,21 @@
     _, rank, rows = received[0].shape
     gram = jax.ShapeDtypeStruct((pairs // 2, 3, rank // 2, rank // 2), F32)
     pair = jax.ShapeDtypeStruct((2, rank, rows), BF16)
-    rows_t, keep, send, *outs = pl.pallas_call(
+    rows_t, *outs = pl.pallas_call(
         functools.partial(cluster_kernel, pairs),
         in_specs=[SMEM, SMEM] + [VMEM] * (2 * pairs),
-        out_specs=[VMEM] * (pairs + 3),
-        out_shape=[jax.ShapeDtypeStruct((pairs, rank, rows), BF16), gram, gram] + [pair] * pairs,
+        out_specs=[VMEM] * (pairs + 1),
+        out_shape=[jax.ShapeDtypeStruct((pairs, rank, rows), BF16)] + [pair] * pairs,
         scratch_shapes=[pltpu.VMEM((pairs, rank, rows), F32)],
         compiler_params=params(),
     )(ids, members, *received, *passed)
+    keep, send = pl.pallas_call(
+        gram_kernel,
+        in_specs=[SMEM, VMEM],
+        out_specs=[VMEM] * 2,
+        out_shape=[gram, gram],
+        compiler_params=params(),
+    )(ids, rows_t)
     return rows_t, keep, send, outs
 
 
@@ -453,7 +460,8 @@
 
 def halves(keep, other):
     cut = keep.shape[0] // 2
-    return keep[:cut] + other[:cut], keep[cut:] + other[cut:]
+    first, second = other if isinstance(other, tuple) else (other[:cut], other[cut:])
+    return keep[:cut] + first, keep[cut:] + second
 
 
 def local(down_proj, cov_factor, sketch, membership):
@@ -508,27 +516,33 @@
             places += [(k, 0), (len(keys) + n, 2 * g.index(q) + 1)]
         return arrays, places
 
-    cut = len(even) // 2
-    send = start(even[:cut] + inner_parts[0], send)
-    send = start(even[cut:], send)
+    share = len(even) // 2
+    rows_t = start(inner_parts[0] + even, rows_t)
     other = swap(send, 1)
     for bit in range(1, last):
         keep, send = halves(keep, other)
         if bit == 2:
-            send = tied(send, values, even[:cut] + inner_parts[0])
+            for q in even[:share]:
+                pass_on([q])
+            send = tied(send, values, inner_parts[0])
+            send = tied(send, passed, [(q,) for q in even[:share]])
             send = start(inner_parts[1] + inner_parts[2], send)
-        other = swap(send, 1 << bit)
-    gram = tied(keep + other, values, even[cut:] + inner_parts[1])
+        if bit == 1 and last > 2:
+            cut = send.shape[0] // 2
+            other = swap(send[:cut], 1 << bit), swap(send[cut:], 1 << bit)
+        else:
+            other = swap(send, 1 << bit)
+    gram = tied(keep + other, values, even[share:] + inner_parts[1])
     gram = gram + swap(gram, half)
     gram = tied(gram, values, inner_parts[2])
 
     cut = len(last_pairs) // 2
-    gram = start(last_pairs[:cut], gram)
     early = [q for q in every if q not in last_pairs]
     for q in early:
         if (q,) not in passed:
             values[q], gram = lax.optimization_barrier((values[q], gram))
             pass_on([q])
+    gram = start(last_pairs[:cut], gram)
     inverse, rows = inverse_factor(gram[0], rows_t, math.sqrt(width))
     near = tied(inverse[None], passed, list(passed))
     first, late_weights = first_product(ids, weights, early, last_pairs, *blocks_for(early))
@@ -540,14 +554,15 @@
         pieces += [swap(piece, 1 << bit) for piece in pieces]
         if bit == last - 1:
             pieces[1] = tied(pieces[1], values, last_pairs[:cut])
+            pieces[1], first = lax.optimization_barrier((pieces[1], first))
+    far = jnp.concatenate([swap(piece, 1) for piece in pieces], axis=0)
     near = jnp.concatenate(pieces, axis=0)
-    near, first = lax.optimization_barrier((near, first))
-    near = tied(near, values, last_pairs[cut:])
     for q in last_pairs:
         pass_on([q])
-    far = swap(near, 1)
+    near, far = lax.optimization_barrier((near, far))
+    basis = basis_rows(ids, rows, near, far)
+    near = tied(near, passed, [(q,) for q in last_pairs[cut:]])
     product = late_product(late_weights, first, *blocks_for(last_pairs))
-    basis = basis_rows(ids, rows, near, far)
     coef = coefficients(ids, membership, product, near, far)
     return (coef[None], basis)
 

time: 140 us -> 137 us (0.979); the launches traced: 137 us -> 136 us
  starting transfers between devices: 40.4 us -> 38.2 us
  waiting for transfers between devices: 67.6 us -> 69.4 us
    ppermute x38 -> x42, starting transfers between devices: 40.4 us -> 38.2 us  [swap(): lax.ppermute(block, 'expert', [(i, i ^ distance) for i in range(count)])]
    ppermute x38 -> x42, waiting for transfers between devices: 67.6 us -> 69.4 us  [swap(): lax.ppermute(block, 'expert', [(i, i ^ distance) for i in range(count)])]
  transfers between devices with their start and end apart: 38 -> 42, of which waited for: 18 -> 17; matrix products, arithmetic and copies ran while one was open for 0% -> 0% of each run, Pallas kernels for 10% -> 11%
where the time goes in v4:
time: 137 us; the launch traced here: 136 us
  waiting for transfers between devices  69.4 us (51%)
  starting transfers between devices  38.2 us (28%)
  Pallas kernels  23.6 us (17%)
  local copies, waits for them, and re-layouts  3.83 us (3%)
    ppermute x42, waiting for transfers between devices, swap(): lax.ppermute(block, 'expert', [(i, i ^ distance) for i in range(count)])  69.4 us
    ppermute x42, starting transfers between devices, swap(): lax.ppermute(block, 'expert', [(i, i ^ distance) for i in range(count)])  38.2 us
    pallas_call x1, Pallas kernels, inverse_factor(): pl.pallas_call(functools.partial(inverse_kernel, scale), in_specs=[VMEM]...  9.55 us
    pallas_call x1, Pallas kernels, partial_blocks(): pl.pallas_call(functools.partial(far_partial_kernel, half), in_specs=[SME...  4.46 us
    unnamed x16, local copies, waits for them, and re-layouts  3.81 us
  transfers between devices with their start and end apart: 42, of which 17 were waited for; matrix products, arithmetic and copies ran while one was open for 0% of the time, Pallas kernels for 11%

profile of v4, /device:TPU:9, one launch (start us, length us, event | category | flops | bytes accessed | tf_op | source)
XLA Modules:
  0.0 136.3 jit_solution(1636258979265230455)
XLA Ops:
  0.6 4.5 %shard_map.59 = (bf16[2,256,256]{2,1,0:T(8,128)(2,1)}, bf16[2,256,256]{2,1,0:T(8,128)(2,1)}, bf16[2,256,256]{2,1,0:T(8,128)(2,1)}, bf16[2,256,256]{2,1,0:T(8,128)(2,1)}, bf16[256,768]{1,0:T(8,128)(2,1)}) custom-call(s32[1]{0:T(128)} %bitcast.ids_ref, bf16[768,768]{1,0:T(8,128)(2,1)} %bitcast.17, bf16[768,256]{1,0:T(8,128)(2,1)} %bitcast.18, ...), custom_call_target="tpu_custom_call" | custom-call | tf_op jit(solution)/shard_map/pallas_call | solution.py:108
  5.1 2.4 %collective-permute-start = (bf16[2,256,256]{2,1,0:T(8,128)(2,1)}, bf16[2,256,256]{2,1,0:T(8,128)(2,1)S(1)}, u32[]{:S(2)}, u32[]{:S(2)}) collective-permute-start(bf16[2,256,256]{2,1,0:T(8,128)(2,1)} %get-tuple-element.86), channel_id=1, source_target_pairs={{0,8},{1,9},{2,10},{3,11},{4,12},{5,13},{6,14},{7,15},{8,0},{9,1},... | collective-permute-start | bytes 786440 | tf_op jit(solution)/shard_map/ppermute | solution.py:452
  7.5 2.8 %copy-done = bf16[1,768,4096]{2,1,0:T(8,128)(2,1)S(1)} copy-done((bf16[1,768,4096]{2,1,0:T(8,128)(2,1)S(1)}, bf16[1,768,4096]{2,1,0:T(8,128)(2,1)}, u32[]{:S(2)}) %copy-start) | copy-done | bytes 6291480
  11.3 1.7 %shard_map.60 = (bf16[2,256,256]{2,1,0:T(8,128)(2,1)S(1)}, bf16[2,256,256]{2,1,0:T(8,128)(2,1)S(1)}, bf16[2,256,256]{2,1,0:T(8,128)(2,1)S(1)}, bf16[2,256,256]{2,1,0:T(8,128)(2,1)S(1)}) custom-call(s32[1]{0:T(128)} %bitcast.ids_ref, bf16[256,768]{1,0:T(8,128)(2,1)S(1)} %copy-done.1, bf16[768,4096]{1,0:T(8,128)(2,1)S(1)} %bitcast.8), custom_call_target="tpu_custom_call" | custom-call | tf_op jit(solution)/shard_map/pallas_call | solution.py:118
  13.0 1.3 collective-permute-start.1
  14.5 2.2 %collective-permute-start.4 = (bf16[2,256,256]{2,1,0:T(8,128)(2,1)S(1)}, bf16[2,256,256]{2,1,0:T(8,128)(2,1)S(1)}, u32[]{:S(2)}, u32[]{:S(2)}) collective-permute-start(bf16[2,256,256]{2,1,0:T(8,128)(2,1)S(1)} %get-tuple-element.93), channel_id=1, source_target_pairs={{0,6},{1,7},{2,4},{3,5},{4,2},{5,3},{6,0},{7,1},{8,14},{9,15},{10,... | collective-permute-start | bytes 786440 | tf_op jit(solution)/shard_map/ppermute | solution.py:452
  16.7 2.6 %collective-permute-done.refs_4_ = bf16[2,256,256]{2,1,0:T(8,128)(2,1)S(1)} collective-permute-done((bf16[2,256,256]{2,1,0:T(8,128)(2,1)}, bf16[2,256,256]{2,1,0:T(8,128)(2,1)S(1)}, u32[]{:S(2)}, u32[]{:S(2)}) %collective-permute-start) | collective-permute-done | bytes 262176 | tf_op jit(solution)/shard_map/ppermute | solution.py:452
  20.0 7.0 %collective-permute-done.2.refs_2_ = bf16[2,256,256]{2,1,0:T(8,128)(2,1)S(1)} collective-permute-done((bf16[2,256,256]{2,1,0:T(8,128)(2,1)S(1)}, bf16[2,256,256]{2,1,0:T(8,128)(2,1)S(1)}, u32[]{:S(2)}, u32[]{:S(2)}) %collective-permute-start.2) | collective-permute-done | bytes 262176 | tf_op jit(solution)/shard_map/ppermute | solution.py:452
  27.0 2.6 %collective-permute-start.5 = (bf16[2,256,256]{2,1,0:T(8,128)(2,1)S(1)}, bf16[2,256,256]{2,1,0:T(8,128)(2,1)S(1)}, u32[]{:S(2)}, u32[]{:S(2)}) collective-permute-start(bf16[2,256,256]{2,1,0:T(8,128)(2,1)S(1)} %copy-done.4), channel_id=1, source_target_pairs={{0,12},{1,13},{2,14},{3,15},{4,8},{5,9},{6,10},{7,11},{8,4},{9,5},... | collective-permute-start | bytes 786440 | tf_op jit(solution)/shard_map/ppermute | solution.py:452
  31.1 9.4 %collective-permute-done.4.refs_3_ = bf16[2,256,256]{2,1,0:T(8,128)(2,1)S(1)} collective-permute-done((bf16[2,256,256]{2,1,0:T(8,128)(2,1)S(1)}, bf16[2,256,256]{2,1,0:T(8,128)(2,1)S(1)}, u32[]{:S(2)}, u32[]{:S(2)}) %collective-permute-start.4) | collective-permute-done | bytes 262176 | tf_op jit(solution)/shard_map/ppermute | solution.py:452
  40.5 1.4 %collective-permute-start.6 = (bf16[2,256,256]{2,1,0:T(8,128)(2,1)S(1)}, bf16[2,256,256]{2,1,0:T(8,128)(2,1)S(1)}, u32[]{:S(2)}, u32[]{:S(2)}) collective-permute-start(bf16[2,256,256]{2,1,0:T(8,128)(2,1)S(1)} %copy-done.3), channel_id=1, source_target_pairs={{0,14},{1,15},{2,12},{3,13},{4,10},{5,11},{6,8},{7,9},{8,6},{9,7},... | collective-permute-start | bytes 786440 | tf_op jit(solution)/shard_map/ppermute | solution.py:452
  42.0 1.8 %collective-permute-start.11 = (bf16[2,256,256]{2,1,0:T(8,128)(2,1)S(1)}, bf16[2,256,256]{2,1,0:T(8,128)(2,1)S(1)}, u32[]{:S(2)}, u32[]{:S(2)}) collective-permute-start(bf16[2,256,256]{2,1,0:T(8,128)(2,1)S(1)} %collective-permute-done.refs_4_), channel_id=1, source_target_pairs={{0,1},{1,0},{2,3},{3,2},{4,5},{5,4},{6,7},{7,6},{8,9},{9,8},{10,11... | collective-permute-start | bytes 786440 | tf_op jit(solution)/shard_map/ppermute | solution.py:452
  44.4 10.0 %collective-permute-done.6.refs_7_ = bf16[2,256,256]{2,1,0:T(8,128)(2,1)S(1)} collective-permute-done((bf16[2,256,256]{2,1,0:T(8,128)(2,1)S(1)}, bf16[2,256,256]{2,1,0:T(8,128)(2,1)S(1)}, u32[]{:S(2)}, u32[]{:S(2)}) %collective-permute-start.6) | collective-permute-done | bytes 262176 | tf_op jit(solution)/shard_map/ppermute | solution.py:452
  54.4 1.3 collective-permute-start.14
  56.9 1.3 shard_map.61
  59.1 2.4 %collective-permute-start.19 = (bf16[2,256,256]{2,1,0:T(8,128)(2,1)S(1)}, bf16[2,256,256]{2,1,0:T(8,128)(2,1)S(1)}, u32[]{:S(2)}, u32[]{:S(2)}) collective-permute-start(bf16[2,256,256]{2,1,0:T(8,128)(2,1)S(1)} %get-tuple-element.110), channel_id=1, source_target_pairs={{0,12},{1,13},{2,14},{3,15},{4,8},{5,9},{6,10},{7,11},{8,4},{9,5},... | collective-permute-start | bytes 786440 | tf_op jit(solution)/shard_map/ppermute | solution.py:452
  62.5 10.6 %collective-permute-done.19.refs_5_ = bf16[2,256,256]{2,1,0:T(8,128)(2,1)S(1)} collective-permute-done((bf16[2,256,256]{2,1,0:T(8,128)(2,1)S(1)}, bf16[2,256,256]{2,1,0:T(8,128)(2,1)S(1)}, u32[]{:S(2)}, u32[]{:S(2)}) %collective-permute-start.19) | collective-permute-done | bytes 262176 | tf_op jit(solution)/shard_map/ppermute | solution.py:452
  74.7 1.8 %collective-permute-start.22 = (bf16[2,256,256]{2,1,0:T(8,128)(2,1)S(1)}, bf16[2,256,256]{2,1,0:T(8,128)(2,1)S(1)}, u32[]{:S(2)}, u32[]{:S(2)}) collective-permute-start(bf16[2,256,256]{2,1,0:T(8,128)(2,1)S(1)} %get-tuple-element.116), channel_id=1, source_target_pairs={{0,8},{1,9},{2,10},{3,11},{4,12},{5,13},{6,14},{7,15},{8,0},{9,1},... | collective-permute-start | bytes 786440 | tf_op jit(solution)/shard_map/ppermute | solution.py:452
  77.8 2.2 %collective-permute-done.16 = f32[1,3,128,128]{3,2,1,0:T(8,128)S(1)} collective-permute-done((f32[1,3,128,128]{3,2,1,0:T(8,128)S(1)}, f32[1,3,128,128]{3,2,1,0:T(8,128)S(1)}, u32[]{:S(2)}, u32[]{:S(2)}) %collective-permute-start.16) | collective-permute-done | bytes 196640 | tf_op jit(solution)/shard_map/ppermute | solution.py:452
  80.0 2.1 %collective-permute-done.21 = f32[1,3,128,128]{3,2,1,0:T(8,128)S(1)} collective-permute-done((f32[1,3,128,128]{3,2,1,0:T(8,128)S(1)}, f32[1,3,128,128]{3,2,1,0:T(8,128)S(1)}, u32[]{:S(2)}, u32[]{:S(2)}) %collective-permute-start.21) | collective-permute-done | bytes 196640 | tf_op jit(solution)/shard_map/ppermute | solution.py:452
  82.2 4.6 %collective-permute-done.22.refs_4_ = bf16[2,256,256]{2,1,0:T(8,128)(2,1)S(1)} collective-permute-done((bf16[2,256,256]{2,1,0:T(8,128)(2,1)S(1)}, bf16[2,256,256]{2,1,0:T(8,128)(2,1)S(1)}, u32[]{:S(2)}, u32[]{:S(2)}) %collective-permute-start.22) | collective-permute-done | bytes 262176 | tf_op jit(solution)/shard_map/ppermute | solution.py:452
  86.8 3.5 %collective-permute-start.24 = (f32[1,3,128,128]{3,2,1,0:T(8,128)S(1)}, f32[1,3,128,128]{3,2,1,0:T(8,128)S(1)}, u32[]{:S(2)}, u32[]{:S(2)}) collective-permute-start(f32[1,3,128,128]{3,2,1,0:T(8,128)S(1)} %fusion), channel_id=1, source_target_pairs={{0,8},{1,9},{2,10},{3,11},{4,12},{5,13},{6,14},{7,15},{8,0},{9,1},... | collective-permute-start | bytes 589832 | tf_op jit(solution)/shard_map/ppermute | solution.py:452
  90.3 7.7 %collective-permute-done.24 = f32[1,3,128,128]{3,2,1,0:T(8,128)S(1)} collective-permute-done((f32[1,3,128,128]{3,2,1,0:T(8,128)S(1)}, f32[1,3,128,128]{3,2,1,0:T(8,128)S(1)}, u32[]{:S(2)}, u32[]{:S(2)}) %collective-permute-start.24) | collective-permute-done | bytes 196640 | tf_op jit(solution)/shard_map/ppermute | solution.py:452
  98.0 1.7 %collective-permute-start.30 = (bf16[2,256,256]{2,1,0:T(8,128)(2,1)S(1)}, bf16[2,256,256]{2,1,0:T(8,128)(2,1)S(1)}, u32[]{:S(2)}, u32[]{:S(2)}) collective-permute-start(bf16[2,256,256]{2,1,0:T(8,128)(2,1)S(1)} %collective-permute-done.22.refs_4_), channel_id=1, source_target_pairs={{0,1},{1,0},{2,3},{3,2},{4,5},{5,4},{6,7},{7,6},{8,9},{9,8},{10,11... | collective-permute-start | bytes 786440 | tf_op jit(solution)/shard_map/ppermute | solution.py:452
  100.9 3.7 %collective-permute-start.32 = (bf16[2,256,256]{2,1,0:T(8,128)(2,1)S(1)}, bf16[2,256,256]{2,1,0:T(8,128)(2,1)S(1)}, u32[]{:S(2)}, u32[]{:S(2)}) collective-permute-start(bf16[2,256,256]{2,1,0:T(8,128)(2,1)S(1)} %get-tuple-element.150), channel_id=1, source_target_pairs={{0,10},{1,11},{2,8},{3,9},{4,14},{5,15},{6,12},{7,13},{8,2},{9,3},... | collective-permute-start | bytes 786440 | tf_op jit(solution)/shard_map/ppermute | solution.py:452
  104.6 9.6 %shard_map.63 = (bf16[3,128,128]{2,1,0:T(8,128)(2,1)S(1)}, bf16[8,256,256]{2,1,0:T(8,128)(2,1)S(1)}) custom-call(f32[3,128,128]{2,1,0:T(8,128)S(1)} %bitcast.12, bf16[8,256,256]{2,1,0:T(8,128)(2,1)S(1)} %get-tuple-element.137.rows_ref.rows_t_ref), custom_call_target="tpu_custom_call" | custom-call | bytes 140000000 | tf_op jit(solution)/shard_map/pallas_call | solution.py:298
  114.2 1.2 collective-permute-start.33
  117.2 2.3 %shard_map.64 = (f32[768,256]{1,0:T(8,128)S(1)}, bf16[768,1024]{1,0:T(8,128)(2,1)S(1)}) custom-call(s32[1]{0:T(128)} %bitcast.ids_ref, bf16[768,4096]{1,0:T(8,128)(2,1)S(1)} %bitcast.11, bf16[2,256,256]{2,1,0:T(8,128)(2,1)S(1)} %get-tuple-element.121.refs_0_, bf16[2,256,256]{2,1,0:T(8,128)(2,1)S(1)} %collective-permute-done.23.refs_1_, ...), custom_call_target="tpu_custom_call" | custom-call | tf_op jit(solution)/shard_map/pallas_call | solution.py:413
  119.5 4.2 %collective-permute-done.31 = bf16[1,3,128,128]{3,2,1,0:T(8,128)(2,1)S(1)} collective-permute-done((bf16[1,3,128,128]{3,2,1,0:T(8,128)(2,1)S(1)}, bf16[1,3,128,128]{3,2,1,0:T(8,128)(2,1)S(1)}, u32[]{:S(2)}, u32[]{:S(2)}) %collective-permute-start.31) | collective-permute-done | bytes 98336 | tf_op jit(solution)/shard_map/ppermute | solution.py:452
  124.1 4.7 %collective-permute-done.33.refs_1_ = bf16[2,256,256]{2,1,0:T(8,128)(2,1)S(1)} collective-permute-done((bf16[2,256,256]{2,1,0:T(8,128)(2,1)S(1)}, bf16[2,256,256]{2,1,0:T(8,128)(2,1)S(1)}, u32[]{:S(2)}, u32[]{:S(2)}) %collective-permute-start.33) | collective-permute-done | bytes 262176 | tf_op jit(solution)/shard_map/ppermute | solution.py:452
  132.4 1.4 %shard_map.67 = bf16[8,256,256]{2,1,0:T(8,128)(2,1)} custom-call(s32[1]{0:T(128)} %bitcast.ids_ref, bf16[8,256,256]{2,1,0:T(8,128)(2,1)S(1)} %get-tuple-element.163.rows_ref, bf16[4,3,128,128]{3,2,1,0:T(8,128)(2,1)S(1)} %pad_maximum_fusion.near_ref, bf16[4,3,128,128]{3,2,1,0:T(8,128)(2,1)S(1)} %pad_maximum_fusion.1.far_ref), custom_call_target="tpu_custom_call" | custom-call | bytes 7000000 | tf_op jit(solution)/shard_map/pallas_call | solution.py:334
  134.4 1.8 %shard_map.66 = bf16[768,256]{1,0:T(8,128)(2,1)} custom-call(s32[1]{0:T(128)} %bitcast.ids_ref, s32[16]{0:T(128)S(1)} %copy-done.2, bf16[768,256]{1,0:T(8,128)(2,1)S(1)} %get-tuple-element.159.high_ref, bf16[768,256]{1,0:T(8,128)(2,1)S(1)} %get-tuple-element.160.low_ref, bf16[4,3,128,128]{3,2,1,0:T(8,128)(2,1)S(1)} %pad_maximum_fusion.near_ref, ...), custom_call_target="tpu_custom_call" | custom-call | tf_op jit(solution)/shard_map/pallas_call | solution.py:440
  (85 shorter events, 17.4 us)
Async XLA Ops:
  5.1 14.3 %collective-permute-start = (bf16[2,256,256]{2,1,0:T(8,128)(2,1)}, bf16[2,256,256]{2,1,0:T(8,128)(2,1)S(1)}, u32[]{:S(2)}, u32[]{:S(2)}) collective-permute-start(bf16[2,256,256]{2,1,0:T(8,128)(2,1)} %get-tuple-element.86), channel_id=1, source_target_pairs={{0,8},{1,9},{2,10},{3,11},{4,12},{5,13},{6,14},{7,15},{8,0},{9,1},... | collective-permute-start | bytes 786440 | tf_op jit(solution)/shard_map/ppermute | solution.py:452
  13.0 7.0 %collective-permute-start.1 = (bf16[2,256,256]{2,1,0:T(8,128)(2,1)S(1)}, bf16[2,256,256]{2,1,0:T(8,128)(2,1)S(1)}, u32[]{:S(2)}, u32[]{:S(2)}) collective-permute-start(bf16[2,256,256]{2,1,0:T(8,128)(2,1)S(1)} %get-tuple-element.87), channel_id=1, source_target_pairs={{0,2},{1,3},{2,0},{3,1},{4,6},{5,7},{6,4},{7,5},{8,10},{9,11},{10,... | collective-permute-start | bytes 786440 | tf_op jit(solution)/shard_map/ppermute | solution.py:452
  14.3 12.7 %collective-permute-start.2 = (bf16[2,256,256]{2,1,0:T(8,128)(2,1)S(1)}, bf16[2,256,256]{2,1,0:T(8,128)(2,1)S(1)}, u32[]{:S(2)}, u32[]{:S(2)}) collective-permute-start(bf16[2,256,256]{2,1,0:T(8,128)(2,1)S(1)} %get-tuple-element.88), channel_id=1, source_target_pairs={{0,4},{1,5},{2,6},{3,7},{4,0},{5,1},{6,2},{7,3},{8,12},{9,13},{10,... | collective-permute-start | bytes 786440 | tf_op jit(solution)/shard_map/ppermute | solution.py:452
  14.5 16.3 %collective-permute-start.3 = (bf16[2,256,256]{2,1,0:T(8,128)(2,1)S(1)}, bf16[2,256,256]{2,1,0:T(8,128)(2,1)S(1)}, u32[]{:S(2)}, u32[]{:S(2)}) collective-permute-start(bf16[2,256,256]{2,1,0:T(8,128)(2,1)S(1)} %copy-done.5), channel_id=1, source_target_pairs={{0,10},{1,11},{2,8},{3,9},{4,14},{5,15},{6,12},{7,13},{8,2},{9,3},... | collective-permute-start | bytes 786440 | tf_op jit(solution)/shard_map/ppermute | solution.py:452
  14.5 26.0 %collective-permute-start.4 = (bf16[2,256,256]{2,1,0:T(8,128)(2,1)S(1)}, bf16[2,256,256]{2,1,0:T(8,128)(2,1)S(1)}, u32[]{:S(2)}, u32[]{:S(2)}) collective-permute-start(bf16[2,256,256]{2,1,0:T(8,128)(2,1)S(1)} %get-tuple-element.93), channel_id=1, source_target_pairs={{0,6},{1,7},{2,4},{3,5},{4,2},{5,3},{6,0},{7,1},{8,14},{9,15},{10,... | collective-permute-start | bytes 786440 | tf_op jit(solution)/shard_map/ppermute | solution.py:452
  19.4 22.6 %collective-permute-start.7 = (bf16[2,256,256]{2,1,0:T(8,128)(2,1)S(1)}, bf16[2,256,256]{2,1,0:T(8,128)(2,1)S(1)}, u32[]{:S(2)}, u32[]{:S(2)}) collective-permute-start(bf16[2,256,256]{2,1,0:T(8,128)(2,1)S(1)} %get-tuple-element.84.refs_0_), channel_id=1, source_target_pairs={{0,1},{1,0},{2,3},{3,2},{4,5},{5,4},{6,7},{7,6},{8,9},{9,8},{10,11... | collective-permute-start | bytes 786440 | tf_op jit(solution)/shard_map/ppermute | solution.py:452
  27.0 16.7 %collective-permute-start.5 = (bf16[2,256,256]{2,1,0:T(8,128)(2,1)S(1)}, bf16[2,256,256]{2,1,0:T(8,128)(2,1)S(1)}, u32[]{:S(2)}, u32[]{:S(2)}) collective-permute-start(bf16[2,256,256]{2,1,0:T(8,128)(2,1)S(1)} %copy-done.4), channel_id=1, source_target_pairs={{0,12},{1,13},{2,14},{3,15},{4,8},{5,9},{6,10},{7,11},{8,4},{9,5},... | collective-permute-start | bytes 786440 | tf_op jit(solution)/shard_map/ppermute | solution.py:452
  29.6 14.2 %collective-permute-start.8 = (bf16[2,256,256]{2,1,0:T(8,128)(2,1)S(1)}, bf16[2,256,256]{2,1,0:T(8,128)(2,1)S(1)}, u32[]{:S(2)}, u32[]{:S(2)}) collective-permute-start(bf16[2,256,256]{2,1,0:T(8,128)(2,1)S(1)} %collective-permute-done.1.refs_1_), channel_id=1, source_target_pairs={{0,1},{1,0},{2,3},{3,2},{4,5},{5,4},{6,7},{7,6},{8,9},{9,8},{10,11... | collective-permute-start | bytes 786440 | tf_op jit(solution)/shard_map/ppermute | solution.py:452
  30.8 13.5 %collective-permute-start.9 = (bf16[2,256,256]{2,1,0:T(8,128)(2,1)S(1)}, bf16[2,256,256]{2,1,0:T(8,128)(2,1)S(1)}, u32[]{:S(2)}, u32[]{:S(2)}) collective-permute-start(bf16[2,256,256]{2,1,0:T(8,128)(2,1)S(1)} %collective-permute-done.2.refs_2_), channel_id=1, source_target_pairs={{0,1},{1,0},{2,3},{3,2},{4,5},{5,4},{6,7},{7,6},{8,9},{9,8},{10,11... | collective-permute-start | bytes 786440 | tf_op jit(solution)/shard_map/ppermute | solution.py:452
  40.5 13.9 %collective-permute-start.6 = (bf16[2,256,256]{2,1,0:T(8,128)(2,1)S(1)}, bf16[2,256,256]{2,1,0:T(8,128)(2,1)S(1)}, u32[]{:S(2)}, u32[]{:S(2)}) collective-permute-start(bf16[2,256,256]{2,1,0:T(8,128)(2,1)S(1)} %copy-done.3), channel_id=1, source_target_pairs={{0,14},{1,15},{2,12},{3,13},{4,10},{5,11},{6,8},{7,9},{8,6},{9,7},... | collective-permute-start | bytes 786440 | tf_op jit(solution)/shard_map/ppermute | solution.py:452
  42.0 13.8 %collective-permute-start.11 = (bf16[2,256,256]{2,1,0:T(8,128)(2,1)S(1)}, bf16[2,256,256]{2,1,0:T(8,128)(2,1)S(1)}, u32[]{:S(2)}, u32[]{:S(2)}) collective-permute-start(bf16[2,256,256]{2,1,0:T(8,128)(2,1)S(1)} %collective-permute-done.refs_4_), channel_id=1, source_target_pairs={{0,1},{1,0},{2,3},{3,2},{4,5},{5,4},{6,7},{7,6},{8,9},{9,8},{10,11... | collective-permute-start | bytes 786440 | tf_op jit(solution)/shard_map/ppermute | solution.py:452
  43.8 12.0 %collective-permute-start.10 = (bf16[2,256,256]{2,1,0:T(8,128)(2,1)S(1)}, bf16[2,256,256]{2,1,0:T(8,128)(2,1)S(1)}, u32[]{:S(2)}, u32[]{:S(2)}) collective-permute-start(bf16[2,256,256]{2,1,0:T(8,128)(2,1)S(1)} %collective-permute-done.4.refs_3_), channel_id=1, source_target_pairs={{0,1},{1,0},{2,3},{3,2},{4,5},{5,4},{6,7},{7,6},{8,9},{9,8},{10,11... | collective-permute-start | bytes 786440 | tf_op jit(solution)/shard_map/ppermute | solution.py:452
  43.9 11.9 %collective-permute-start.12 = (bf16[2,256,256]{2,1,0:T(8,128)(2,1)S(1)}, bf16[2,256,256]{2,1,0:T(8,128)(2,1)S(1)}, u32[]{:S(2)}, u32[]{:S(2)}) collective-permute-start(bf16[2,256,256]{2,1,0:T(8,128)(2,1)S(1)} %collective-permute-done.3.refs_5_), channel_id=1, source_target_pairs={{0,1},{1,0},{2,3},{3,2},{4,5},{5,4},{6,7},{7,6},{8,9},{9,8},{10,11... | collective-permute-start | bytes 786440 | tf_op jit(solution)/shard_map/ppermute | solution.py:452
  44.3 11.5 %collective-permute-start.13 = (bf16[2,256,256]{2,1,0:T(8,128)(2,1)S(1)}, bf16[2,256,256]{2,1,0:T(8,128)(2,1)S(1)}, u32[]{:S(2)}, u32[]{:S(2)}) collective-permute-start(bf16[2,256,256]{2,1,0:T(8,128)(2,1)S(1)} %collective-permute-done.5.refs_6_), channel_id=1, source_target_pairs={{0,1},{1,0},{2,3},{3,2},{4,5},{5,4},{6,7},{7,6},{8,9},{9,8},{10,11... | collective-permute-start | bytes 786440 | tf_op jit(solution)/shard_map/ppermute | solution.py:452
  59.1 14.0 %collective-permute-start.19 = (bf16[2,256,256]{2,1,0:T(8,128)(2,1)S(1)}, bf16[2,256,256]{2,1,0:T(8,128)(2,1)S(1)}, u32[]{:S(2)}, u32[]{:S(2)}) collective-permute-start(bf16[2,256,256]{2,1,0:T(8,128)(2,1)S(1)} %get-tuple-element.110), channel_id=1, source_target_pairs={{0,12},{1,13},{2,14},{3,15},{4,8},{5,9},{6,10},{7,11},{8,4},{9,5},... | collective-permute-start | bytes 786440 | tf_op jit(solution)/shard_map/ppermute | solution.py:452
  61.6 12.1 %collective-permute-start.17 = (f32[1,3,128,128]{3,2,1,0:T(8,128)S(1)}, f32[1,3,128,128]{3,2,1,0:T(8,128)S(1)}, u32[]{:S(2)}, u32[]{:S(2)}) collective-permute-start(f32[1,3,128,128]{3,2,1,0:T(8,128)S(1)} %get-tuple-element.167), channel_id=1, source_target_pairs={{0,2},{1,3},{2,0},{3,1},{4,6},{5,7},{6,4},{7,5},{8,10},{9,11},{10,... | collective-permute-start | bytes 589832 | tf_op jit(solution)/shard_map/ppermute | solution.py:452
  62.5 11.3 %collective-permute-start.18 = (bf16[2,256,256]{2,1,0:T(8,128)(2,1)S(1)}, bf16[2,256,256]{2,1,0:T(8,128)(2,1)S(1)}, u32[]{:S(2)}, u32[]{:S(2)}) collective-permute-start(bf16[2,256,256]{2,1,0:T(8,128)(2,1)S(1)} %get-tuple-element.106), channel_id=1, source_target_pairs={{0,4},{1,5},{2,6},{3,7},{4,0},{5,1},{6,2},{7,3},{8,12},{9,13},{10,... | collective-permute-start | bytes 786440 | tf_op jit(solution)/shard_map/ppermute | solution.py:452
  74.7 7.4 %collective-permute-start.21 = (f32[1,3,128,128]{3,2,1,0:T(8,128)S(1)}, f32[1,3,128,128]{3,2,1,0:T(8,128)S(1)}, u32[]{:S(2)}, u32[]{:S(2)}) collective-permute-start(f32[1,3,128,128]{3,2,1,0:T(8,128)S(1)} %slice_add_fusion.2), channel_id=1, source_target_pairs={{0,4},{1,5},{2,6},{3,7},{4,0},{5,1},{6,2},{7,3},{8,12},{9,13},{10,... | collective-permute-start | bytes 589832 | tf_op jit(solution)/shard_map/ppermute | solution.py:452
  74.7 12.1 %collective-permute-start.22 = (bf16[2,256,256]{2,1,0:T(8,128)(2,1)S(1)}, bf16[2,256,256]{2,1,0:T(8,128)(2,1)S(1)}, u32[]{:S(2)}, u32[]{:S(2)}) collective-permute-start(bf16[2,256,256]{2,1,0:T(8,128)(2,1)S(1)} %get-tuple-element.116), channel_id=1, source_target_pairs={{0,8},{1,9},{2,10},{3,11},{4,12},{5,13},{6,14},{7,15},{8,0},{9,1},... | collective-permute-start | bytes 786440 | tf_op jit(solution)/shard_map/ppermute | solution.py:452
  76.5 10.3 %collective-permute-start.23 = (bf16[2,256,256]{2,1,0:T(8,128)(2,1)S(1)}, bf16[2,256,256]{2,1,0:T(8,128)(2,1)S(1)}, u32[]{:S(2)}, u32[]{:S(2)}) collective-permute-start(bf16[2,256,256]{2,1,0:T(8,128)(2,1)S(1)} %get-tuple-element.117), channel_id=1, source_target_pairs={{0,2},{1,3},{2,0},{3,1},{4,6},{5,7},{6,4},{7,5},{8,10},{9,11},{10,... | collective-permute-start | bytes 786440 | tf_op jit(solution)/shard_map/ppermute | solution.py:452
  77.6 20.5 %collective-permute-start.25 = (bf16[2,256,256]{2,1,0:T(8,128)(2,1)S(1)}, bf16[2,256,256]{2,1,0:T(8,128)(2,1)S(1)}, u32[]{:S(2)}, u32[]{:S(2)}) collective-permute-start(bf16[2,256,256]{2,1,0:T(8,128)(2,1)S(1)} %get-tuple-element.119), channel_id=1, source_target_pairs={{0,6},{1,7},{2,4},{3,5},{4,2},{5,3},{6,0},{7,1},{8,14},{9,15},{10,... | collective-permute-start | bytes 786440 | tf_op jit(solution)/shard_map/ppermute | solution.py:452
  86.8 11.2 %collective-permute-start.24 = (f32[1,3,128,128]{3,2,1,0:T(8,128)S(1)}, f32[1,3,128,128]{3,2,1,0:T(8,128)S(1)}, u32[]{:S(2)}, u32[]{:S(2)}) collective-permute-start(f32[1,3,128,128]{3,2,1,0:T(8,128)S(1)} %fusion), channel_id=1, source_target_pairs={{0,8},{1,9},{2,10},{3,11},{4,12},{5,13},{6,14},{7,15},{8,0},{9,1},... | collective-permute-start | bytes 589832 | tf_op jit(solution)/shard_map/ppermute | solution.py:452
  99.8 14.4 %collective-permute-start.29 = (bf16[2,256,256]{2,1,0:T(8,128)(2,1)S(1)}, bf16[2,256,256]{2,1,0:T(8,128)(2,1)S(1)}, u32[]{:S(2)}, u32[]{:S(2)}) collective-permute-start(bf16[2,256,256]{2,1,0:T(8,128)(2,1)S(1)} %collective-permute-done.25.refs_3_), channel_id=1, source_target_pairs={{0,1},{1,0},{2,3},{3,2},{4,5},{5,4},{6,7},{7,6},{8,9},{9,8},{10,11... | collective-permute-start | bytes 786440 | tf_op jit(solution)/shard_map/ppermute | solution.py:452
  99.8 14.4 %collective-permute-start.28 = (bf16[2,256,256]{2,1,0:T(8,128)(2,1)S(1)}, bf16[2,256,256]{2,1,0:T(8,128)(2,1)S(1)}, u32[]{:S(2)}, u32[]{:S(2)}) collective-permute-start(bf16[2,256,256]{2,1,0:T(8,128)(2,1)S(1)} %collective-permute-done.18.refs_2_), channel_id=1, source_target_pairs={{0,1},{1,0},{2,3},{3,2},{4,5},{5,4},{6,7},{7,6},{8,9},{9,8},{10,11... | collective-permute-start | bytes 786440 | tf_op jit(solution)/shard_map/ppermute | solution.py:452
  100.3 13.9 %collective-permute-start.27 = (bf16[2,256,256]{2,1,0:T(8,128)(2,1)S(1)}, bf16[2,256,256]{2,1,0:T(8,128)(2,1)S(1)}, u32[]{:S(2)}, u32[]{:S(2)}) collective-permute-start(bf16[2,256,256]{2,1,0:T(8,128)(2,1)S(1)} %collective-permute-done.23.refs_1_), channel_id=1, source_target_pairs={{0,1},{1,0},{2,3},{3,2},{4,5},{5,4},{6,7},{7,6},{8,9},{9,8},{10,11... | collective-permute-start | bytes 786440 | tf_op jit(solution)/shard_map/ppermute | solution.py:452
  100.3 13.9 %collective-permute-start.26 = (bf16[2,256,256]{2,1,0:T(8,128)(2,1)S(1)}, bf16[2,256,256]{2,1,0:T(8,128)(2,1)S(1)}, u32[]{:S(2)}, u32[]{:S(2)}) collective-permute-start(bf16[2,256,256]{2,1,0:T(8,128)(2,1)S(1)} %get-tuple-element.121.refs_0_), channel_id=1, source_target_pairs={{0,1},{1,0},{2,3},{3,2},{4,5},{5,4},{6,7},{7,6},{8,9},{9,8},{10,11... | collective-permute-start | bytes 786440 | tf_op jit(solution)/shard_map/ppermute | solution.py:452
  100.9 18.5 %collective-permute-start.32 = (bf16[2,256,256]{2,1,0:T(8,128)(2,1)S(1)}, bf16[2,256,256]{2,1,0:T(8,128)(2,1)S(1)}, u32[]{:S(2)}, u32[]{:S(2)}) collective-permute-start(bf16[2,256,256]{2,1,0:T(8,128)(2,1)S(1)} %get-tuple-element.150), channel_id=1, source_target_pairs={{0,10},{1,11},{2,8},{3,9},{4,14},{5,15},{6,12},{7,13},{8,2},{9,3},... | collective-permute-start | bytes 786440 | tf_op jit(solution)/shard_map/ppermute | solution.py:452
  114.2 14.6 %collective-permute-start.33 = (bf16[2,256,256]{2,1,0:T(8,128)(2,1)S(1)}, bf16[2,256,256]{2,1,0:T(8,128)(2,1)S(1)}, u32[]{:S(2)}, u32[]{:S(2)}) collective-permute-start(bf16[2,256,256]{2,1,0:T(8,128)(2,1)S(1)} %get-tuple-element.155), channel_id=1, source_target_pairs={{0,14},{1,15},{2,12},{3,13},{4,10},{5,11},{6,8},{7,9},{8,6},{9,7},... | collective-permute-start | bytes 786440 | tf_op jit(solution)/shard_map/ppermute | solution.py:452
  115.5 8.2 %collective-permute-start.31 = (bf16[1,3,128,128]{3,2,1,0:T(8,128)(2,1)S(1)}, bf16[1,3,128,128]{3,2,1,0:T(8,128)(2,1)S(1)}, u32[]{:S(2)}, u32[]{:S(2)}) collective-permute-start(bf16[1,3,128,128]{3,2,1,0:T(8,128)(2,1)S(1)} %bitcast.13), channel_id=1, source_target_pairs={{0,4},{1,5},{2,6},{3,7},{4,0},{5,1},{6,2},{7,3},{8,12},{9,13},{10,... | collective-permute-start | bytes 294920 | tf_op jit(solution)/shard_map/ppermute | solution.py:452
  115.5 13.9 %collective-permute-start.37 = (bf16[1,3,128,128]{3,2,1,0:T(8,128)(2,1)S(1)}, bf16[1,3,128,128]{3,2,1,0:T(8,128)(2,1)S(1)}, u32[]{:S(2)}, u32[]{:S(2)}) collective-permute-start(bf16[1,3,128,128]{3,2,1,0:T(8,128)(2,1)S(1)} %bitcast.14), channel_id=1, source_target_pairs={{0,1},{1,0},{2,3},{3,2},{4,5},{5,4},{6,7},{7,6},{8,9},{9,8},{10,11... | collective-permute-start | bytes 294920 | tf_op jit(solution)/shard_map/ppermute | solution.py:452
  116.4 13.4 %collective-permute-start.35 = (bf16[1,3,128,128]{3,2,1,0:T(8,128)(2,1)S(1)}, bf16[1,3,128,128]{3,2,1,0:T(8,128)(2,1)S(1)}, u32[]{:S(2)}, u32[]{:S(2)}) collective-permute-start(bf16[1,3,128,128]{3,2,1,0:T(8,128)(2,1)S(1)} %bitcast.15), channel_id=1, source_target_pairs={{0,2},{1,3},{2,0},{3,1},{4,6},{5,7},{6,4},{7,5},{8,10},{9,11},{10,... | collective-permute-start | bytes 294920 | tf_op jit(solution)/shard_map/ppermute | solution.py:452
  123.7 7.2 %collective-permute-start.36 = (bf16[1,3,128,128]{3,2,1,0:T(8,128)(2,1)S(1)}, bf16[1,3,128,128]{3,2,1,0:T(8,128)(2,1)S(1)}, u32[]{:S(2)}, u32[]{:S(2)}) collective-permute-start(bf16[1,3,128,128]{3,2,1,0:T(8,128)(2,1)S(1)} %collective-permute-done.31), channel_id=1, source_target_pairs={{0,2},{1,3},{2,0},{3,1},{4,6},{5,7},{6,4},{7,5},{8,10},{9,11},{10,... | collective-permute-start | bytes 294920 | tf_op jit(solution)/shard_map/ppermute | solution.py:452
  (18 other events, 310.8 us)

commit v5 on v4

--- a/solution.py
+++ b/solution.py
@@ -75,9 +75,9 @@
     cov_copy.start()
     sketch_copy.start()
     copies[0].start()
+    copies[1].start()
     cov_copy.wait()
     sketch_copy.wait()
-    copies[1].start()
     weighted = dot(sketch[...], cov[...], ((0,), (1,))).astype(BF16)
     weighted_ref[...] = weighted
     for part in range(2):
@@ -309,8 +309,13 @@
     )(gram, rows_t)
 
 
+def whole_factor(ref, index):
+    first, below, second = (ref[index, i] for i in range(3))
+    top = jnp.concatenate([first, jnp.zeros_like(first)], axis=1)
+    return jnp.concatenate([top, jnp.concatenate([below, second], axis=1)], axis=0)
+
+
 def basis_kernel(ids_ref, rows_ref, near_ref, far_ref, out_hbm, out, sems):
-    half = out.shape[2] // 2
     count = near_ref.shape[0]
     base = base_cluster(ids_ref[0], 4 * count)
 
@@ -318,13 +323,8 @@
         return pltpu.make_async_copy(out.at[k], out_hbm.at[base ^ k], sems.at[k])
 
     for k in range(2 * count):
-        refs, i = (near_ref, k) if k < count else (far_ref, k - count)
-        block = rows_ref[base ^ k]
-        out[k, :, :half] = dot(block[:, :half], refs[i, 0], ((1,), (1,))).astype(BF16)
-        out[k, :, half:] = (
-            dot(block[:, :half], refs[i, 1], ((1,), (1,)))
-            + dot(block[:, half:], refs[i, 2], ((1,), (1,)))
-        ).astype(BF16)
+        ref, i = (near_ref, k) if k < count else (far_ref, k - count)
+        out[k] = dot(rows_ref[base ^ k], whole_factor(ref, i), ((1,), (1,))).astype(BF16)
         copy(k).start()
     for k in range(2 * count):
         copy(k).wait()
@@ -390,21 +390,21 @@
 def coef_kernel(ids_ref, member_ref, high_ref, low_ref, near_ref, far_ref, out_hbm, out, out_sem):
     me = ids_ref[0]
     slot = member_ref[me] ^ base_cluster(me, member_ref.shape[0])
-    near = slot < near_ref.shape[0]
     inside = lax.rem(slot, near_ref.shape[0])
-    half = out.shape[1] // 2
-
-    def times(i, part):
-        factor = jnp.where(near, near_ref[inside, i], far_ref[inside, i])
-        high, low = high_ref[:, part], low_ref[:, part]
-        return dot(high, factor, ((1,), (1,))) + dot(low, factor, ((1,), (1,)))
-
-    left, right = slice(0, half), slice(half, 2 * half)
-    out[:, left] = times(0, left).astype(BF16)
-    out[:, right] = (times(1, left) + times(2, right)).astype(BF16)
-    out_copy = pltpu.make_async_copy(out, out_hbm, out_sem)
-    out_copy.start()
-    out_copy.wait()
+    factor = jnp.where(
+        slot < near_ref.shape[0], whole_factor(near_ref, inside), whole_factor(far_ref, inside)
+    )
+    twice = jnp.concatenate([factor, factor], axis=1)
+    part = out.shape[0] // 2
+    copies = []
+    for i in range(2):
+        piece = pl.ds(i * part, part)
+        both = jnp.concatenate([high_ref[piece], low_ref[piece]], axis=1)
+        out[piece] = dot(both, twice, ((1,), (1,))).astype(BF16)
+        copies.append(pltpu.make_async_copy(out.at[piece], out_hbm.at[piece], out_sem.at[i]))
+        copies[i].start()
+    for copy in copies:
+        copy.wait()
 
 
 def first_product(ids, weights, early, late, arrays, places):
@@ -442,7 +442,7 @@
         in_specs=[SMEM, SMEM] + [VMEM] * 4,
         out_specs=HBM,
         out_shape=jax.ShapeDtypeStruct(out, BF16),
-        scratch_shapes=[pltpu.VMEM(out, BF16), pltpu.SemaphoreType.DMA],
+        scratch_shapes=[pltpu.VMEM(out, BF16), pltpu.SemaphoreType.DMA((2,))],
         compiler_params=params(),
     )(ids, members, *product, near, far)
 

time: 137 us -> 136 us (level)
  no operation moved by 1% of the time
where the time goes in v5:
time: 136 us
  waiting for transfers between devices  69.4 us (51%)
  starting transfers between devices  38.2 us (28%)
  Pallas kernels  23 us (17%)
  local copies, waits for them, and re-layouts  3.83 us (3%)
    ppermute x42, waiting for transfers between devices, swap(): lax.ppermute(block, 'expert', [(i, i ^ distance) for i in range(count)])  69.4 us
    ppermute x42, starting transfers between devices, swap(): lax.ppermute(block, 'expert', [(i, i ^ distance) for i in range(count)])  38.2 us
    pallas_call x1, Pallas kernels, inverse_factor(): pl.pallas_call(functools.partial(inverse_kernel, scale), in_specs=[VMEM]...  9.56 us
    pallas_call x1, Pallas kernels, partial_blocks(): pl.pallas_call(functools.partial(far_partial_kernel, half), in_specs=[SME...  4.07 us
    unnamed x16, local copies, waits for them, and re-layouts  3.81 us
  transfers between devices with their start and end apart: 42, of which 17 were waited for; matrix products, arithmetic and copies ran while one was open for 0% of the time, Pallas kernels for 11%

profile of v5, /device:TPU:9, one launch (start us, length us, event | category | flops | bytes accessed | tf_op | source)
XLA Modules:
  0.0 135.8 jit_solution(6721799290408530215)
XLA Ops:
  0.6 4.1 %shard_map.59 = (bf16[2,256,256]{2,1,0:T(8,128)(2,1)}, bf16[2,256,256]{2,1,0:T(8,128)(2,1)}, bf16[2,256,256]{2,1,0:T(8,128)(2,1)}, bf16[2,256,256]{2,1,0:T(8,128)(2,1)}, bf16[256,768]{1,0:T(8,128)(2,1)}) custom-call(s32[1]{0:T(128)} %bitcast.ids_ref, bf16[768,768]{1,0:T(8,128)(2,1)} %bitcast.17, bf16[768,256]{1,0:T(8,128)(2,1)} %bitcast.18, ...), custom_call_target="tpu_custom_call" | custom-call | tf_op jit(solution)/shard_map/pallas_call | solution.py:108
  4.7 2.4 %collective-permute-start = (bf16[2,256,256]{2,1,0:T(8,128)(2,1)}, bf16[2,256,256]{2,1,0:T(8,128)(2,1)S(1)}, u32[]{:S(2)}, u32[]{:S(2)}) collective-permute-start(bf16[2,256,256]{2,1,0:T(8,128)(2,1)} %get-tuple-element.86), channel_id=1, source_target_pairs={{0,8},{1,9},{2,10},{3,11},{4,12},{5,13},{6,14},{7,15},{8,0},{9,1},... | collective-permute-start | bytes 786440 | tf_op jit(solution)/shard_map/ppermute | solution.py:452
  7.1 2.8 %copy-done = bf16[1,768,4096]{2,1,0:T(8,128)(2,1)S(1)} copy-done((bf16[1,768,4096]{2,1,0:T(8,128)(2,1)S(1)}, bf16[1,768,4096]{2,1,0:T(8,128)(2,1)}, u32[]{:S(2)}) %copy-start) | copy-done | bytes 6291480
  10.9 1.7 %shard_map.60 = (bf16[2,256,256]{2,1,0:T(8,128)(2,1)S(1)}, bf16[2,256,256]{2,1,0:T(8,128)(2,1)S(1)}, bf16[2,256,256]{2,1,0:T(8,128)(2,1)S(1)}, bf16[2,256,256]{2,1,0:T(8,128)(2,1)S(1)}) custom-call(s32[1]{0:T(128)} %bitcast.ids_ref, bf16[256,768]{1,0:T(8,128)(2,1)S(1)} %copy-done.1, bf16[768,4096]{1,0:T(8,128)(2,1)S(1)} %bitcast.8), custom_call_target="tpu_custom_call" | custom-call | tf_op jit(solution)/shard_map/pallas_call | solution.py:118
  12.6 1.3 collective-permute-start.1
  14.1 2.2 %collective-permute-start.4 = (bf16[2,256,256]{2,1,0:T(8,128)(2,1)S(1)}, bf16[2,256,256]{2,1,0:T(8,128)(2,1)S(1)}, u32[]{:S(2)}, u32[]{:S(2)}) collective-permute-start(bf16[2,256,256]{2,1,0:T(8,128)(2,1)S(1)} %get-tuple-element.93), channel_id=1, source_target_pairs={{0,6},{1,7},{2,4},{3,5},{4,2},{5,3},{6,0},{7,1},{8,14},{9,15},{10,... | collective-permute-start | bytes 786440 | tf_op jit(solution)/shard_map/ppermute | solution.py:452
  16.3 2.6 %collective-permute-done.refs_4_ = bf16[2,256,256]{2,1,0:T(8,128)(2,1)S(1)} collective-permute-done((bf16[2,256,256]{2,1,0:T(8,128)(2,1)}, bf16[2,256,256]{2,1,0:T(8,128)(2,1)S(1)}, u32[]{:S(2)}, u32[]{:S(2)}) %collective-permute-start) | collective-permute-done | bytes 262176 | tf_op jit(solution)/shard_map/ppermute | solution.py:452
  19.6 7.0 %collective-permute-done.2.refs_2_ = bf16[2,256,256]{2,1,0:T(8,128)(2,1)S(1)} collective-permute-done((bf16[2,256,256]{2,1,0:T(8,128)(2,1)S(1)}, bf16[2,256,256]{2,1,0:T(8,128)(2,1)S(1)}, u32[]{:S(2)}, u32[]{:S(2)}) %collective-permute-start.2) | collective-permute-done | bytes 262176 | tf_op jit(solution)/shard_map/ppermute | solution.py:452
  26.6 2.6 %collective-permute-start.5 = (bf16[2,256,256]{2,1,0:T(8,128)(2,1)S(1)}, bf16[2,256,256]{2,1,0:T(8,128)(2,1)S(1)}, u32[]{:S(2)}, u32[]{:S(2)}) collective-permute-start(bf16[2,256,256]{2,1,0:T(8,128)(2,1)S(1)} %copy-done.4), channel_id=1, source_target_pairs={{0,12},{1,13},{2,14},{3,15},{4,8},{5,9},{6,10},{7,11},{8,4},{9,5},... | collective-permute-start | bytes 786440 | tf_op jit(solution)/shard_map/ppermute | solution.py:452
  30.7 9.4 %collective-permute-done.4.refs_3_ = bf16[2,256,256]{2,1,0:T(8,128)(2,1)S(1)} collective-permute-done((bf16[2,256,256]{2,1,0:T(8,128)(2,1)S(1)}, bf16[2,256,256]{2,1,0:T(8,128)(2,1)S(1)}, u32[]{:S(2)}, u32[]{:S(2)}) %collective-permute-start.4) | collective-permute-done | bytes 262176 | tf_op jit(solution)/shard_map/ppermute | solution.py:452
  40.1 1.4 %collective-permute-start.6 = (bf16[2,256,256]{2,1,0:T(8,128)(2,1)S(1)}, bf16[2,256,256]{2,1,0:T(8,128)(2,1)S(1)}, u32[]{:S(2)}, u32[]{:S(2)}) collective-permute-start(bf16[2,256,256]{2,1,0:T(8,128)(2,1)S(1)} %copy-done.3), channel_id=1, source_target_pairs={{0,14},{1,15},{2,12},{3,13},{4,10},{5,11},{6,8},{7,9},{8,6},{9,7},... | collective-permute-start | bytes 786440 | tf_op jit(solution)/shard_map/ppermute | solution.py:452
  41.6 1.8 %collective-permute-start.11 = (bf16[2,256,256]{2,1,0:T(8,128)(2,1)S(1)}, bf16[2,256,256]{2,1,0:T(8,128)(2,1)S(1)}, u32[]{:S(2)}, u32[]{:S(2)}) collective-permute-start(bf16[2,256,256]{2,1,0:T(8,128)(2,1)S(1)} %collective-permute-done.refs_4_), channel_id=1, source_target_pairs={{0,1},{1,0},{2,3},{3,2},{4,5},{5,4},{6,7},{7,6},{8,9},{9,8},{10,11... | collective-permute-start | bytes 786440 | tf_op jit(solution)/shard_map/ppermute | solution.py:452
  44.0 10.0 %collective-permute-done.6.refs_7_ = bf16[2,256,256]{2,1,0:T(8,128)(2,1)S(1)} collective-permute-done((bf16[2,256,256]{2,1,0:T(8,128)(2,1)S(1)}, bf16[2,256,256]{2,1,0:T(8,128)(2,1)S(1)}, u32[]{:S(2)}, u32[]{:S(2)}) %collective-permute-start.6) | collective-permute-done | bytes 262176 | tf_op jit(solution)/shard_map/ppermute | solution.py:452
  54.0 1.3 collective-permute-start.14
  56.5 1.3 shard_map.61
  58.8 2.4 %collective-permute-start.19 = (bf16[2,256,256]{2,1,0:T(8,128)(2,1)S(1)}, bf16[2,256,256]{2,1,0:T(8,128)(2,1)S(1)}, u32[]{:S(2)}, u32[]{:S(2)}) collective-permute-start(bf16[2,256,256]{2,1,0:T(8,128)(2,1)S(1)} %get-tuple-element.110), channel_id=1, source_target_pairs={{0,12},{1,13},{2,14},{3,15},{4,8},{5,9},{6,10},{7,11},{8,4},{9,5},... | collective-permute-start | bytes 786440 | tf_op jit(solution)/shard_map/ppermute | solution.py:452
  62.2 10.6 %collective-permute-done.19.refs_5_ = bf16[2,256,256]{2,1,0:T(8,128)(2,1)S(1)} collective-permute-done((bf16[2,256,256]{2,1,0:T(8,128)(2,1)S(1)}, bf16[2,256,256]{2,1,0:T(8,128)(2,1)S(1)}, u32[]{:S(2)}, u32[]{:S(2)}) %collective-permute-start.19) | collective-permute-done | bytes 262176 | tf_op jit(solution)/shard_map/ppermute | solution.py:452
  74.4 1.8 %collective-permute-start.22 = (bf16[2,256,256]{2,1,0:T(8,128)(2,1)S(1)}, bf16[2,256,256]{2,1,0:T(8,128)(2,1)S(1)}, u32[]{:S(2)}, u32[]{:S(2)}) collective-permute-start(bf16[2,256,256]{2,1,0:T(8,128)(2,1)S(1)} %get-tuple-element.116), channel_id=1, source_target_pairs={{0,8},{1,9},{2,10},{3,11},{4,12},{5,13},{6,14},{7,15},{8,0},{9,1},... | collective-permute-start | bytes 786440 | tf_op jit(solution)/shard_map/ppermute | solution.py:452
  77.5 2.2 %collective-permute-done.16 = f32[1,3,128,128]{3,2,1,0:T(8,128)S(1)} collective-permute-done((f32[1,3,128,128]{3,2,1,0:T(8,128)S(1)}, f32[1,3,128,128]{3,2,1,0:T(8,128)S(1)}, u32[]{:S(2)}, u32[]{:S(2)}) %collective-permute-start.16) | collective-permute-done | bytes 196640 | tf_op jit(solution)/shard_map/ppermute | solution.py:452
  79.7 2.1 %collective-permute-done.21 = f32[1,3,128,128]{3,2,1,0:T(8,128)S(1)} collective-permute-done((f32[1,3,128,128]{3,2,1,0:T(8,128)S(1)}, f32[1,3,128,128]{3,2,1,0:T(8,128)S(1)}, u32[]{:S(2)}, u32[]{:S(2)}) %collective-permute-start.21) | collective-permute-done | bytes 196640 | tf_op jit(solution)/shard_map/ppermute | solution.py:452
  81.8 4.6 %collective-permute-done.22.refs_4_ = bf16[2,256,256]{2,1,0:T(8,128)(2,1)S(1)} collective-permute-done((bf16[2,256,256]{2,1,0:T(8,128)(2,1)S(1)}, bf16[2,256,256]{2,1,0:T(8,128)(2,1)S(1)}, u32[]{:S(2)}, u32[]{:S(2)}) %collective-permute-start.22) | collective-permute-done | bytes 262176 | tf_op jit(solution)/shard_map/ppermute | solution.py:452
  86.4 3.5 %collective-permute-start.24 = (f32[1,3,128,128]{3,2,1,0:T(8,128)S(1)}, f32[1,3,128,128]{3,2,1,0:T(8,128)S(1)}, u32[]{:S(2)}, u32[]{:S(2)}) collective-permute-start(f32[1,3,128,128]{3,2,1,0:T(8,128)S(1)} %fusion), channel_id=1, source_target_pairs={{0,8},{1,9},{2,10},{3,11},{4,12},{5,13},{6,14},{7,15},{8,0},{9,1},... | collective-permute-start | bytes 589832 | tf_op jit(solution)/shard_map/ppermute | solution.py:452
  89.9 7.7 %collective-permute-done.24 = f32[1,3,128,128]{3,2,1,0:T(8,128)S(1)} collective-permute-done((f32[1,3,128,128]{3,2,1,0:T(8,128)S(1)}, f32[1,3,128,128]{3,2,1,0:T(8,128)S(1)}, u32[]{:S(2)}, u32[]{:S(2)}) %collective-permute-start.24) | collective-permute-done | bytes 196640 | tf_op jit(solution)/shard_map/ppermute | solution.py:452
  97.6 1.7 %collective-permute-start.30 = (bf16[2,256,256]{2,1,0:T(8,128)(2,1)S(1)}, bf16[2,256,256]{2,1,0:T(8,128)(2,1)S(1)}, u32[]{:S(2)}, u32[]{:S(2)}) collective-permute-start(bf16[2,256,256]{2,1,0:T(8,128)(2,1)S(1)} %collective-permute-done.22.refs_4_), channel_id=1, source_target_pairs={{0,1},{1,0},{2,3},{3,2},{4,5},{5,4},{6,7},{7,6},{8,9},{9,8},{10,11... | collective-permute-start | bytes 786440 | tf_op jit(solution)/shard_map/ppermute | solution.py:452
  100.5 3.7 %collective-permute-start.32 = (bf16[2,256,256]{2,1,0:T(8,128)(2,1)S(1)}, bf16[2,256,256]{2,1,0:T(8,128)(2,1)S(1)}, u32[]{:S(2)}, u32[]{:S(2)}) collective-permute-start(bf16[2,256,256]{2,1,0:T(8,128)(2,1)S(1)} %get-tuple-element.150), channel_id=1, source_target_pairs={{0,10},{1,11},{2,8},{3,9},{4,14},{5,15},{6,12},{7,13},{8,2},{9,3},... | collective-permute-start | bytes 786440 | tf_op jit(solution)/shard_map/ppermute | solution.py:452
  104.2 9.6 %shard_map.63 = (bf16[3,128,128]{2,1,0:T(8,128)(2,1)S(1)}, bf16[8,256,256]{2,1,0:T(8,128)(2,1)S(1)}) custom-call(f32[3,128,128]{2,1,0:T(8,128)S(1)} %bitcast.12, bf16[8,256,256]{2,1,0:T(8,128)(2,1)S(1)} %get-tuple-element.137.rows_ref.rows_t_ref), custom_call_target="tpu_custom_call" | custom-call | bytes 140000000 | tf_op jit(solution)/shard_map/pallas_call | solution.py:298
  113.9 1.2 collective-permute-start.33
  116.8 2.3 %shard_map.64 = (f32[768,256]{1,0:T(8,128)S(1)}, bf16[768,1024]{1,0:T(8,128)(2,1)S(1)}) custom-call(s32[1]{0:T(128)} %bitcast.ids_ref, bf16[768,4096]{1,0:T(8,128)(2,1)S(1)} %bitcast.11, bf16[2,256,256]{2,1,0:T(8,128)(2,1)S(1)} %get-tuple-element.121.refs_0_, bf16[2,256,256]{2,1,0:T(8,128)(2,1)S(1)} %collective-permute-done.23.refs_1_, ...), custom_call_target="tpu_custom_call" | custom-call | tf_op jit(solution)/shard_map/pallas_call | solution.py:413
  119.1 4.2 %collective-permute-done.31 = bf16[1,3,128,128]{3,2,1,0:T(8,128)(2,1)S(1)} collective-permute-done((bf16[1,3,128,128]{3,2,1,0:T(8,128)(2,1)S(1)}, bf16[1,3,128,128]{3,2,1,0:T(8,128)(2,1)S(1)}, u32[]{:S(2)}, u32[]{:S(2)}) %collective-permute-start.31) | collective-permute-done | bytes 98336 | tf_op jit(solution)/shard_map/ppermute | solution.py:452
  123.7 4.7 %collective-permute-done.33.refs_1_ = bf16[2,256,256]{2,1,0:T(8,128)(2,1)S(1)} collective-permute-done((bf16[2,256,256]{2,1,0:T(8,128)(2,1)S(1)}, bf16[2,256,256]{2,1,0:T(8,128)(2,1)S(1)}, u32[]{:S(2)}, u32[]{:S(2)}) %collective-permute-start.33) | collective-permute-done | bytes 262176 | tf_op jit(solution)/shard_map/ppermute | solution.py:452
  132.0 1.3 shard_map.67
  133.9 1.7 %shard_map.66 = bf16[768,256]{1,0:T(8,128)(2,1)} custom-call(s32[1]{0:T(128)} %bitcast.ids_ref, s32[16]{0:T(128)S(1)} %copy-done.2, bf16[768,256]{1,0:T(8,128)(2,1)S(1)} %get-tuple-element.159.high_ref, bf16[768,256]{1,0:T(8,128)(2,1)S(1)} %get-tuple-element.160.low_ref, bf16[4,3,128,128]{3,2,1,0:T(8,128)(2,1)S(1)} %pad_maximum_fusion.near_ref, ...), custom_call_target="tpu_custom_call" | custom-call | tf_op jit(solution)/shard_map/pallas_call | solution.py:440
  (85 shorter events, 17.4 us)
Async XLA Ops:
  4.7 14.3 %collective-permute-start = (bf16[2,256,256]{2,1,0:T(8,128)(2,1)}, bf16[2,256,256]{2,1,0:T(8,128)(2,1)S(1)}, u32[]{:S(2)}, u32[]{:S(2)}) collective-permute-start(bf16[2,256,256]{2,1,0:T(8,128)(2,1)} %get-tuple-element.86), channel_id=1, source_target_pairs={{0,8},{1,9},{2,10},{3,11},{4,12},{5,13},{6,14},{7,15},{8,0},{9,1},... | collective-permute-start | bytes 786440 | tf_op jit(solution)/shard_map/ppermute | solution.py:452
  12.6 7.0 %collective-permute-start.1 = (bf16[2,256,256]{2,1,0:T(8,128)(2,1)S(1)}, bf16[2,256,256]{2,1,0:T(8,128)(2,1)S(1)}, u32[]{:S(2)}, u32[]{:S(2)}) collective-permute-start(bf16[2,256,256]{2,1,0:T(8,128)(2,1)S(1)} %get-tuple-element.87), channel_id=1, source_target_pairs={{0,2},{1,3},{2,0},{3,1},{4,6},{5,7},{6,4},{7,5},{8,10},{9,11},{10,... | collective-permute-start | bytes 786440 | tf_op jit(solution)/shard_map/ppermute | solution.py:452
  13.9 12.7 %collective-permute-start.2 = (bf16[2,256,256]{2,1,0:T(8,128)(2,1)S(1)}, bf16[2,256,256]{2,1,0:T(8,128)(2,1)S(1)}, u32[]{:S(2)}, u32[]{:S(2)}) collective-permute-start(bf16[2,256,256]{2,1,0:T(8,128)(2,1)S(1)} %get-tuple-element.88), channel_id=1, source_target_pairs={{0,4},{1,5},{2,6},{3,7},{4,0},{5,1},{6,2},{7,3},{8,12},{9,13},{10,... | collective-permute-start | bytes 786440 | tf_op jit(solution)/shard_map/ppermute | solution.py:452
  14.1 16.3 %collective-permute-start.3 = (bf16[2,256,256]{2,1,0:T(8,128)(2,1)S(1)}, bf16[2,256,256]{2,1,0:T(8,128)(2,1)S(1)}, u32[]{:S(2)}, u32[]{:S(2)}) collective-permute-start(bf16[2,256,256]{2,1,0:T(8,128)(2,1)S(1)} %copy-done.5), channel_id=1, source_target_pairs={{0,10},{1,11},{2,8},{3,9},{4,14},{5,15},{6,12},{7,13},{8,2},{9,3},... | collective-permute-start | bytes 786440 | tf_op jit(solution)/shard_map/ppermute | solution.py:452
  14.1 26.0 %collective-permute-start.4 = (bf16[2,256,256]{2,1,0:T(8,128)(2,1)S(1)}, bf16[2,256,256]{2,1,0:T(8,128)(2,1)S(1)}, u32[]{:S(2)}, u32[]{:S(2)}) collective-permute-start(bf16[2,256,256]{2,1,0:T(8,128)(2,1)S(1)} %get-tuple-element.93), channel_id=1, source_target_pairs={{0,6},{1,7},{2,4},{3,5},{4,2},{5,3},{6,0},{7,1},{8,14},{9,15},{10,... | collective-permute-start | bytes 786440 | tf_op jit(solution)/shard_map/ppermute | solution.py:452
  19.0 22.6 %collective-permute-start.7 = (bf16[2,256,256]{2,1,0:T(8,128)(2,1)S(1)}, bf16[2,256,256]{2,1,0:T(8,128)(2,1)S(1)}, u32[]{:S(2)}, u32[]{:S(2)}) collective-permute-start(bf16[2,256,256]{2,1,0:T(8,128)(2,1)S(1)} %get-tuple-element.84.refs_0_), channel_id=1, source_target_pairs={{0,1},{1,0},{2,3},{3,2},{4,5},{5,4},{6,7},{7,6},{8,9},{9,8},{10,11... | collective-permute-start | bytes 786440 | tf_op jit(solution)/shard_map/ppermute | solution.py:452
  26.6 16.7 %collective-permute-start.5 = (bf16[2,256,256]{2,1,0:T(8,128)(2,1)S(1)}, bf16[2,256,256]{2,1,0:T(8,128)(2,1)S(1)}, u32[]{:S(2)}, u32[]{:S(2)}) collective-permute-start(bf16[2,256,256]{2,1,0:T(8,128)(2,1)S(1)} %copy-done.4), channel_id=1, source_target_pairs={{0,12},{1,13},{2,14},{3,15},{4,8},{5,9},{6,10},{7,11},{8,4},{9,5},... | collective-permute-start | bytes 786440 | tf_op jit(solution)/shard_map/ppermute | solution.py:452
  29.2 14.2 %collective-permute-start.8 = (bf16[2,256,256]{2,1,0:T(8,128)(2,1)S(1)}, bf16[2,256,256]{2,1,0:T(8,128)(2,1)S(1)}, u32[]{:S(2)}, u32[]{:S(2)}) collective-permute-start(bf16[2,256,256]{2,1,0:T(8,128)(2,1)S(1)} %collective-permute-done.1.refs_1_), channel_id=1, source_target_pairs={{0,1},{1,0},{2,3},{3,2},{4,5},{5,4},{6,7},{7,6},{8,9},{9,8},{10,11... | collective-permute-start | bytes 786440 | tf_op jit(solution)/shard_map/ppermute | solution.py:452
  30.4 13.5 %collective-permute-start.9 = (bf16[2,256,256]{2,1,0:T(8,128)(2,1)S(1)}, bf16[2,256,256]{2,1,0:T(8,128)(2,1)S(1)}, u32[]{:S(2)}, u32[]{:S(2)}) collective-permute-start(bf16[2,256,256]{2,1,0:T(8,128)(2,1)S(1)} %collective-permute-done.2.refs_2_), channel_id=1, source_target_pairs={{0,1},{1,0},{2,3},{3,2},{4,5},{5,4},{6,7},{7,6},{8,9},{9,8},{10,11... | collective-permute-start | bytes 786440 | tf_op jit(solution)/shard_map/ppermute | solution.py:452
  40.1 13.9 %collective-permute-start.6 = (bf16[2,256,256]{2,1,0:T(8,128)(2,1)S(1)}, bf16[2,256,256]{2,1,0:T(8,128)(2,1)S(1)}, u32[]{:S(2)}, u32[]{:S(2)}) collective-permute-start(bf16[2,256,256]{2,1,0:T(8,128)(2,1)S(1)} %copy-done.3), channel_id=1, source_target_pairs={{0,14},{1,15},{2,12},{3,13},{4,10},{5,11},{6,8},{7,9},{8,6},{9,7},... | collective-permute-start | bytes 786440 | tf_op jit(solution)/shard_map/ppermute | solution.py:452
  41.6 13.8 %collective-permute-start.11 = (bf16[2,256,256]{2,1,0:T(8,128)(2,1)S(1)}, bf16[2,256,256]{2,1,0:T(8,128)(2,1)S(1)}, u32[]{:S(2)}, u32[]{:S(2)}) collective-permute-start(bf16[2,256,256]{2,1,0:T(8,128)(2,1)S(1)} %collective-permute-done.refs_4_), channel_id=1, source_target_pairs={{0,1},{1,0},{2,3},{3,2},{4,5},{5,4},{6,7},{7,6},{8,9},{9,8},{10,11... | collective-permute-start | bytes 786440 | tf_op jit(solution)/shard_map/ppermute | solution.py:452
  43.4 12.0 %collective-permute-start.10 = (bf16[2,256,256]{2,1,0:T(8,128)(2,1)S(1)}, bf16[2,256,256]{2,1,0:T(8,128)(2,1)S(1)}, u32[]{:S(2)}, u32[]{:S(2)}) collective-permute-start(bf16[2,256,256]{2,1,0:T(8,128)(2,1)S(1)} %collective-permute-done.4.refs_3_), channel_id=1, source_target_pairs={{0,1},{1,0},{2,3},{3,2},{4,5},{5,4},{6,7},{7,6},{8,9},{9,8},{10,11... | collective-permute-start | bytes 786440 | tf_op jit(solution)/shard_map/ppermute | solution.py:452
  43.5 11.9 %collective-permute-start.12 = (bf16[2,256,256]{2,1,0:T(8,128)(2,1)S(1)}, bf16[2,256,256]{2,1,0:T(8,128)(2,1)S(1)}, u32[]{:S(2)}, u32[]{:S(2)}) collective-permute-start(bf16[2,256,256]{2,1,0:T(8,128)(2,1)S(1)} %collective-permute-done.3.refs_5_), channel_id=1, source_target_pairs={{0,1},{1,0},{2,3},{3,2},{4,5},{5,4},{6,7},{7,6},{8,9},{9,8},{10,11... | collective-permute-start | bytes 786440 | tf_op jit(solution)/shard_map/ppermute | solution.py:452
  43.9 11.5 %collective-permute-start.13 = (bf16[2,256,256]{2,1,0:T(8,128)(2,1)S(1)}, bf16[2,256,256]{2,1,0:T(8,128)(2,1)S(1)}, u32[]{:S(2)}, u32[]{:S(2)}) collective-permute-start(bf16[2,256,256]{2,1,0:T(8,128)(2,1)S(1)} %collective-permute-done.5.refs_6_), channel_id=1, source_target_pairs={{0,1},{1,0},{2,3},{3,2},{4,5},{5,4},{6,7},{7,6},{8,9},{9,8},{10,11... | collective-permute-start | bytes 786440 | tf_op jit(solution)/shard_map/ppermute | solution.py:452
  58.8 14.0 %collective-permute-start.19 = (bf16[2,256,256]{2,1,0:T(8,128)(2,1)S(1)}, bf16[2,256,256]{2,1,0:T(8,128)(2,1)S(1)}, u32[]{:S(2)}, u32[]{:S(2)}) collective-permute-start(bf16[2,256,256]{2,1,0:T(8,128)(2,1)S(1)} %get-tuple-element.110), channel_id=1, source_target_pairs={{0,12},{1,13},{2,14},{3,15},{4,8},{5,9},{6,10},{7,11},{8,4},{9,5},... | collective-permute-start | bytes 786440 | tf_op jit(solution)/shard_map/ppermute | solution.py:452
  61.2 12.1 %collective-permute-start.17 = (f32[1,3,128,128]{3,2,1,0:T(8,128)S(1)}, f32[1,3,128,128]{3,2,1,0:T(8,128)S(1)}, u32[]{:S(2)}, u32[]{:S(2)}) collective-permute-start(f32[1,3,128,128]{3,2,1,0:T(8,128)S(1)} %get-tuple-element.167), channel_id=1, source_target_pairs={{0,2},{1,3},{2,0},{3,1},{4,6},{5,7},{6,4},{7,5},{8,10},{9,11},{10,... | collective-permute-start | bytes 589832 | tf_op jit(solution)/shard_map/ppermute | solution.py:452
  62.2 11.3 %collective-permute-start.18 = (bf16[2,256,256]{2,1,0:T(8,128)(2,1)S(1)}, bf16[2,256,256]{2,1,0:T(8,128)(2,1)S(1)}, u32[]{:S(2)}, u32[]{:S(2)}) collective-permute-start(bf16[2,256,256]{2,1,0:T(8,128)(2,1)S(1)} %get-tuple-element.106), channel_id=1, source_target_pairs={{0,4},{1,5},{2,6},{3,7},{4,0},{5,1},{6,2},{7,3},{8,12},{9,13},{10,... | collective-permute-start | bytes 786440 | tf_op jit(solution)/shard_map/ppermute | solution.py:452
  74.4 7.4 %collective-permute-start.21 = (f32[1,3,128,128]{3,2,1,0:T(8,128)S(1)}, f32[1,3,128,128]{3,2,1,0:T(8,128)S(1)}, u32[]{:S(2)}, u32[]{:S(2)}) collective-permute-start(f32[1,3,128,128]{3,2,1,0:T(8,128)S(1)} %slice_add_fusion.2), channel_id=1, source_target_pairs={{0,4},{1,5},{2,6},{3,7},{4,0},{5,1},{6,2},{7,3},{8,12},{9,13},{10,... | collective-permute-start | bytes 589832 | tf_op jit(solution)/shard_map/ppermute | solution.py:452
  74.4 12.1 %collective-permute-start.22 = (bf16[2,256,256]{2,1,0:T(8,128)(2,1)S(1)}, bf16[2,256,256]{2,1,0:T(8,128)(2,1)S(1)}, u32[]{:S(2)}, u32[]{:S(2)}) collective-permute-start(bf16[2,256,256]{2,1,0:T(8,128)(2,1)S(1)} %get-tuple-element.116), channel_id=1, source_target_pairs={{0,8},{1,9},{2,10},{3,11},{4,12},{5,13},{6,14},{7,15},{8,0},{9,1},... | collective-permute-start | bytes 786440 | tf_op jit(solution)/shard_map/ppermute | solution.py:452
  76.1 10.3 %collective-permute-start.23 = (bf16[2,256,256]{2,1,0:T(8,128)(2,1)S(1)}, bf16[2,256,256]{2,1,0:T(8,128)(2,1)S(1)}, u32[]{:S(2)}, u32[]{:S(2)}) collective-permute-start(bf16[2,256,256]{2,1,0:T(8,128)(2,1)S(1)} %get-tuple-element.117), channel_id=1, source_target_pairs={{0,2},{1,3},{2,0},{3,1},{4,6},{5,7},{6,4},{7,5},{8,10},{9,11},{10,... | collective-permute-start | bytes 786440 | tf_op jit(solution)/shard_map/ppermute | solution.py:452
  77.2 20.5 %collective-permute-start.25 = (bf16[2,256,256]{2,1,0:T(8,128)(2,1)S(1)}, bf16[2,256,256]{2,1,0:T(8,128)(2,1)S(1)}, u32[]{:S(2)}, u32[]{:S(2)}) collective-permute-start(bf16[2,256,256]{2,1,0:T(8,128)(2,1)S(1)} %get-tuple-element.119), channel_id=1, source_target_pairs={{0,6},{1,7},{2,4},{3,5},{4,2},{5,3},{6,0},{7,1},{8,14},{9,15},{10,... | collective-permute-start | bytes 786440 | tf_op jit(solution)/shard_map/ppermute | solution.py:452
  86.4 11.2 %collective-permute-start.24 = (f32[1,3,128,128]{3,2,1,0:T(8,128)S(1)}, f32[1,3,128,128]{3,2,1,0:T(8,128)S(1)}, u32[]{:S(2)}, u32[]{:S(2)}) collective-permute-start(f32[1,3,128,128]{3,2,1,0:T(8,128)S(1)} %fusion), channel_id=1, source_target_pairs={{0,8},{1,9},{2,10},{3,11},{4,12},{5,13},{6,14},{7,15},{8,0},{9,1},... | collective-permute-start | bytes 589832 | tf_op jit(solution)/shard_map/ppermute | solution.py:452
  99.4 14.4 %collective-permute-start.29 = (bf16[2,256,256]{2,1,0:T(8,128)(2,1)S(1)}, bf16[2,256,256]{2,1,0:T(8,128)(2,1)S(1)}, u32[]{:S(2)}, u32[]{:S(2)}) collective-permute-start(bf16[2,256,256]{2,1,0:T(8,128)(2,1)S(1)} %collective-permute-done.25.refs_3_), channel_id=1, source_target_pairs={{0,1},{1,0},{2,3},{3,2},{4,5},{5,4},{6,7},{7,6},{8,9},{9,8},{10,11... | collective-permute-start | bytes 786440 | tf_op jit(solution)/shard_map/ppermute | solution.py:452
  99.5 14.4 %collective-permute-start.28 = (bf16[2,256,256]{2,1,0:T(8,128)(2,1)S(1)}, bf16[2,256,256]{2,1,0:T(8,128)(2,1)S(1)}, u32[]{:S(2)}, u32[]{:S(2)}) collective-permute-start(bf16[2,256,256]{2,1,0:T(8,128)(2,1)S(1)} %collective-permute-done.18.refs_2_), channel_id=1, source_target_pairs={{0,1},{1,0},{2,3},{3,2},{4,5},{5,4},{6,7},{7,6},{8,9},{9,8},{10,11... | collective-permute-start | bytes 786440 | tf_op jit(solution)/shard_map/ppermute | solution.py:452
  99.9 14.0 %collective-permute-start.27 = (bf16[2,256,256]{2,1,0:T(8,128)(2,1)S(1)}, bf16[2,256,256]{2,1,0:T(8,128)(2,1)S(1)}, u32[]{:S(2)}, u32[]{:S(2)}) collective-permute-start(bf16[2,256,256]{2,1,0:T(8,128)(2,1)S(1)} %collective-permute-done.23.refs_1_), channel_id=1, source_target_pairs={{0,1},{1,0},{2,3},{3,2},{4,5},{5,4},{6,7},{7,6},{8,9},{9,8},{10,11... | collective-permute-start | bytes 786440 | tf_op jit(solution)/shard_map/ppermute | solution.py:452
  100.0 13.9 %collective-permute-start.26 = (bf16[2,256,256]{2,1,0:T(8,128)(2,1)S(1)}, bf16[2,256,256]{2,1,0:T(8,128)(2,1)S(1)}, u32[]{:S(2)}, u32[]{:S(2)}) collective-permute-start(bf16[2,256,256]{2,1,0:T(8,128)(2,1)S(1)} %get-tuple-element.121.refs_0_), channel_id=1, source_target_pairs={{0,1},{1,0},{2,3},{3,2},{4,5},{5,4},{6,7},{7,6},{8,9},{9,8},{10,11... | collective-permute-start | bytes 786440 | tf_op jit(solution)/shard_map/ppermute | solution.py:452
  100.5 18.5 %collective-permute-start.32 = (bf16[2,256,256]{2,1,0:T(8,128)(2,1)S(1)}, bf16[2,256,256]{2,1,0:T(8,128)(2,1)S(1)}, u32[]{:S(2)}, u32[]{:S(2)}) collective-permute-start(bf16[2,256,256]{2,1,0:T(8,128)(2,1)S(1)} %get-tuple-element.150), channel_id=1, source_target_pairs={{0,10},{1,11},{2,8},{3,9},{4,14},{5,15},{6,12},{7,13},{8,2},{9,3},... | collective-permute-start | bytes 786440 | tf_op jit(solution)/shard_map/ppermute | solution.py:452
  113.9 14.6 %collective-permute-start.33 = (bf16[2,256,256]{2,1,0:T(8,128)(2,1)S(1)}, bf16[2,256,256]{2,1,0:T(8,128)(2,1)S(1)}, u32[]{:S(2)}, u32[]{:S(2)}) collective-permute-start(bf16[2,256,256]{2,1,0:T(8,128)(2,1)S(1)} %get-tuple-element.155), channel_id=1, source_target_pairs={{0,14},{1,15},{2,12},{3,13},{4,10},{5,11},{6,8},{7,9},{8,6},{9,7},... | collective-permute-start | bytes 786440 | tf_op jit(solution)/shard_map/ppermute | solution.py:452
  115.1 8.2 %collective-permute-start.31 = (bf16[1,3,128,128]{3,2,1,0:T(8,128)(2,1)S(1)}, bf16[1,3,128,128]{3,2,1,0:T(8,128)(2,1)S(1)}, u32[]{:S(2)}, u32[]{:S(2)}) collective-permute-start(bf16[1,3,128,128]{3,2,1,0:T(8,128)(2,1)S(1)} %bitcast.13), channel_id=1, source_target_pairs={{0,4},{1,5},{2,6},{3,7},{4,0},{5,1},{6,2},{7,3},{8,12},{9,13},{10,... | collective-permute-start | bytes 294920 | tf_op jit(solution)/shard_map/ppermute | solution.py:452
  115.1 13.9 %collective-permute-start.37 = (bf16[1,3,128,128]{3,2,1,0:T(8,128)(2,1)S(1)}, bf16[1,3,128,128]{3,2,1,0:T(8,128)(2,1)S(1)}, u32[]{:S(2)}, u32[]{:S(2)}) collective-permute-start(bf16[1,3,128,128]{3,2,1,0:T(8,128)(2,1)S(1)} %bitcast.14), channel_id=1, source_target_pairs={{0,1},{1,0},{2,3},{3,2},{4,5},{5,4},{6,7},{7,6},{8,9},{9,8},{10,11... | collective-permute-start | bytes 294920 | tf_op jit(solution)/shard_map/ppermute | solution.py:452
  116.0 13.4 %collective-permute-start.35 = (bf16[1,3,128,128]{3,2,1,0:T(8,128)(2,1)S(1)}, bf16[1,3,128,128]{3,2,1,0:T(8,128)(2,1)S(1)}, u32[]{:S(2)}, u32[]{:S(2)}) collective-permute-start(bf16[1,3,128,128]{3,2,1,0:T(8,128)(2,1)S(1)} %bitcast.15), channel_id=1, source_target_pairs={{0,2},{1,3},{2,0},{3,1},{4,6},{5,7},{6,4},{7,5},{8,10},{9,11},{10,... | collective-permute-start | bytes 294920 | tf_op jit(solution)/shard_map/ppermute | solution.py:452
  123.3 7.2 %collective-permute-start.36 = (bf16[1,3,128,128]{3,2,1,0:T(8,128)(2,1)S(1)}, bf16[1,3,128,128]{3,2,1,0:T(8,128)(2,1)S(1)}, u32[]{:S(2)}, u32[]{:S(2)}) collective-permute-start(bf16[1,3,128,128]{3,2,1,0:T(8,128)(2,1)S(1)} %collective-permute-done.31), channel_id=1, source_target_pairs={{0,2},{1,3},{2,0},{3,1},{4,6},{5,7},{6,4},{7,5},{8,10},{9,11},{10,... | collective-permute-start | bytes 294920 | tf_op jit(solution)/shard_map/ppermute | solution.py:452
  (18 other events, 310.7 us)
